TPU v7x, 128 devices: a whole 4x4x4 slice. The times are simulated.
128 devices in a mesh: wide: 16 (over z_lo, x, core), narrow: 8 (over y, z_hi).
Axes of the slice: x: 4, y: 4, z: 4 (z_hi: 2, z_lo: 2; z = z_hi * 2 + z_lo), core: 2. Of those that a mesh axis runs over, the one named last changes fastest.
Arguments:
- x_stash: bfloat16 [1536, 8192], P('wide', 'narrow'), may hold values from -6 to 6
- token_ids: int32 [1024], P('wide'), may hold values from 0 to 1535, as said below
- grad_out: bfloat16 [1024, 8192], P('wide', 'narrow'), may hold values from -1.5 to 1.5
- w_up: bfloat16 [8192, 30720], P('narrow', 'wide'), may hold values from -0.0625 to 0.0625
- w_down: bfloat16 [8192, 30720], P('narrow', 'wide'), may hold values from -0.03125 to 0.03125
- acc_up: bfloat16 [8, 16, 1966592], P('narrow', 'wide'), may hold values from -6 to 6
- acc_down: bfloat16 [8, 16, 1966592], P('narrow', 'wide'), may hold values from -6 to 6
- offsets: int32 [2, 8, 16], P(None, 'narrow', 'wide'), may hold values from 0 to 512, as said below
Outputs:
- out_y: bfloat16 [1024, 8192], P('wide', 'narrow')
- grad_in: bfloat16 [1024, 8192], P('wide', 'narrow')
- new_up: bfloat16 [8192, 30720], P('narrow', 'wide')
- new_down: bfloat16 [8192, 30720], P('narrow', 'wide')
Inputs may be any that keep to these rules, and one draw needn't show every extreme that they name: `token_ids`: entries j * 64 to (j + 1) * 64 - 1 are distinct rows between j * 96 and (j + 1) * 96 - 1. `offsets`: multiples of 128.
All inputs are finite; a program needn't handle non-finite values.
Results may differ from a plain program's by a relative error of at most 0.005.
Values may be sent and summed in bfloat16 or wider, within the bound.
No kernel may reach another device: no remote copies, remote signals or barrier semaphores. Data moves between devices by JAX's collectives and lax.ppermute only.
A program may use at most 192 MiB of HBM per device.

v0:
```python
import jax
import jax.numpy as jnp
from jax import lax
from jax.sharding import PartitionSpec as P

SLACK = 512


def gelu_parts(hidden):
    normal_cdf = 0.5 * (1.0 + jax.scipy.special.erf(hidden * 0.7071067811865476))
    density = jnp.exp(-0.5 * hidden * hidden) * 0.3989422804014327
    return (hidden * normal_cdf, normal_cdf + hidden * density)


def shard_matrix(accum, start, full_width):
    buffer = accum[0, 0]
    shard_rows = (buffer.shape[0] - SLACK) // full_width
    segment = lax.dynamic_slice_in_dim(buffer, start, shard_rows * full_width)
    return segment.reshape(shard_rows, full_width)


def body(x_stash, token_ids, grad_out, w_up, w_down, acc_up, acc_down, offsets):
    local_rows = token_ids - lax.axis_index("wide") * x_stash.shape[0]
    picked = jnp.take(x_stash, local_rows, axis=0)
    inputs, upstream = (
        lax.all_gather(picked, "wide", axis=0, tiled=True),
        lax.all_gather(grad_out, "wide", axis=0, tiled=True),
    )
    partial_hidden = jnp.dot(inputs, w_up, preferred_element_type=jnp.float32)
    hidden = lax.psum(partial_hidden, "narrow")
    gelu_value, slope = gelu_parts(hidden)
    activation = gelu_value.astype(jnp.bfloat16)
    output_terms = jnp.dot(activation, w_down.T, preferred_element_type=jnp.float32)
    out_y = lax.psum_scatter(output_terms, "wide", scatter_dimension=0, tiled=True).astype(
        jnp.bfloat16
    )
    partial_back = jnp.dot(upstream, w_down, preferred_element_type=jnp.float32)
    back = lax.psum(partial_back, "narrow")
    hidden_grad = (back * slope).astype(jnp.bfloat16)
    input_terms = jnp.dot(hidden_grad, w_up.T, preferred_element_type=jnp.float32)
    grad_in = lax.psum_scatter(input_terms, "wide", scatter_dimension=0, tiled=True).astype(
        jnp.bfloat16
    )
    full_width = w_up.shape[1] * lax.axis_size("wide")
    up_segment = shard_matrix(acc_up, offsets[0, 0, 0], full_width)
    down_segment = shard_matrix(acc_down, offsets[1, 0, 0], full_width)
    up_blocks, down_blocks = (
        lax.all_to_all(up_segment, "wide", split_axis=1, concat_axis=0, tiled=True),
        lax.all_to_all(down_segment, "wide", split_axis=1, concat_axis=0, tiled=True),
    )
    up_update = jnp.dot(inputs.T, hidden_grad, preferred_element_type=jnp.float32)
    new_up = (up_blocks.astype(jnp.float32) + up_update).astype(jnp.bfloat16)
    down_update = jnp.dot(upstream.T, activation, preferred_element_type=jnp.float32)
    new_down = (down_blocks.astype(jnp.float32) + down_update).astype(jnp.bfloat16)
    return (out_y, grad_in, new_up, new_down)


def solution(mesh):
    in_specs = (
        P("wide", "narrow"),
        P("wide"),
        P("wide", "narrow"),
        P("narrow", "wide"),
        P("narrow", "wide"),
        P("narrow", "wide", None),
        P("narrow", "wide", None),
        P(None, "narrow", "wide"),
    )
    out_specs = (P("wide", "narrow"), P("wide", "narrow"), P("narrow", "wide"), P("narrow", "wide"))
    return jax.shard_map(body, mesh=mesh, in_specs=in_specs, out_specs=out_specs, check_vma=False)
```

profile of v0, /device:TPU:0, one launch (start us, length us, event | category | flops | bytes accessed | tf_op | source)
XLA Modules:
  0.0 1023.4 jit_solution(17352734077567030862)
XLA Ops:
  7.2 0.7 compare_and_fusion
  8.1 0.7 gather_fusion
  8.8 0.7 broadcast_select_fusion
  9.6 0.7 all-gather.5.cloned.1.call-update
  10.4 36.5 %all-gather.3.cloned.1.call-done = bf16[1024,1024]{1,0:T(8,128)(2,1)} async-done(((bf16[64,1024]{1,0:T(8,128)(2,1)}), bf16[1024,1024]{1,0:T(8,128)(2,1)}) %all-gather.3.cloned.1.call-update) | async-done | bytes 2097168 | tf_op jit(solution)/shard_map/all_gather | solution.py:26
  46.8 10.4 %fusion.9 = f32[1024,1920]{1,0:T(8,128)} fusion(bf16[1024,1024]{1,0:T(8,128)(2,1)} %all-gather.3.cloned.1.call-done, bf16[1024,1920]{1,0:T(8,128)(2,1)} %param.11), kind=kOutput, calls=%fused_computation.21 | convolution fusion | flops 4026531840 | bytes 13893632 | tf_op jit(solution)/shard_map/dot_general | solution.py:29
  57.2 25.4 %all-gather.5.cloned.1.call-done = bf16[1024,1024]{1,0:T(8,128)(2,1)} async-done(((bf16[64,1024]{1,0:T(8,128)(2,1)}), bf16[1024,1024]{1,0:T(8,128)(2,1)}) %all-gather.5.cloned.1.call-update) | async-done | bytes 2097168 | tf_op jit(solution)/shard_map/all_gather | solution.py:27
  82.6 10.4 %fusion.11 = f32[1024,1920]{1,0:T(8,128)} fusion(bf16[1024,1024]{1,0:T(8,128)(2,1)} %all-gather.5.cloned.1.call-done, bf16[1024,1920]{1,0:T(8,128)(2,1)} %param.12), kind=kOutput, calls=%fused_computation.23 | convolution fusion | flops 4026531840 | bytes 13893632 | tf_op jit(solution)/shard_map/dot_general | solution.py:37
  93.3 617.8 %all-reduce.3.cloned.1.call-done = (f32[1024,1920]{1,0:T(8,128)}, f32[1024,1920]{1,0:T(8,128)}) async-done(((f32[1024,1920]{1,0:T(8,128)}, f32[1024,1920]{1,0:T(8,128)}), (f32[1024,1920]{1,0:T(8,128)}, f32[1024,1920]{1,0:T(8,128)})) %all-reduce.3.cloned.1.call-update) | async-done | bytes 15728656 | tf_op jit(solution)/shard_map/psum | solution.py:30
  711.1 10.1 fusion.5
  721.2 2.0 copy-done.2
  723.2 6.1 fusion.10
  729.3 0.6 copy-done.3
  729.9 0.6 fusion.8
  732.4 85.5 %dynamic-slice_reduce_fusion = bf16[1966080]{0:T(1024)(128)(2,1)} fusion(bf16[1,1,1966592]{2,1,0:T(2,128)(2,1)} %param.14, s32[]{:T(128)S(6)} %select_n.18), kind=kLoop, calls=%fused_computation.12 | loop fusion | bytes 7864324 | tf_op jit(solution)/shard_map/dynamic_slice | solution.py:18
  817.9 8.2 all_to_all.22
  826.1 4.8 copy.18
  830.9 4.5 all-to-all-start.1
  835.5 0.3 reduce-scatter.5.cloned.1.call-start
  835.8 9.8 fusion.12
  847.5 85.5 %dynamic-slice_reduce_fusion.1 = bf16[1966080]{0:T(1024)(128)(2,1)} fusion(bf16[1,1,1966592]{2,1,0:T(2,128)(2,1)} %param.13, s32[]{:T(128)S(6)} %select_n.17), kind=kLoop, calls=%fused_computation.13 | loop fusion | bytes 7864324 | tf_op jit(solution)/shard_map/dynamic_slice | solution.py:18
  933.0 8.2 all_to_all.20
  941.2 4.9 copy.17
  946.1 5.7 all-to-all-start
  951.8 6.1 convert_element_type.51
  957.9 9.2 copy.19
  967.1 9.1 fusion.7
  976.2 6.4 copy.20
  982.6 22.1 %all-to-all-done = bf16[64,16,1920]{2,0,1:T(8,128)(2,1)} async-done(((bf16[64,16,1920]{2,0,1:T(8,128)(2,1)}), bf16[64,16,1920]{2,0,1:T(8,128)(2,1)}, u32[]{:S(2)}, u32[]{:S(2)}) %all-to-all-start) | async-done | bytes 3932192 | tf_op jit(solution)/shard_map/all_to_all | solution.py:48
  1004.8 8.8 fusion.6
  1013.6 1.6 convert_element_type.37
  1015.2 1.6 convert_element_type.39
  (24 shorter events, 0.6 us)
Async XLA Ops:
  7.2 0.9 copy-start
  7.2 39.7 %all-gather.3.cloned.1.call-start = ((), (), s32[]{:S(2)}) async-start(), calls=%async_computation.4 | async-start | bytes 2228224 | tf_op jit(solution)/shard_map/all_gather | solution.py:26
  9.6 73.1 %all-gather.5.cloned.1.call-start = ((), (), s32[]{:S(2)}) async-start(), calls=%async_computation.6 | async-start | bytes 2228224 | tf_op jit(solution)/shard_map/all_gather | solution.py:27
  10.3 700.8 %all-reduce.3.cloned.1.call-start = ((), (), s32[]{:S(2)}) async-start(), calls=%async_computation.8 | async-start | bytes 31457280 | tf_op jit(solution)/shard_map/psum | solution.py:30
  93.1 920.5 %reduce-scatter.3.cloned.1.call-start = ((), (), s32[]{:S(2)}) async-start(), calls=%async_computation.5 | async-start | bytes 4456448 | tf_op jit(solution)/shard_map/reduce_scatter | solution.py:34
  711.1 12.0 %copy-start.4 = (bf16[1024,1920]{1,0:T(8,128)(2,1)S(1)}, bf16[1024,1920]{1,0:T(8,128)(2,1)}, u32[]{:S(2)}) copy-start(bf16[1024,1920]{1,0:T(8,128)(2,1)} %param.12) | copy-start | bytes 11796484
  721.2 2.0 copy-start.2
  729.3 0.7 copy-start.3
  830.9 115.1 %all-to-all-start.1 = ((bf16[64,16,1920]{2,0,1:T(8,128)(2,1)}), bf16[64,16,1920]{2,0,1:T(8,128)(2,1)}, u32[]{:S(2)}, u32[]{:S(2)}) async-start(bf16[64,16,1920]{2,0,1:T(8,128)(2,1)} %copy.18), calls=%async_computation.3 | async-start | bytes 7864320 | tf_op jit(solution)/shard_map/all_to_all | solution.py:49
  835.5 179.7 %reduce-scatter.5.cloned.1.call-start = ((), (), s32[]{:S(2)}) async-start(), calls=%async_computation.7 | async-start | bytes 4456448 | tf_op jit(solution)/shard_map/reduce_scatter | solution.py:41
  946.1 58.7 %all-to-all-start = ((bf16[64,16,1920]{2,0,1:T(8,128)(2,1)}), bf16[64,16,1920]{2,0,1:T(8,128)(2,1)}, u32[]{:S(2)}, u32[]{:S(2)}) async-start(bf16[64,16,1920]{2,0,1:T(8,128)(2,1)} %copy.17), calls=%async_computation.2 | async-start | bytes 7864320 | tf_op jit(solution)/shard_map/all_to_all | solution.py:48
  957.9 9.2 copy-start.6
  976.2 28.6 %copy-start.5 = (bf16[1024,1024]{1,0:T(8,128)(2,1)S(1)}, bf16[1024,1024]{1,0:T(8,128)(2,1)}, u32[]{:S(2)}) copy-start(bf16[1024,1024]{1,0:T(8,128)(2,1)} %all-gather.3.cloned.1.call-done) | copy-start | bytes 6291460
  1004.8 12.1 %copy-start.1 = (bf16[96,1024]{1,0:T(8,128)(2,1)S(1)}, bf16[96,1024]{1,0:T(8,128)(2,1)}, u32[]{:S(2)}) copy-start(bf16[96,1024]{1,0:T(8,128)(2,1)} %param.8) | copy-start | bytes 589828
Sparse Core Ops, SparseCore 0:
  10.3 36.5 all-gather.2
  48.6 34.0 all-gather.4
  93.2 617.8 all-reduce.2
  729.4 71.1 reduce-scatter.2
  845.7 85.4 reduce-scatter.4
where the time goes:
time: 1030 us; the launch traced here: 1020 us
  waiting for transfers between devices  703 us (68%)
  local copies, waits for them, and re-layouts  217 us (21%)
  matrix products  54.6 us (5%)
  other arithmetic  20.8 us (2%)
  between operations  17.7 us (2%)
  starting transfers between devices  10.9 us (1%)
    psum x1, waiting for transfers between devices, body(): hidden = lax.psum(partial_hidden, 'narrow')  618 us
    dynamic_slice x2, local copies, waits for them, and re-layouts, shard_matrix(): segment = lax.dynamic_slice_in_dim(buffer, start, shard_rows * full_width)  171 us
    all_gather x1, waiting for transfers between devices, body(): lax.all_gather(picked, 'wide', axis=0, tiled=True)  36.5 us
    all_gather x1, waiting for transfers between devices, body(): lax.all_gather(grad_out, 'wide', axis=0, tiled=True)  25.4 us
    all_to_all x1, waiting for transfers between devices, body(): lax.all_to_all(up_segment, 'wide', split_axis=1, concat_axis=0, tiled=True)  22.1 us
  transfers between devices with their start and end apart: 7, of which 4 were waited for; matrix products, arithmetic and copies ran while one was open for 24% of the time, Pallas kernels for 0%

commit v1 on v0

v1 whole, which is shorter than its diff:
```python
import functools

import jax
import jax.numpy as jnp
from jax import lax
from jax.experimental import pallas as pl
from jax.experimental.pallas import tpu as pltpu
from jax.sharding import PartitionSpec as P

SLACK = 512
MIB = 2**20
BF16 = jnp.bfloat16
F32 = jnp.float32
WIDE = "wide"
NARROW = "narrow"

CORE_SWAP = [(k, k ^ 1) for k in range(16)]
Z_SWAP = [(k, k ^ 8) for k in range(16)]
X_SHIFT = [[(k, (k & 8) | ((k + 2 * d) & 7)) for k in range(16)] for d in range(4)]
ZHI_SWAP = [(k, k ^ 1) for k in range(8)]
Y_RIGHT = [(k, (k + 2) % 8) for k in range(8)]
Y_LEFT = [(k, (k - 2) % 8) for k in range(8)]
PLANES = [list(range(8)), list(range(8, 16))]
CB = 384
DB = 256


def sds(shape, dtype):
    return jax.ShapeDtypeStruct(shape, dtype)


def cost(flops, nbytes):
    return pl.CostEstimate(flops=int(flops), bytes_accessed=int(nbytes), transcendentals=0)


def gelu_parts(hidden):
    normal_cdf = 0.5 * (1.0 + jax.scipy.special.erf(hidden * 0.7071067811865476))
    density = jnp.exp(-0.5 * hidden * hidden) * 0.3989422804014327
    return (hidden * normal_cdf, normal_cdf + hidden * density)


HBM = pl.BlockSpec(memory_space=pl.ANY)


def call(kernel, place, grid, ins, outs, scratch, mib, work, name, after=()):
    n, m = len(ins), len(after)

    def run(s_ref, *refs):
        kernel(s_ref, *refs[:n], *refs[n + m :])

    return pl.pallas_call(
        run,
        out_shape=[shape for shape, _, _ in outs],
        grid_spec=pltpu.PrefetchScalarGridSpec(
            num_scalar_prefetch=1,
            grid=grid,
            in_specs=[pl.BlockSpec(block, index) for _, block, index in ins] + [HBM] * m,
            out_specs=[pl.BlockSpec(block, index) for _, block, index in outs],
            scratch_shapes=scratch,
        ),
        compiler_params=pltpu.CompilerParams(vmem_limit_bytes=mib * MIB),
        cost_estimate=cost(*work),
        name=name,
    )(place, *[a for a, _, _ in ins], *after)


def whole(a):
    zeros = (0,) * a.ndim
    return (a, a.shape, lambda i, s: zeros)


def col(a):
    return (a, (a.shape[0], CB), lambda j, s: (0, j))


def pick_kernel(s_ref, ids_ref, stash_ref, grad_ref, out_ref, wide, rows):
    tokens = grad_ref.shape[0]
    n = tokens // 4
    wide[...] = stash_ref[...].astype(F32)
    for d in range(4):
        group = (s_ref[0] + d) % 4
        at = tokens + d * n
        out_ref[at : at + n] = grad_ref[pl.ds(pl.multiple_of(group * n, n), n)]
        for i in range(n):
            row = ids_ref[group * n + i] - s_ref[5]
            rows[d * n + i : d * n + i + 1] = wide[pl.ds(row, 1)]
    out_ref[:tokens] = rows[...].astype(BF16)


def simple_call(kernel, ins, outs, scratch, nbytes, name, after=(), mib=16):
    n, m = len(ins), len(after)

    def run(*refs):
        kernel(*refs[:n], *refs[n + m :])

    def spec(a):
        return pl.BlockSpec(memory_space=pltpu.SMEM if a.dtype == jnp.int32 else pltpu.VMEM)

    return pl.pallas_call(
        run,
        out_shape=outs,
        in_specs=[spec(a) for a in ins] + [HBM] * m,
        out_specs=[pl.BlockSpec(memory_space=pltpu.VMEM)] * len(outs),
        scratch_shapes=scratch,
        compiler_params=pltpu.CompilerParams(vmem_limit_bytes=mib * MIB),
        cost_estimate=cost(0, nbytes),
        name=name,
    )(*ins, *after)


def pick(place, ids, stash, grad):
    return simple_call(
        pick_kernel,
        [place, ids, stash, grad],
        [sds((2 * grad.shape[0], grad.shape[1]), BF16)],
        [pltpu.VMEM(stash.shape, F32), pltpu.VMEM(grad.shape, F32)],
        2e6,
        "pick",
    )[0]


def hold(x, after):
    return pl.pallas_call(
        lambda *refs: None,
        out_shape=sds(x.shape, x.dtype),
        in_specs=[HBM] * (1 + len(after)),
        out_specs=HBM,
        input_output_aliases={0: 0},
        cost_estimate=cost(0, 0),
        name="hold",
    )(x, *after)


def join_kernel(*refs):
    at = 0
    for ref in refs[:-1]:
        refs[-1][at : at + ref.shape[0]] = ref[...]
        at += ref.shape[0]


def join(blocks, name, after=()):
    rows = sum(b.shape[0] for b in blocks)
    return simple_call(join_kernel, blocks, [sds((rows, *blocks[0].shape[1:]), BF16)], [], 2e6, name, after)[0]


STEP = 16


def relay_kernel(s_ref, up_ref, down_ref, own_ref, over_ref, seg, rows, sem):
    parts, _, width = rows.shape
    plane = parts // 2
    line = parts * width
    chunks = own_ref.shape[2] // STEP
    z = s_ref[2]
    for i, ref in enumerate((up_ref, down_ref)):
        for c in range(chunks):
            at = pl.multiple_of(s_ref[3 + i] + c * STEP * line, 128)
            k = i * chunks + c
            pltpu.make_async_copy(ref.at[:, :, pl.ds(at, STEP * line)], seg.at[k], sem.at[k]).start()
    for i, ref in enumerate((up_ref, down_ref)):
        for c in range(chunks):
            k = i * chunks + c
            pltpu.make_async_copy(ref.at[:, :, pl.ds(0, STEP * line)], seg.at[k], sem.at[k]).wait()

            @pl.loop(0, STEP)
            def _(r):
                for w in range(parts):
                    at = pl.multiple_of(r * line + w * width, 128)
                    rows[w, pl.ds(r, 1), :] = seg[k, 0, :, pl.ds(at, width)].astype(F32)

            @pl.loop(0, plane)
            def _(w):
                own_ref[w, i, c * STEP : (c + 1) * STEP] = rows[z * plane + w].astype(BF16)
                over_ref[w, i, c * STEP : (c + 1) * STEP] = rows[(1 - z) * plane + w].astype(BF16)


def relay(place, acc_up, acc_down, width, parts, after=()):
    line = width * parts
    n_rows = (acc_up.shape[2] - SLACK) // line
    plane = parts // 2
    n = len(after)

    def run(s_ref, up_ref, down_ref, *refs):
        relay_kernel(s_ref, up_ref, down_ref, *refs[n:])

    return pl.pallas_call(
        run,
        out_shape=[sds((plane, 2, n_rows, width), BF16)] * 2,
        in_specs=[pl.BlockSpec(memory_space=pltpu.SMEM)] + [HBM] * (2 + n),
        out_specs=[pl.BlockSpec(memory_space=pltpu.VMEM)] * 2,
        scratch_shapes=[
            pltpu.VMEM((2 * n_rows // STEP, 1, 1, STEP * line), BF16),
            pltpu.VMEM((parts, STEP, width), F32),
            pltpu.SemaphoreType.DMA((2 * n_rows // STEP,)),
        ],
        compiler_params=pltpu.CompilerParams(vmem_limit_bytes=32 * MIB),
        cost_estimate=cost(0, 32e6),
        name="relay",
    )(place, acc_up, acc_down, *after)


def rows_of(ref0, ref1):
    depth = ref0.shape[-1]
    return jnp.concatenate([ref0[...].reshape(-1, depth), ref1[...].reshape(-1, depth)], axis=0)


def far_kernel(s_ref, x0_ref, x1_ref, g0_ref, g1_ref, up_ref, down_ref, a_ref, b_ref):
    half = a_ref.shape[1]
    for i, (r0, r1, w_ref) in enumerate(((x0_ref, x1_ref, up_ref), (g0_ref, g1_ref, down_ref))):
        total = jnp.dot(rows_of(r0, r1), w_ref[...], preferred_element_type=F32)
        a_ref[i] = total[:half].astype(BF16)
        b_ref[i] = total[half:].astype(BF16)


def near_kernel(s_ref, r0_ref, r1_ref, l0_ref, l1_ref, w_ref, a_ref, b_ref, right_ref, left_ref):
    half = a_ref.shape[1]
    right = jnp.dot(rows_of(r0_ref, r1_ref), w_ref[...], preferred_element_type=F32)
    right_ref[:half] = (right[:half] + a_ref[0].astype(F32)).astype(BF16)
    right_ref[half:] = right[half:].astype(BF16)
    left = jnp.dot(rows_of(l0_ref, l1_ref), w_ref[...], preferred_element_type=F32)
    left_ref[:half] = left[:half].astype(BF16)
    left_ref[half:] = (left[half:] + b_ref[0].astype(F32)).astype(BF16)


def own_kernel(s_ref, x0_ref, x1_ref, w_ref, p1_ref, p3_ref, keep_ref, send_ref):
    half = keep_ref.shape[0]
    total = jnp.dot(rows_of(x0_ref, x1_ref), w_ref[...], preferred_element_type=F32)
    total = total + p1_ref[...].astype(F32) + p3_ref[...].astype(F32)
    first = s_ref[1] == 0
    keep_ref[...] = jnp.where(first, total[:half], total[half:])
    send_ref[...] = jnp.where(first, total[half:], total[:half]).astype(BF16)


def rows_spec(a, i, k):
    blocks, _, _, r, depth = a.shape
    return (a, (blocks, None, 1, r, depth), lambda j, s: (0, i, k, 0, 0))


def layer(a, i):
    return (a, (1, a.shape[1], CB), lambda j, s: (i, 0, j))


def half_rows(x):
    return x[0].shape[0] * x[0].shape[3]


def feature_call(kernel, place, rows, ws, extra, outs, name, after=()):
    depth, width = ws[0].shape
    m = 128 * len(rows)
    return call(
        kernel,
        place,
        (width // CB,),
        rows + [col(w) for w in ws] + extra,
        outs,
        [],
        20,
        (2 * m * depth * width, 2 * depth * width + 2 * m * width),
        name,
        after,
    )


def far_sum(place, x, w_up, w_down, after=()):
    width = w_up.shape[1]
    out = layer(sds((2, half_rows(x), width), BF16), 0)
    out = (out[0], (2, half_rows(x), CB), lambda j, s: (0, 0, j))
    rows = [rows_spec(a, i, 2) for i in range(2) for a in x]
    a, b = feature_call(far_kernel, place, rows, (w_up, w_down), [], [out, out], "far", after)
    return (lax.ppermute(a, NARROW, Y_RIGHT), lax.ppermute(b, NARROW, Y_LEFT)), a


def near_sum(place, x, i, w, terms, tag, after=()):
    out = col(sds((2 * half_rows(x), w.shape[1]), BF16))
    rows = [rows_spec(a, i, k) for k in (1, 3) for a in x]
    extra = [layer(t, i) for t in terms]
    right, left = feature_call(near_kernel, place, rows, (w,), extra, [out, out], tag + "_near", after)
    return (lax.ppermute(right, NARROW, Y_RIGHT), lax.ppermute(left, NARROW, Y_LEFT)), right


def own_sum(place, x, i, w, terms, tag, after=()):
    outs = [col(sds((half_rows(x), w.shape[1]), dtype)) for dtype in (F32, BF16)]
    rows = [rows_spec(a, i, 0) for a in x]
    keep, send = feature_call(own_kernel, place, rows, (w,), [col(t) for t in terms], outs, tag + "_own", after)
    return keep, lax.ppermute(send, NARROW, ZHI_SWAP), send


def narrow_gather(mine, other, tag, after):
    half = mine.shape[0]
    own = join([mine, other], "join_" + tag, after)
    prev, nxt = lax.ppermute(own, NARROW, Y_RIGHT), lax.ppermute(own, NARROW, Y_LEFT)
    far_m, far_o = lax.ppermute(prev[:half], NARROW, Y_RIGHT), lax.ppermute(nxt[half:], NARROW, Y_LEFT)
    return [own, nxt, prev], [far_m, far_o]


def rows_kernel(s_ref, *refs):
    pieces, w_ref, out0_ref, out1_ref, held = refs[:-4], refs[-4], refs[-3], refs[-2], refs[-1]
    groups, _, half, width = held.shape

    @pl.when(pl.program_id(0) == 0)
    def _():
        at = 0
        for ref in pieces:
            for i in range(ref.shape[0] // half):
                second = s_ref[1] if at % 2 == 0 else 1 - s_ref[1]
                held[at // 2, second] = ref[i * half : (i + 1) * half]
                at += 1

    total = lax.dot_general(
        held[...].reshape(-1, width), w_ref[...], (((1,), (1,)), ((), ())), preferred_element_type=F32
    )
    for g in range(groups):
        at = g * 2 * half
        out0_ref[g] = total[at : at + half]
        out1_ref[g] = total[at + half : at + 2 * half]


def rows_call(place, pieces, half, w, name, after=()):
    width = pieces[0].shape[1]
    depth = w.shape[0]
    groups = sum(a.shape[0] for a in pieces) // (2 * half)

    def out():
        return (sds((groups, half, depth), F32), (groups, half, DB), lambda j, s: (0, 0, j))

    return call(
        rows_kernel,
        place,
        (depth // DB,),
        [whole(a) for a in pieces] + [(w, (DB, width), lambda j, s: (j, 0))],
        [out(), out()],
        [pltpu.VMEM((groups, 2, half, width), BF16)],
        30,
        (4 * groups * half * depth * width, 2 * depth * width + 4 * groups * half * (width + 4 * depth)),
        name,
        after,
    )


def merge_kernel(*refs):
    own_ref, outs = refs[-4], refs[-3:]
    n = (len(refs) - 4) // 2
    b = own_ref.shape[1]
    at = 0
    for i in range(n):
        for g in range(refs[i].shape[0]):
            own_ref[at] = refs[i][g, :b] + refs[n + i][g, :b]
            for d in range(1, 4):
                rows = slice(d * b, (d + 1) * b)
                outs[d - 1][at] = (refs[i][g, rows] + refs[n + i][g, rows]).astype(BF16)
            at += 1


def cross_kernel(own_ref, *refs):
    keep_ref, send_ref = refs[-2:]
    r = keep_ref.shape[1]
    for g in range(own_ref.shape[0]):
        total = own_ref[g] + refs[0][g].astype(F32) + refs[1][g].astype(F32) + refs[2][g].astype(F32)
        keep_ref[g] = total[:r]
        send_ref[g] = total[r:].astype(BF16)


def finish_kernel(s_ref, keep_ref, other_ref, out_ref):
    r = keep_ref.shape[1]
    for i, d in enumerate((0, 1, 3, 2)):
        at = pl.multiple_of(((s_ref[0] + d) % 4) * r, r)
        out_ref[pl.ds(at, r)] = (keep_ref[i] + other_ref[i].astype(F32)).astype(BF16)


def wide_sum(place, kept, given, tag, later):
    taken = lax.ppermute(given, WIDE, CORE_SWAP)
    groups, rows, depth = kept.shape
    b, r = rows // 4, rows // 8
    outs = [sds((groups, b, depth), F32)] + [sds((groups, b, depth), BF16)] * 3
    own, *blocks = simple_call(merge_kernel, [kept, taken], outs, [], 8e6, "merge_" + tag, (), 20)
    got = [lax.ppermute(block, WIDE, X_SHIFT[d]) for d, block in zip((1, 2, 3), blocks)]
    outs = [sds((groups, r, depth), F32), sds((groups, r, depth), BF16)]
    keep, send = simple_call(cross_kernel, [own, *got], outs, [], 2e6, "cross_" + tag, later(own))
    other = lax.ppermute(send, WIDE, Z_SWAP)
    outs = [sds((groups * r, depth), BF16)]
    return simple_call(finish_kernel, [place, keep, other], outs, [], 1e6, "finish_" + tag)[0], own, send


def wide_gather(rows, work):
    pair = jnp.stack([rows, lax.ppermute(rows, WIDE, Z_SWAP)])
    after = work(pair)
    blocks = [pair] + [lax.ppermute(pair, WIDE, X_SHIFT[(4 - d) % 4]) for d in (1, 2, 3)]
    mine = join(blocks, "join_rows", after)
    theirs = lax.ppermute(mine, WIDE, CORE_SWAP)
    shape = (mine.shape[0], 2, 4, mine.shape[1] // 8, mine.shape[2])
    return [mine.reshape(shape), theirs.reshape(shape)], after


def update_kernel(s_ref, x0_ref, x1_ref, *refs):
    pieces, own_ref, other_ref, out_ref, turned = refs[:5], refs[5], refs[6], refs[7], refs[8]
    half, cols = pieces[4].shape
    depth = out_ref.shape[0]

    @pl.when(pl.program_id(0) == 0)
    def _():
        for i, g in enumerate((0, 1, 3, 2)):
            for core, ref in enumerate((x0_ref, x1_ref)):
                second = s_ref[1] if core == 0 else 1 - s_ref[1]
                at = pl.multiple_of((2 * i + second) * half, 128)
                turned[:, pl.ds(at, half)] = ref[:, g].reshape(half, depth).T

    rhs = jnp.concatenate([p[...] for p in pieces], axis=0)
    first = s_ref[2] == 0
    own = own_ref[...].reshape(depth // 2, cols)
    other = other_ref[...].reshape(depth // 2, cols)
    for i in range(2):
        at = i * (depth // 2)
        total = jnp.dot(turned[at : at + depth // 2], rhs, preferred_element_type=F32)
        block = jnp.where(first, own, other) if i == 0 else jnp.where(first, other, own)
        out_ref[at : at + depth // 2] = (total + block.astype(F32)).astype(BF16)


def update_call(place, x, k, pieces, own, which, other, name, after=()):
    half, width = pieces[4].shape
    blocks, _, groups, r, depth = x[0].shape
    plane, _, n_rows, _ = other.shape
    return call(
        update_kernel,
        place,
        (width // CB,),
        [(a, (blocks, None, groups, r, depth), lambda j, s: (0, k, 0, 0, 0)) for a in x]
        + [col(a) for a in pieces]
        + [
            (own, (plane, 1, n_rows, CB), lambda j, s: (0, which, 0, j)),
            (other, (plane, 1, n_rows, CB), lambda j, s: (0, which, 0, j)),
        ],
        [col(sds((depth, width), BF16))],
        [pltpu.VMEM((depth, 8 * half), BF16)],
        32,
        (16 * half * depth * width, 16 * half * (depth + width) + 4 * depth * width),
        name,
        after,
    )[0]


def body(x_stash, token_ids, grad_out, w_up, w_down, acc_up, acc_down, offsets):
    narrow, wide = lax.axis_index(NARROW), lax.axis_index(WIDE)
    parts = lax.axis_size(WIDE)
    width = w_up.shape[1]
    where = jnp.stack([narrow // 2, narrow % 2, wide // 8]).astype(jnp.int32)
    base = (wide * x_stash.shape[0]).astype(jnp.int32)
    place = jnp.concatenate([where, offsets.reshape(2), base[None]])

    x, (own, over) = wide_gather(
        pick(place, token_ids, x_stash, grad_out),
        lambda pair: relay(place, acc_up, acc_down, width, parts, (pair,)),
    )
    half = half_rows(x)

    far, far_done = far_sum(place, x, w_up, w_down, ())
    near_h, done = near_sum(place, x, 0, w_up, far, "hidden", (far_done,))
    near_b, done = near_sum(place, x, 1, w_down, far, "back", (done,))
    over = lax.ppermute(hold(over, (far_done,)), WIDE, Z_SWAP)
    own_blocks = lax.all_to_all(hold(own, (far_done,)), WIDE, 0, 0, tiled=True, axis_index_groups=PLANES)
    keep, other, done = own_sum(place, x, 0, w_up, near_h, "hidden", (done,))
    gelu_value, slope = gelu_parts(keep + other.astype(F32))
    mine = gelu_value.astype(BF16)
    act_other = lax.ppermute(mine, NARROW, ZHI_SWAP)
    keep, other, done = own_sum(place, x, 1, w_down, near_b, "back", (act_other,))
    held = hold(over, (done,))
    other_blocks = lax.all_to_all(held, WIDE, 0, 0, tiled=True, axis_index_groups=PLANES)
    act, act_far = narrow_gather(mine, act_other, "act", (done, own_blocks))
    hidden_grad = ((keep + other.astype(F32)) * slope).astype(BF16)
    grad, grad_far = narrow_gather(hidden_grad, lax.ppermute(hidden_grad, NARROW, ZHI_SWAP), "grad", (act_far[0], act_far[1]))
    k0, g0 = rows_call(place, act + act_far, half, w_down, "out_rows", (grad[0],))
    k1, g1 = rows_call(place, grad + grad_far, half, w_up, "grad_rows", (g0, other_blocks))
    results = {}

    def grad_first(own_out):
        results["grad"] = wide_sum(place, k1, g1, "grad", lambda own: ())
        return (results["grad"][1],)

    out_y, _, out_sent = wide_sum(place, k0, g0, "out", grad_first)
    grad_in, own, sent = results["grad"]
    after = (own, out_sent)
    new_up = update_call(place, x, 0, grad + grad_far, own_blocks, 0, other_blocks, "up_update", after)
    new_down = update_call(place, x, 1, act + act_far, own_blocks, 1, other_blocks, "down_update", (new_up, sent))
    return (out_y, grad_in, new_up, new_down)


def solution(mesh):
    in_specs = (
        P("wide", "narrow"),
        P("wide"),
        P("wide", "narrow"),
        P("narrow", "wide"),
        P("narrow", "wide"),
        P("narrow", "wide", None),
        P("narrow", "wide", None),
        P(None, "narrow", "wide"),
    )
    out_specs = (P("wide", "narrow"), P("wide", "narrow"), P("narrow", "wide"), P("narrow", "wide"))
    return jax.shard_map(body, mesh=mesh, in_specs=in_specs, out_specs=out_specs, check_vma=False)
```

time: 1030 us -> 321 us (0.31)
  waiting for transfers between devices: 703 us -> 158 us
  local copies, waits for them, and re-layouts: 217 us -> 30.4 us
  Pallas kernels: 0 us -> 72.2 us
  matrix products: 54.6 us -> 0 us
  starting transfers between devices: 10.9 us -> 56.9 us
  other arithmetic: 20.8 us -> 0.84 us
  between operations: 17.7 us -> 1.05 us
    psum x1 -> x0, waiting for transfers between devices: 618 us -> none  [body(): hidden = lax.psum(partial_hidden, 'narrow')]
    dynamic_slice x2 -> x0, local copies, waits for them, and re-layouts: 171 us -> none  [shard_matrix(): segment = lax.dynamic_slice_in_dim(buffer, start, shard_rows * full_width)]
    ppermute x0 -> x34, waiting for transfers between devices: none -> 158 us  [the longest x2 35.6 us: own_sum(): return (keep, lax.ppermute(send, NARROW, ZHI_SWAP), send)]
    pallas_call x0 -> x23, Pallas kernels: none -> 72.2 us  [the longest x9 58.4 us: call(): pl.pallas_call(run, out_shape=[shape for shape, _, _ in outs], grid_spec=...]
    all_gather x2 -> x0, waiting for transfers between devices: 61.9 us -> none  [the longest x1 36.5 us: body(): lax.all_gather(picked, 'wide', axis=0, tiled=True)]
    dot_general x6 -> x0, matrix products: 54.6 us -> none  [the longest x1 10.4 us: body(): partial_back = jnp.dot(upstream, w_down, preferred_element_type=jnp.float32)]
    ppermute x0 -> x34, starting transfers between devices: none -> 47.8 us  [the longest x6 10.3 us: wide_sum(): lax.ppermute(block, WIDE, X_SHIFT[d])]
    all_to_all x4 -> x0, local copies, waits for them, and re-layouts: 26 us -> none  [the longest x2 13 us: body(): lax.all_to_all(up_segment, 'wide', split_axis=1, concat_axis=0, tiled=True)]
  transfers between devices with their start and end apart: 7 -> 36, of which waited for: 4 -> 15; matrix products, arithmetic and copies ran while one was open for 24% -> 0% of each run, Pallas kernels for 0% -> 20%
where the time goes in v1:
time: 321 us; the launch traced here: 320 us
  waiting for transfers between devices  158 us (49%)
  Pallas kernels  72.2 us (22%)
  starting transfers between devices  56.9 us (18%)
  local copies, waits for them, and re-layouts  30.4 us (9%)
    pallas_call x9, Pallas kernels, call(): pl.pallas_call(run, out_shape=[shape for shape, _, _ in outs], grid_spec=...  58.4 us
    ppermute x2, waiting for transfers between devices, own_sum(): return (keep, lax.ppermute(send, NARROW, ZHI_SWAP), send)  35.6 us
    ppermute x2, waiting for transfers between devices, narrow_gather(): lax.ppermute(own, NARROW, Y_RIGHT)  32.6 us
    unnamed x100, local copies, waits for them, and re-layouts  29.5 us
    ppermute x1, waiting for transfers between devices, far_sum(): lax.ppermute(b, NARROW, Y_LEFT)  16.8 us
    ppermute x2, waiting for transfers between devices, near_sum(): lax.ppermute(left, NARROW, Y_LEFT)  14.5 us
    ppermute x1, waiting for transfers between devices, body(): act_other = lax.ppermute(mine, NARROW, ZHI_SWAP)  13.1 us
    ppermute x6, waiting for transfers between devices, wide_sum(): lax.ppermute(block, WIDE, X_SHIFT[d])  10.5 us
  transfers between devices with their start and end apart: 36, of which 15 were waited for; matrix products, arithmetic and copies ran while one was open for 0% of the time, Pallas kernels for 20%

profile of v1, /device:TPU:0, one launch (start us, length us, event | category | flops | bytes accessed | tf_op | source)
XLA Modules:
  0.0 319.7 jit_solution(2228693619227583882)
XLA Ops:
  6.7 6.3 %collective-permute-done = bf16[128,1024]{1,0:T(8,128)(2,1)S(1)} collective-permute-done((bf16[128,1024]{1,0:T(8,128)(2,1)S(1)}, bf16[128,1024]{1,0:T(8,128)(2,1)S(1)}, u32[]{:S(2)}, u32[]{:S(2)}) %collective-permute-start) | collective-permute-done | bytes 262176 | tf_op jit(solution)/shard_map/ppermute | solution.py:385
  18.8 3.2 %copy-done.13 = bf16[1,1,1966592]{2,1,0:T(2,128)(2,1)S(1)} copy-done((bf16[1,1,1966592]{2,1,0:T(2,128)(2,1)S(1)}, bf16[1,1,1966592]{2,1,0:T(2,128)(2,1)}, u32[]{:S(2)}) %copy-start.13) | copy-done | bytes 3933208
  22.0 8.0 %relay.1 = (bf16[8,2,64,1920]{3,2,1,0:T(8,128)(2,1)S(1)}, bf16[8,2,64,1920]{3,2,1,0:T(8,128)(2,1)S(1)}) custom-call(s32[6]{0:T(128)S(1)} %concatenate.3.refs_0_.s_ref, bf16[1,1,1966592]{2,1,0:T(2,128)(2,1)S(1)} %copy-done.13, bf16[1,1,1966592]{2,1,0:T(2,128)(2,1)} %down_ref.1, bf16[2,128,1024]{2,1,0:T(8,128)(2,1)S(1)} %pad_maximum_fusion.refs_0_), custom_call_target="tpu_custom_call" | custom-call | bytes 32000000 | tf_op jit(solution)/shard_map/relay/pallas_call | solution.py:186
  30.1 9.5 %collective-permute-done.2.refs_2_ = bf16[2,128,1024]{2,1,0:T(8,128)(2,1)S(1)} collective-permute-done((bf16[2,128,1024]{2,1,0:T(8,128)(2,1)S(1)}, bf16[2,128,1024]{2,1,0:T(8,128)(2,1)S(1)}, u32[]{:S(2)}, u32[]{:S(2)}) %collective-permute-start.2) | collective-permute-done | bytes 524320 | tf_op jit(solution)/shard_map/ppermute | solution.py:387
  39.8 4.1 %collective-permute-done.4 = bf16[8,128,1024]{2,1,0:T(8,128)(2,1)S(1)} collective-permute-done((bf16[8,128,1024]{2,1,0:T(8,128)(2,1)S(1)}, bf16[8,128,1024]{2,1,0:T(8,128)(2,1)S(1)}, u32[]{:S(2)}, u32[]{:S(2)}) %collective-permute-start.4) | collective-permute-done | bytes 2097184 | tf_op jit(solution)/shard_map/ppermute | solution.py:389
  44.0 5.8 %far.1 = (bf16[2,128,1920]{2,1,0:T(8,128)(2,1)}, bf16[2,128,1920]{2,1,0:T(8,128)(2,1)S(1)}) custom-call(s32[6]{0:T(128)S(1)} %concatenate.3.refs_0_.s_ref, bf16[8,2,4,16,1024]{4,3,2,1,0:T(8,128)(2,1)S(1)} %bitcast.9, bf16[8,2,4,16,1024]{4,3,2,1,0:T(8,128)(2,1)S(1)} %bitcast.19, bf16[8,2,4,16,1024]{4,3,2,1,0:T(8,128)(2,1)S(1)} %bitcast.10, ...), custom_call_target="tpu_custom_call" | custom-call | flops 2013265920 | bytes 5898240 | tf_op jit(solution)/shard_map/far/pallas_call | solution.py:51
  52.3 3.0 collective-permute-start.6
  55.3 4.5 %all-to-all-start = ((bf16[8,2,64,1920]{3,2,1,0:T(8,128)(2,1)}), bf16[8,2,64,1920]{3,2,1,0:T(8,128)(2,1)}, u32[]{:S(2)}, u32[]{:S(2)}) async-start(bf16[8,2,64,1920]{3,2,1,0:T(8,128)(2,1)} %hold.3), calls=%async_computation | async-start | bytes 7864320 | tf_op jit(solution)/shard_map/all_to_all | solution.py:459
  59.9 16.8 %collective-permute-done.6.refs_6_ = bf16[2,128,1920]{2,1,0:T(8,128)(2,1)S(1)} collective-permute-done((bf16[2,128,1920]{2,1,0:T(8,128)(2,1)}, bf16[2,128,1920]{2,1,0:T(8,128)(2,1)S(1)}, u32[]{:S(2)}, u32[]{:S(2)}) %collective-permute-start.6) | collective-permute-done | bytes 983072 | tf_op jit(solution)/shard_map/ppermute | solution.py:270
  76.7 3.4 %collective-permute-done.5.refs_5_ = bf16[2,128,1920]{2,1,0:T(8,128)(2,1)} collective-permute-done((bf16[2,128,1920]{2,1,0:T(8,128)(2,1)}, bf16[2,128,1920]{2,1,0:T(8,128)(2,1)}, u32[]{:S(2)}, u32[]{:S(2)}) %collective-permute-start.5) | collective-permute-done | bytes 983072 | tf_op jit(solution)/shard_map/ppermute | solution.py:270
  83.8 6.1 %hidden_near.1 = (bf16[256,1920]{1,0:T(8,128)(2,1)S(1)}, bf16[256,1920]{1,0:T(8,128)(2,1)S(1)}) custom-call(s32[6]{0:T(128)S(1)} %concatenate.3.refs_0_.s_ref, bf16[8,2,4,16,1024]{4,3,2,1,0:T(8,128)(2,1)S(1)} %bitcast.11, bf16[8,2,4,16,1024]{4,3,2,1,0:T(8,128)(2,1)S(1)} %bitcast.21, bf16[8,2,4,16,1024]{4,3,2,1,0:T(8,128)(2,1)S(1)} %bitcast.12, ...), custom_call_target="tpu_custom_call" | custom-call | flops 2013265920 | bytes 5898240 | tf_op jit(solution)/shard_map/hidden_near/pallas_call | solution.py:51
  92.0 5.8 %back_near.1 = (bf16[256,1920]{1,0:T(8,128)(2,1)S(1)}, bf16[256,1920]{1,0:T(8,128)(2,1)S(1)}) custom-call(s32[6]{0:T(128)S(1)} %concatenate.3.refs_0_.s_ref, bf16[8,2,4,16,1024]{4,3,2,1,0:T(8,128)(2,1)S(1)} %bitcast.13, bf16[8,2,4,16,1024]{4,3,2,1,0:T(8,128)(2,1)S(1)} %bitcast.23, bf16[8,2,4,16,1024]{4,3,2,1,0:T(8,128)(2,1)S(1)} %bitcast.14, ...), custom_call_target="tpu_custom_call" | custom-call | flops 2013265920 | bytes 5898240 | tf_op jit(solution)/shard_map/back_near/pallas_call | solution.py:51
  97.7 14.5 %collective-permute-done.8.refs_4_ = bf16[256,1920]{1,0:T(8,128)(2,1)S(1)} collective-permute-done((bf16[256,1920]{1,0:T(8,128)(2,1)S(1)}, bf16[256,1920]{1,0:T(8,128)(2,1)S(1)}, u32[]{:S(2)}, u32[]{:S(2)}) %collective-permute-start.8) | collective-permute-done | bytes 983072 | tf_op jit(solution)/shard_map/ppermute | solution.py:278
  113.7 3.7 %hidden_own.1 = (f32[128,1920]{1,0:T(8,128)S(1)}, bf16[128,1920]{1,0:T(8,128)(2,1)S(1)}) custom-call(s32[6]{0:T(128)S(1)} %concatenate.3.refs_0_.s_ref, bf16[8,2,4,16,1024]{4,3,2,1,0:T(8,128)(2,1)S(1)} %bitcast.15, bf16[8,2,4,16,1024]{4,3,2,1,0:T(8,128)(2,1)S(1)} %bitcast.25, bf16[1024,1920]{1,0:T(8,128)(2,1)S(1)} %copy-done.9, ...), custom_call_target="tpu_custom_call" | custom-call | flops 1006632960 | bytes 4915200 | tf_op jit(solution)/shard_map/hidden_own/pallas_call | solution.py:51
  117.4 3.7 %collective-permute-start.9 = (bf16[128,1920]{1,0:T(8,128)(2,1)S(1)}, bf16[128,1920]{1,0:T(8,128)(2,1)S(1)}, u32[]{:S(2)}, u32[]{:S(2)}) collective-permute-start(bf16[128,1920]{1,0:T(8,128)(2,1)S(1)} %get-tuple-element.40), channel_id=1, source_target_pairs={{0,1},{1,0},{2,3},{3,2},{4,5},{5,4},{6,7},{7,6},{8,9},{9,8},{10,11... | collective-permute-start | bytes 1474568 | tf_op jit(solution)/shard_map/ppermute | solution.py:285
  121.4 2.9 collective-permute-start.12
  124.3 27.3 %collective-permute-done.9 = bf16[128,1920]{1,0:T(8,128)(2,1)S(1)} collective-permute-done((bf16[128,1920]{1,0:T(8,128)(2,1)S(1)}, bf16[128,1920]{1,0:T(8,128)(2,1)S(1)}, u32[]{:S(2)}, u32[]{:S(2)}) %collective-permute-start.9) | collective-permute-done | bytes 491552 | tf_op jit(solution)/shard_map/ppermute | solution.py:285
  152.7 13.1 %collective-permute-done.10.refs_5_.refs_1_ = bf16[128,1920]{1,0:T(8,128)(2,1)S(1)} collective-permute-done((bf16[128,1920]{1,0:T(8,128)(2,1)S(1)}, bf16[128,1920]{1,0:T(8,128)(2,1)S(1)}, u32[]{:S(2)}, u32[]{:S(2)}) %collective-permute-start.10) | collective-permute-done | bytes 491552 | tf_op jit(solution)/shard_map/ppermute | solution.py:463
  165.9 3.7 %back_own.1 = (f32[128,1920]{1,0:T(8,128)S(1)}, bf16[128,1920]{1,0:T(8,128)(2,1)S(1)}) custom-call(s32[6]{0:T(128)S(1)} %concatenate.3.refs_0_.s_ref, bf16[8,2,4,16,1024]{4,3,2,1,0:T(8,128)(2,1)S(1)} %bitcast.16, bf16[8,2,4,16,1024]{4,3,2,1,0:T(8,128)(2,1)S(1)} %bitcast.26, bf16[1024,1920]{1,0:T(8,128)(2,1)S(1)} %copy-done.4, ...), custom_call_target="tpu_custom_call" | custom-call | flops 1006632960 | bytes 4915200 | tf_op jit(solution)/shard_map/back_own/pallas_call | solution.py:51
  171.4 4.6 %all-to-all-start.1 = ((bf16[8,2,64,1920]{3,2,1,0:T(8,128)(2,1)}), bf16[8,2,64,1920]{3,2,1,0:T(8,128)(2,1)}, u32[]{:S(2)}, u32[]{:S(2)}) async-start(bf16[8,2,64,1920]{3,2,1,0:T(8,128)(2,1)} %hold.5), calls=%async_computation.1 | async-start | bytes 7864320 | tf_op jit(solution)/shard_map/all_to_all | solution.py:466
  182.9 8.3 %collective-permute-done.17 = bf16[128,1920]{1,0:T(8,128)(2,1)S(1)} collective-permute-done((bf16[128,1920]{1,0:T(8,128)(2,1)}, bf16[128,1920]{1,0:T(8,128)(2,1)S(1)}, u32[]{:S(2)}, u32[]{:S(2)}) %collective-permute-start.17) | collective-permute-done | bytes 491552 | tf_op jit(solution)/shard_map/ppermute | solution.py:285
  192.1 12.5 %collective-permute-done.14.refs_2_.refs_4_ = bf16[256,1920]{1,0:T(8,128)(2,1)S(1)} collective-permute-done((bf16[256,1920]{1,0:T(8,128)(2,1)S(1)}, bf16[256,1920]{1,0:T(8,128)(2,1)S(1)}, u32[]{:S(2)}, u32[]{:S(2)}) %collective-permute-start.14) | collective-permute-done | bytes 983072 | tf_op jit(solution)/shard_map/ppermute | solution.py:291
  205.0 3.0 collective-permute-start.16
  208.0 10.3 %collective-permute-done.15.refs_2_.refs_3_.refs_5_ = bf16[128,1920]{1,0:T(8,128)(2,1)S(1)} collective-permute-done((bf16[128,1920]{1,0:T(8,128)(2,1)S(1)}, bf16[128,1920]{1,0:T(8,128)(2,1)S(1)}, u32[]{:S(2)}, u32[]{:S(2)}) %collective-permute-start.15) | collective-permute-done | bytes 491552 | tf_op jit(solution)/shard_map/ppermute | solution.py:292
  221.8 20.2 %collective-permute-done.24.refs_2_.refs_4_ = bf16[256,1920]{1,0:T(8,128)(2,1)S(1)} collective-permute-done((bf16[256,1920]{1,0:T(8,128)(2,1)S(1)}, bf16[256,1920]{1,0:T(8,128)(2,1)S(1)}, u32[]{:S(2)}, u32[]{:S(2)}) %collective-permute-start.24) | collective-permute-done | bytes 983072 | tf_op jit(solution)/shard_map/ppermute | solution.py:291
  246.2 6.9 %out_rows.1 = (f32[4,128,1024]{2,1,0:T(8,128)S(1)}, f32[4,128,1024]{2,1,0:T(8,128)}) custom-call(s32[6]{0:T(128)S(1)} %concatenate.3.refs_0_.s_ref, bf16[256,1920]{1,0:T(8,128)(2,1)S(1)} %join_act.1.refs_0_.refs_2_, bf16[256,1920]{1,0:T(8,128)(2,1)S(1)} %collective-permute-done.13.refs_1_.refs_3_, ...), custom_call_target="tpu_custom_call" | custom-call | flops 4026531840 | bytes 16252928 | tf_op jit(solution)/shard_map/out_rows/pallas_call | solution.py:51
  262.7 6.3 %grad_rows.1 = (f32[4,128,1024]{2,1,0:T(8,128)S(1)}, f32[4,128,1024]{2,1,0:T(8,128)S(1)}) custom-call(s32[6]{0:T(128)S(1)} %concatenate.3.refs_0_.s_ref, bf16[256,1920]{1,0:T(8,128)(2,1)S(1)} %join_grad.1.refs_6_.refs_0_.refs_2_, bf16[256,1920]{1,0:T(8,128)(2,1)S(1)} %copy-done.19, bf16[256,1920]{1,0:T(8,128)(2,1)S(1)} %copy-done.17, ...), custom_call_target="tpu_custom_call" | custom-call | flops 4026531840 | bytes 16252928 | tf_op jit(solution)/shard_map/grad_rows/pallas_call | solution.py:51
  272.6 3.0 collective-permute-start.21
  276.9 4.2 %collective-permute-done.20.refs_1_ = bf16[4,32,1024]{2,1,0:T(8,128)(2,1)S(1)} collective-permute-done((bf16[4,32,1024]{2,1,0:T(8,128)(2,1)S(1)}, bf16[4,32,1024]{2,1,0:T(8,128)(2,1)S(1)}, u32[]{:S(2)}, u32[]{:S(2)}) %collective-permute-start.20) | collective-permute-done | bytes 262176 | tf_op jit(solution)/shard_map/ppermute | solution.py:376
  281.1 6.3 %collective-permute-done.21.refs_2_ = bf16[4,32,1024]{2,1,0:T(8,128)(2,1)S(1)} collective-permute-done((bf16[4,32,1024]{2,1,0:T(8,128)(2,1)S(1)}, bf16[4,32,1024]{2,1,0:T(8,128)(2,1)S(1)}, u32[]{:S(2)}, u32[]{:S(2)}) %collective-permute-start.21) | collective-permute-done | bytes 262176 | tf_op jit(solution)/shard_map/ppermute | solution.py:376
  292.8 10.1 %up_update.1.refs_9_ = bf16[1024,1920]{1,0:T(8,128)(2,1)} custom-call(s32[6]{0:T(128)S(1)} %concatenate.3.refs_0_.s_ref, bf16[8,2,4,16,1024]{4,3,2,1,0:T(8,128)(2,1)S(1)} %bitcast.17, bf16[8,2,4,16,1024]{4,3,2,1,0:T(8,128)(2,1)S(1)} %bitcast.27, bf16[256,1920]{1,0:T(8,128)(2,1)S(1)} %join_grad.1.refs_6_.refs_0_.refs_2_, bf16[256,1920]{1,0:T(8,128)(2,1)S(1)} %copy-done.20, ...), custom_call_target="tpu_custom_call" | custom-call | flops 4026531840 | bytes 13893632 | tf_op jit(solution)/shard_map/up_update/pallas_call | solution.py:51
  308.4 10.1 %down_update.1 = bf16[1024,1920]{1,0:T(8,128)(2,1)} custom-call(s32[6]{0:T(128)S(1)} %concatenate.3.refs_0_.s_ref, bf16[8,2,4,16,1024]{4,3,2,1,0:T(8,128)(2,1)S(1)} %bitcast.18, bf16[8,2,4,16,1024]{4,3,2,1,0:T(8,128)(2,1)S(1)} %bitcast.28, bf16[256,1920]{1,0:T(8,128)(2,1)S(1)} %copy-done.15, bf16[256,1920]{1,0:T(8,128)(2,1)S(1)} %copy-done.24, ...), custom_call_target="tpu_custom_call" | custom-call | flops 4026531840 | bytes 13893632 | tf_op jit(solution)/shard_map/down_update/pallas_call | solution.py:51
  (171 shorter events, 67.4 us)
Async XLA Ops:
  13.1 17.0 %collective-permute-start.3 = (bf16[2,128,1024]{2,1,0:T(8,128)(2,1)S(1)}, bf16[2,128,1024]{2,1,0:T(8,128)(2,1)S(1)}, u32[]{:S(2)}, u32[]{:S(2)}) collective-permute-start(bf16[2,128,1024]{2,1,0:T(8,128)(2,1)S(1)} %pad_maximum_fusion.refs_0_), channel_id=1, source_target_pairs={{0,16},{8,24},{16,32},{24,40},{32,48},{40,56},{48,0},{56,8},{64,80... | collective-permute-start | bytes 1572872 | tf_op jit(solution)/shard_map/ppermute | solution.py:387
  14.6 24.9 %collective-permute-start.2 = (bf16[2,128,1024]{2,1,0:T(8,128)(2,1)S(1)}, bf16[2,128,1024]{2,1,0:T(8,128)(2,1)S(1)}, u32[]{:S(2)}, u32[]{:S(2)}) collective-permute-start(bf16[2,128,1024]{2,1,0:T(8,128)(2,1)S(1)} %pad_maximum_fusion.refs_0_), channel_id=1, source_target_pairs={{0,32},{8,40},{16,48},{24,56},{32,0},{40,8},{48,16},{56,24},{64,96... | collective-permute-start | bytes 1572872 | tf_op jit(solution)/shard_map/ppermute | solution.py:387
  17.4 22.2 %collective-permute-start.1 = (bf16[2,128,1024]{2,1,0:T(8,128)(2,1)S(1)}, bf16[2,128,1024]{2,1,0:T(8,128)(2,1)S(1)}, u32[]{:S(2)}, u32[]{:S(2)}) collective-permute-start(bf16[2,128,1024]{2,1,0:T(8,128)(2,1)S(1)} %pad_maximum_fusion.refs_0_), channel_id=1, source_target_pairs={{0,48},{8,56},{16,0},{24,8},{32,16},{40,24},{48,32},{56,40},{64,11... | collective-permute-start | bytes 1572872 | tf_op jit(solution)/shard_map/ppermute | solution.py:387
  50.8 120.6 %collective-permute-start.27 = (bf16[8,2,64,1920]{3,2,1,0:T(8,128)(2,1)}, bf16[8,2,64,1920]{3,2,1,0:T(8,128)(2,1)}, u32[]{:S(2)}, u32[]{:S(2)}) collective-permute-start(bf16[8,2,64,1920]{3,2,1,0:T(8,128)(2,1)} %hold.4), channel_id=1, source_target_pairs={{0,64},{8,72},{16,80},{24,88},{32,96},{40,104},{48,112},{56,120},{... | collective-permute-start | bytes 11796488 | tf_op jit(solution)/shard_map/ppermute | solution.py:458
  52.3 24.4 %collective-permute-start.6 = (bf16[2,128,1920]{2,1,0:T(8,128)(2,1)}, bf16[2,128,1920]{2,1,0:T(8,128)(2,1)S(1)}, u32[]{:S(2)}, u32[]{:S(2)}) collective-permute-start(bf16[2,128,1920]{2,1,0:T(8,128)(2,1)} %copy-done.47), channel_id=1, source_target_pairs={{0,6},{1,7},{2,0},{3,1},{4,2},{5,3},{6,4},{7,5},{8,14},{9,15},{10,... | collective-permute-start | bytes 2949128 | tf_op jit(solution)/shard_map/ppermute | solution.py:270
  55.3 24.8 %collective-permute-start.5 = (bf16[2,128,1920]{2,1,0:T(8,128)(2,1)}, bf16[2,128,1920]{2,1,0:T(8,128)(2,1)}, u32[]{:S(2)}, u32[]{:S(2)}) collective-permute-start(bf16[2,128,1920]{2,1,0:T(8,128)(2,1)} %get-tuple-element.34.refs_7_.refs_1_), channel_id=1, source_target_pairs={{0,2},{1,3},{2,4},{3,5},{4,6},{5,7},{6,0},{7,1},{8,10},{9,11},{10,... | collective-permute-start | bytes 2949128 | tf_op jit(solution)/shard_map/ppermute | solution.py:270
  55.3 116.0 %all-to-all-start = ((bf16[8,2,64,1920]{3,2,1,0:T(8,128)(2,1)}), bf16[8,2,64,1920]{3,2,1,0:T(8,128)(2,1)}, u32[]{:S(2)}, u32[]{:S(2)}) async-start(bf16[8,2,64,1920]{3,2,1,0:T(8,128)(2,1)} %hold.3), calls=%async_computation | async-start | bytes 7864320 | tf_op jit(solution)/shard_map/all_to_all | solution.py:459
  89.9 22.4 %collective-permute-start.8 = (bf16[256,1920]{1,0:T(8,128)(2,1)S(1)}, bf16[256,1920]{1,0:T(8,128)(2,1)S(1)}, u32[]{:S(2)}, u32[]{:S(2)}) collective-permute-start(bf16[256,1920]{1,0:T(8,128)(2,1)S(1)} %get-tuple-element.37), channel_id=1, source_target_pairs={{0,6},{1,7},{2,0},{3,1},{4,2},{5,3},{6,4},{7,5},{8,14},{9,15},{10,... | collective-permute-start | bytes 2949128 | tf_op jit(solution)/shard_map/ppermute | solution.py:278
  90.1 23.6 %collective-permute-start.7 = (bf16[256,1920]{1,0:T(8,128)(2,1)S(1)}, bf16[256,1920]{1,0:T(8,128)(2,1)S(1)}, u32[]{:S(2)}, u32[]{:S(2)}) collective-permute-start(bf16[256,1920]{1,0:T(8,128)(2,1)S(1)} %get-tuple-element.36.refs_7_), channel_id=1, source_target_pairs={{0,2},{1,3},{2,4},{3,5},{4,6},{5,7},{6,0},{7,1},{8,10},{9,11},{10,... | collective-permute-start | bytes 2949128 | tf_op jit(solution)/shard_map/ppermute | solution.py:278
  117.4 34.2 %collective-permute-start.9 = (bf16[128,1920]{1,0:T(8,128)(2,1)S(1)}, bf16[128,1920]{1,0:T(8,128)(2,1)S(1)}, u32[]{:S(2)}, u32[]{:S(2)}) collective-permute-start(bf16[128,1920]{1,0:T(8,128)(2,1)S(1)} %get-tuple-element.40), channel_id=1, source_target_pairs={{0,1},{1,0},{2,3},{3,2},{4,5},{5,4},{6,7},{7,6},{8,9},{9,8},{10,11... | collective-permute-start | bytes 1474568 | tf_op jit(solution)/shard_map/ppermute | solution.py:285
  121.1 31.6 %collective-permute-start.11 = (bf16[256,1920]{1,0:T(8,128)(2,1)S(1)}, bf16[256,1920]{1,0:T(8,128)(2,1)S(1)}, u32[]{:S(2)}, u32[]{:S(2)}) collective-permute-start(bf16[256,1920]{1,0:T(8,128)(2,1)S(1)} %get-tuple-element.38.refs_5_), channel_id=1, source_target_pairs={{0,2},{1,3},{2,4},{3,5},{4,6},{5,7},{6,0},{7,1},{8,10},{9,11},{10,... | collective-permute-start | bytes 2949128 | tf_op jit(solution)/shard_map/ppermute | solution.py:278
  121.4 31.3 %collective-permute-start.12 = (bf16[256,1920]{1,0:T(8,128)(2,1)S(1)}, bf16[256,1920]{1,0:T(8,128)(2,1)S(1)}, u32[]{:S(2)}, u32[]{:S(2)}) collective-permute-start(bf16[256,1920]{1,0:T(8,128)(2,1)S(1)} %get-tuple-element.41), channel_id=1, source_target_pairs={{0,6},{1,7},{2,0},{3,1},{4,2},{5,3},{6,4},{7,5},{8,14},{9,15},{10,... | collective-permute-start | bytes 2949128 | tf_op jit(solution)/shard_map/ppermute | solution.py:278
  151.9 14.0 %collective-permute-start.10 = (bf16[128,1920]{1,0:T(8,128)(2,1)S(1)}, bf16[128,1920]{1,0:T(8,128)(2,1)S(1)}, u32[]{:S(2)}, u32[]{:S(2)}) collective-permute-start(bf16[128,1920]{1,0:T(8,128)(2,1)S(1)} %multiply_convert_fusion.refs_0_), channel_id=1, source_target_pairs={{0,1},{1,0},{2,3},{3,2},{4,5},{5,4},{6,7},{7,6},{8,9},{9,8},{10,11... | collective-permute-start | bytes 1474568 | tf_op jit(solution)/shard_map/ppermute | solution.py:463
  171.4 84.7 %all-to-all-start.1 = ((bf16[8,2,64,1920]{3,2,1,0:T(8,128)(2,1)}), bf16[8,2,64,1920]{3,2,1,0:T(8,128)(2,1)}, u32[]{:S(2)}, u32[]{:S(2)}) async-start(bf16[8,2,64,1920]{3,2,1,0:T(8,128)(2,1)} %hold.5), calls=%async_computation.1 | async-start | bytes 7864320 | tf_op jit(solution)/shard_map/all_to_all | solution.py:466
  176.0 15.2 %collective-permute-start.17 = (bf16[128,1920]{1,0:T(8,128)(2,1)}, bf16[128,1920]{1,0:T(8,128)(2,1)S(1)}, u32[]{:S(2)}, u32[]{:S(2)}) collective-permute-start(bf16[128,1920]{1,0:T(8,128)(2,1)} %copy-done.27), channel_id=1, source_target_pairs={{0,1},{1,0},{2,3},{3,2},{4,5},{5,4},{6,7},{7,6},{8,9},{9,8},{10,11... | collective-permute-start | bytes 1474568 | tf_op jit(solution)/shard_map/ppermute | solution.py:285
  179.5 25.0 %collective-permute-start.14 = (bf16[256,1920]{1,0:T(8,128)(2,1)S(1)}, bf16[256,1920]{1,0:T(8,128)(2,1)S(1)}, u32[]{:S(2)}, u32[]{:S(2)}) collective-permute-start(bf16[256,1920]{1,0:T(8,128)(2,1)S(1)} %join_act.1.refs_0_.refs_2_), channel_id=1, source_target_pairs={{0,2},{1,3},{2,4},{3,5},{4,6},{5,7},{6,0},{7,1},{8,10},{9,11},{10,... | collective-permute-start | bytes 2949128 | tf_op jit(solution)/shard_map/ppermute | solution.py:291
  181.2 23.8 %collective-permute-start.13 = (bf16[256,1920]{1,0:T(8,128)(2,1)S(1)}, bf16[256,1920]{1,0:T(8,128)(2,1)S(1)}, u32[]{:S(2)}, u32[]{:S(2)}) collective-permute-start(bf16[256,1920]{1,0:T(8,128)(2,1)S(1)} %join_act.1.refs_0_.refs_2_), channel_id=1, source_target_pairs={{0,6},{1,7},{2,0},{3,1},{4,2},{5,3},{6,4},{7,5},{8,14},{9,15},{10,... | collective-permute-start | bytes 2949128 | tf_op jit(solution)/shard_map/ppermute | solution.py:291
  191.7 16.3 %collective-permute-start.18 = (bf16[128,1920]{1,0:T(8,128)(2,1)S(1)}, bf16[128,1920]{1,0:T(8,128)(2,1)S(1)}, u32[]{:S(2)}, u32[]{:S(2)}) collective-permute-start(bf16[128,1920]{1,0:T(8,128)(2,1)S(1)} %fusion.5.refs_0_), channel_id=1, source_target_pairs={{0,1},{1,0},{2,3},{3,2},{4,5},{5,4},{6,7},{7,6},{8,9},{9,8},{10,11... | collective-permute-start | bytes 1474568 | tf_op jit(solution)/shard_map/ppermute | solution.py:469
  204.6 13.8 %collective-permute-start.15 = (bf16[128,1920]{1,0:T(8,128)(2,1)S(1)}, bf16[128,1920]{1,0:T(8,128)(2,1)S(1)}, u32[]{:S(2)}, u32[]{:S(2)}) collective-permute-start(bf16[128,1920]{1,0:T(8,128)(2,1)S(1)} %slice.16), channel_id=1, source_target_pairs={{0,2},{1,3},{2,4},{3,5},{4,6},{5,7},{6,0},{7,1},{8,10},{9,11},{10,... | collective-permute-start | bytes 1474568 | tf_op jit(solution)/shard_map/ppermute | solution.py:292
  205.0 13.4 %collective-permute-start.16 = (bf16[128,1920]{1,0:T(8,128)(2,1)S(1)}, bf16[128,1920]{1,0:T(8,128)(2,1)S(1)}, u32[]{:S(2)}, u32[]{:S(2)}) collective-permute-start(bf16[128,1920]{1,0:T(8,128)(2,1)S(1)} %slice.17), channel_id=1, source_target_pairs={{0,6},{1,7},{2,0},{3,1},{4,2},{5,3},{6,4},{7,5},{8,14},{9,15},{10,... | collective-permute-start | bytes 1474568 | tf_op jit(solution)/shard_map/ppermute | solution.py:292
  218.4 23.5 %collective-permute-start.24 = (bf16[256,1920]{1,0:T(8,128)(2,1)S(1)}, bf16[256,1920]{1,0:T(8,128)(2,1)S(1)}, u32[]{:S(2)}, u32[]{:S(2)}) collective-permute-start(bf16[256,1920]{1,0:T(8,128)(2,1)S(1)} %join_grad.1.refs_6_.refs_0_.refs_2_), channel_id=1, source_target_pairs={{0,2},{1,3},{2,4},{3,5},{4,6},{5,7},{6,0},{7,1},{8,10},{9,11},{10,... | collective-permute-start | bytes 2949128 | tf_op jit(solution)/shard_map/ppermute | solution.py:291
  218.9 23.1 %collective-permute-start.23 = (bf16[256,1920]{1,0:T(8,128)(2,1)S(1)}, bf16[256,1920]{1,0:T(8,128)(2,1)S(1)}, u32[]{:S(2)}, u32[]{:S(2)}) collective-permute-start(bf16[256,1920]{1,0:T(8,128)(2,1)S(1)} %join_grad.1.refs_6_.refs_0_.refs_2_), channel_id=1, source_target_pairs={{0,6},{1,7},{2,0},{3,1},{4,2},{5,3},{6,4},{7,5},{8,14},{9,15},{10,... | collective-permute-start | bytes 2949128 | tf_op jit(solution)/shard_map/ppermute | solution.py:291
  242.0 12.5 %collective-permute-start.25 = (bf16[128,1920]{1,0:T(8,128)(2,1)S(1)}, bf16[128,1920]{1,0:T(8,128)(2,1)S(1)}, u32[]{:S(2)}, u32[]{:S(2)}) collective-permute-start(bf16[128,1920]{1,0:T(8,128)(2,1)S(1)} %slice.18), channel_id=1, source_target_pairs={{0,2},{1,3},{2,4},{3,5},{4,6},{5,7},{6,0},{7,1},{8,10},{9,11},{10,... | collective-permute-start | bytes 1474568 | tf_op jit(solution)/shard_map/ppermute | solution.py:292
  243.9 11.4 %collective-permute-start.26 = (bf16[128,1920]{1,0:T(8,128)(2,1)S(1)}, bf16[128,1920]{1,0:T(8,128)(2,1)S(1)}, u32[]{:S(2)}, u32[]{:S(2)}) collective-permute-start(bf16[128,1920]{1,0:T(8,128)(2,1)S(1)} %slice.19), channel_id=1, source_target_pairs={{0,6},{1,7},{2,0},{3,1},{4,2},{5,3},{6,4},{7,5},{8,14},{9,15},{10,... | collective-permute-start | bytes 1474568 | tf_op jit(solution)/shard_map/ppermute | solution.py:292
  254.5 15.0 %collective-permute-start.19 = (f32[4,128,1024]{2,1,0:T(8,128)}, f32[4,128,1024]{2,1,0:T(8,128)}, u32[]{:S(2)}, u32[]{:S(2)}) collective-permute-start(f32[4,128,1024]{2,1,0:T(8,128)} %get-tuple-element.45.refs_6_), channel_id=1, source_target_pairs={{0,8},{8,0},{16,24},{24,16},{32,40},{40,32},{48,56},{56,48},{64,72... | collective-permute-start | bytes 6291464 | tf_op jit(solution)/shard_map/ppermute | solution.py:371
  272.6 14.8 %collective-permute-start.21 = (bf16[4,32,1024]{2,1,0:T(8,128)(2,1)S(1)}, bf16[4,32,1024]{2,1,0:T(8,128)(2,1)S(1)}, u32[]{:S(2)}, u32[]{:S(2)}) collective-permute-start(bf16[4,32,1024]{2,1,0:T(8,128)(2,1)S(1)} %get-tuple-element.48), channel_id=1, source_target_pairs={{0,32},{8,40},{16,48},{24,56},{32,0},{40,8},{48,16},{56,24},{64,96... | collective-permute-start | bytes 786440 | tf_op jit(solution)/shard_map/ppermute | solution.py:376
  275.6 11.8 %collective-permute-start.22 = (bf16[4,32,1024]{2,1,0:T(8,128)(2,1)S(1)}, bf16[4,32,1024]{2,1,0:T(8,128)(2,1)S(1)}, u32[]{:S(2)}, u32[]{:S(2)}) collective-permute-start(bf16[4,32,1024]{2,1,0:T(8,128)(2,1)S(1)} %get-tuple-element.49), channel_id=1, source_target_pairs={{0,48},{8,56},{16,0},{24,8},{32,16},{40,24},{48,32},{56,40},{64,11... | collective-permute-start | bytes 786440 | tf_op jit(solution)/shard_map/ppermute | solution.py:376
  287.5 15.4 %collective-permute-start.29 = (bf16[4,16,1024]{2,1,0:T(8,128)(2,1)S(1)}, bf16[4,16,1024]{2,1,0:T(8,128)(2,1)S(1)}, u32[]{:S(2)}, u32[]{:S(2)}) collective-permute-start(bf16[4,16,1024]{2,1,0:T(8,128)(2,1)S(1)} %get-tuple-element.54.refs_10_), channel_id=1, source_target_pairs={{0,64},{8,72},{16,80},{24,88},{32,96},{40,104},{48,112},{56,120},{... | collective-permute-start | bytes 393224 | tf_op jit(solution)/shard_map/ppermute | solution.py:379
  287.7 16.4 %collective-permute-start.30 = (bf16[4,32,1024]{2,1,0:T(8,128)(2,1)S(1)}, bf16[4,32,1024]{2,1,0:T(8,128)(2,1)S(1)}, u32[]{:S(2)}, u32[]{:S(2)}) collective-permute-start(bf16[4,32,1024]{2,1,0:T(8,128)(2,1)S(1)} %get-tuple-element.55), channel_id=1, source_target_pairs={{0,16},{8,24},{16,32},{24,40},{32,48},{40,56},{48,0},{56,8},{64,80... | collective-permute-start | bytes 786440 | tf_op jit(solution)/shard_map/ppermute | solution.py:376
  289.3 14.9 %collective-permute-start.31 = (bf16[4,32,1024]{2,1,0:T(8,128)(2,1)S(1)}, bf16[4,32,1024]{2,1,0:T(8,128)(2,1)S(1)}, u32[]{:S(2)}, u32[]{:S(2)}) collective-permute-start(bf16[4,32,1024]{2,1,0:T(8,128)(2,1)S(1)} %get-tuple-element.56), channel_id=1, source_target_pairs={{0,32},{8,40},{16,48},{24,56},{32,0},{40,8},{48,16},{56,24},{64,96... | collective-permute-start | bytes 786440 | tf_op jit(solution)/shard_map/ppermute | solution.py:376
  291.7 12.5 %collective-permute-start.32 = (bf16[4,32,1024]{2,1,0:T(8,128)(2,1)S(1)}, bf16[4,32,1024]{2,1,0:T(8,128)(2,1)S(1)}, u32[]{:S(2)}, u32[]{:S(2)}) collective-permute-start(bf16[4,32,1024]{2,1,0:T(8,128)(2,1)S(1)} %get-tuple-element.57), channel_id=1, source_target_pairs={{0,48},{8,56},{16,0},{24,8},{32,16},{40,24},{48,32},{56,40},{64,11... | collective-permute-start | bytes 786440 | tf_op jit(solution)/shard_map/ppermute | solution.py:376
  304.3 14.2 %collective-permute-start.33 = (bf16[4,16,1024]{2,1,0:T(8,128)(2,1)S(1)}, bf16[4,16,1024]{2,1,0:T(8,128)(2,1)S(1)}, u32[]{:S(2)}, u32[]{:S(2)}) collective-permute-start(bf16[4,16,1024]{2,1,0:T(8,128)(2,1)S(1)} %get-tuple-element.59.refs_10_), channel_id=1, source_target_pairs={{0,64},{8,72},{16,80},{24,88},{32,96},{40,104},{48,112},{56,120},{... | collective-permute-start | bytes 393224 | tf_op jit(solution)/shard_map/ppermute | solution.py:379
  (54 other events, 585.2 us)

commit v2 on v1

--- a/solution.py
+++ b/solution.py
@@ -20,7 +20,6 @@
 ZHI_SWAP = [(k, k ^ 1) for k in range(8)]
 Y_RIGHT = [(k, (k + 2) % 8) for k in range(8)]
 Y_LEFT = [(k, (k - 2) % 8) for k in range(8)]
-PLANES = [list(range(8)), list(range(8, 16))]
 CB = 384
 DB = 256
 
@@ -44,6 +43,9 @@
 
 def call(kernel, place, grid, ins, outs, scratch, mib, work, name, after=()):
     n, m = len(ins), len(after)
+
+    def spec(block, index):
+        return pl.BlockSpec(memory_space=pltpu.HBM) if block is None else pl.BlockSpec(block, index)
 
     def run(s_ref, *refs):
         kernel(s_ref, *refs[:n], *refs[n + m :])
@@ -54,7 +56,7 @@
         grid_spec=pltpu.PrefetchScalarGridSpec(
             num_scalar_prefetch=1,
             grid=grid,
-            in_specs=[pl.BlockSpec(block, index) for _, block, index in ins] + [HBM] * m,
+            in_specs=[spec(block, index) for _, block, index in ins] + [HBM] * m,
             out_specs=[pl.BlockSpec(block, index) for _, block, index in outs],
             scratch_shapes=scratch,
         ),
@@ -87,7 +89,7 @@
     out_ref[:tokens] = rows[...].astype(BF16)
 
 
-def simple_call(kernel, ins, outs, scratch, nbytes, name, after=(), mib=16):
+def simple_call(kernel, ins, outs, scratch, nbytes, name, after=(), mib=50):
     n, m = len(ins), len(after)
 
     def run(*refs):
@@ -146,18 +148,17 @@
 STEP = 16
 
 
-def relay_kernel(s_ref, up_ref, down_ref, own_ref, over_ref, seg, rows, sem):
+def relay_kernel(s_ref, up_ref, down_ref, to_up_ref, to_down_ref, seg, rows, sem):
     parts, _, width = rows.shape
-    plane = parts // 2
     line = parts * width
-    chunks = own_ref.shape[2] // STEP
-    z = s_ref[2]
+    chunks = to_up_ref.shape[1] // STEP
     for i, ref in enumerate((up_ref, down_ref)):
         for c in range(chunks):
             at = pl.multiple_of(s_ref[3 + i] + c * STEP * line, 128)
             k = i * chunks + c
             pltpu.make_async_copy(ref.at[:, :, pl.ds(at, STEP * line)], seg.at[k], sem.at[k]).start()
     for i, ref in enumerate((up_ref, down_ref)):
+        out_ref = (to_up_ref, to_down_ref)[i]
         for c in range(chunks):
             k = i * chunks + c
             pltpu.make_async_copy(ref.at[:, :, pl.ds(0, STEP * line)], seg.at[k], sem.at[k]).wait()
@@ -168,16 +169,14 @@
                     at = pl.multiple_of(r * line + w * width, 128)
                     rows[w, pl.ds(r, 1), :] = seg[k, 0, :, pl.ds(at, width)].astype(F32)
 
-            @pl.loop(0, plane)
+            @pl.loop(0, parts)
             def _(w):
-                own_ref[w, i, c * STEP : (c + 1) * STEP] = rows[z * plane + w].astype(BF16)
-                over_ref[w, i, c * STEP : (c + 1) * STEP] = rows[(1 - z) * plane + w].astype(BF16)
+                out_ref[w, c * STEP : (c + 1) * STEP] = rows[w].astype(BF16)
 
 
 def relay(place, acc_up, acc_down, width, parts, after=()):
     line = width * parts
     n_rows = (acc_up.shape[2] - SLACK) // line
-    plane = parts // 2
     n = len(after)
 
     def run(s_ref, up_ref, down_ref, *refs):
@@ -185,7 +184,7 @@
 
     return pl.pallas_call(
         run,
-        out_shape=[sds((plane, 2, n_rows, width), BF16)] * 2,
+        out_shape=[sds((parts, n_rows, width), BF16)] * 2,
         in_specs=[pl.BlockSpec(memory_space=pltpu.SMEM)] + [HBM] * (2 + n),
         out_specs=[pl.BlockSpec(memory_space=pltpu.VMEM)] * 2,
         scratch_shapes=[
@@ -285,31 +284,47 @@
     return keep, lax.ppermute(send, NARROW, ZHI_SWAP), send
 
 
-def narrow_gather(mine, other, tag, after):
-    half = mine.shape[0]
+def far_gather(pieces, after):
+    _, nxt, prev = pieces
+    half = nxt.shape[0] // 2
+    near = prev[:half], nxt[half:]
+    if after:
+        near = [hold(a, after) for a in near]
+    return [lax.ppermute(near[0], NARROW, Y_RIGHT), lax.ppermute(near[1], NARROW, Y_LEFT)]
+
+
+def narrow_gather(mine, other, tag, after, far=True):
     own = join([mine, other], "join_" + tag, after)
     prev, nxt = lax.ppermute(own, NARROW, Y_RIGHT), lax.ppermute(own, NARROW, Y_LEFT)
-    far_m, far_o = lax.ppermute(prev[:half], NARROW, Y_RIGHT), lax.ppermute(nxt[half:], NARROW, Y_LEFT)
-    return [own, nxt, prev], [far_m, far_o]
+    pieces = [own, nxt, prev]
+    return pieces, far_gather(pieces, ()) if far else None
+
+
+def exchange(blocks):
+    return lax.all_to_all(blocks, WIDE, 0, 0, tiled=True)
 
 
 def rows_kernel(s_ref, *refs):
-    pieces, w_ref, out0_ref, out1_ref, held = refs[:-4], refs[-4], refs[-3], refs[-2], refs[-1]
-    groups, _, half, width = held.shape
+    pieces, (w_ref, out0_ref, out1_ref, held, sem) = refs[:-5], refs[-5:]
+    _, _, half, width = held.shape
 
     @pl.when(pl.program_id(0) == 0)
     def _():
-        at = 0
+        copies = []
         for ref in pieces:
             for i in range(ref.shape[0] // half):
+                at = len(copies)
                 second = s_ref[1] if at % 2 == 0 else 1 - s_ref[1]
-                held[at // 2, second] = ref[i * half : (i + 1) * half]
-                at += 1
+                copy = pltpu.make_async_copy(ref.at[pl.ds(i * half, half)], held.at[at // 2, second], sem.at[at])
+                copy.start()
+                copies.append(copy)
+        for copy in copies:
+            copy.wait()
 
     total = lax.dot_general(
         held[...].reshape(-1, width), w_ref[...], (((1,), (1,)), ((), ())), preferred_element_type=F32
     )
-    for g in range(groups):
+    for g in range(held.shape[0]):
         at = g * 2 * half
         out0_ref[g] = total[at : at + half]
         out1_ref[g] = total[at + half : at + 2 * half]
@@ -327,10 +342,10 @@
         rows_kernel,
         place,
         (depth // DB,),
-        [whole(a) for a in pieces] + [(w, (DB, width), lambda j, s: (j, 0))],
+        [(a, None, None) for a in pieces] + [(w, (DB, width), lambda j, s: (j, 0))],
         [out(), out()],
-        [pltpu.VMEM((groups, 2, half, width), BF16)],
-        30,
+        [pltpu.VMEM((groups, 2, half, width), BF16), pltpu.SemaphoreType.DMA((2 * groups,))],
+        50,
         (4 * groups * half * depth * width, 2 * depth * width + 4 * groups * half * (width + 4 * depth)),
         name,
         after,
@@ -372,7 +387,7 @@
     groups, rows, depth = kept.shape
     b, r = rows // 4, rows // 8
     outs = [sds((groups, b, depth), F32)] + [sds((groups, b, depth), BF16)] * 3
-    own, *blocks = simple_call(merge_kernel, [kept, taken], outs, [], 8e6, "merge_" + tag, (), 20)
+    own, *blocks = simple_call(merge_kernel, [kept, taken], outs, [], 8e6, "merge_" + tag)
     got = [lax.ppermute(block, WIDE, X_SHIFT[d]) for d, block in zip((1, 2, 3), blocks)]
     outs = [sds((groups, r, depth), F32), sds((groups, r, depth), BF16)]
     keep, send = simple_call(cross_kernel, [own, *got], outs, [], 2e6, "cross_" + tag, later(own))
@@ -385,14 +400,14 @@
     pair = jnp.stack([rows, lax.ppermute(rows, WIDE, Z_SWAP)])
     after = work(pair)
     blocks = [pair] + [lax.ppermute(pair, WIDE, X_SHIFT[(4 - d) % 4]) for d in (1, 2, 3)]
-    mine = join(blocks, "join_rows", after)
+    mine = join(blocks, "join_rows")
     theirs = lax.ppermute(mine, WIDE, CORE_SWAP)
     shape = (mine.shape[0], 2, 4, mine.shape[1] // 8, mine.shape[2])
-    return [mine.reshape(shape), theirs.reshape(shape)], after
+    return [mine.reshape(shape), theirs.reshape(shape)], after, mine
 
 
 def update_kernel(s_ref, x0_ref, x1_ref, *refs):
-    pieces, own_ref, other_ref, out_ref, turned = refs[:5], refs[5], refs[6], refs[7], refs[8]
+    pieces, blocks_ref, out_ref, turned = refs[:5], refs[5], refs[6], refs[7]
     half, cols = pieces[4].shape
     depth = out_ref.shape[0]
 
@@ -405,33 +420,24 @@
                 turned[:, pl.ds(at, half)] = ref[:, g].reshape(half, depth).T
 
     rhs = jnp.concatenate([p[...] for p in pieces], axis=0)
-    first = s_ref[2] == 0
-    own = own_ref[...].reshape(depth // 2, cols)
-    other = other_ref[...].reshape(depth // 2, cols)
-    for i in range(2):
-        at = i * (depth // 2)
-        total = jnp.dot(turned[at : at + depth // 2], rhs, preferred_element_type=F32)
-        block = jnp.where(first, own, other) if i == 0 else jnp.where(first, other, own)
-        out_ref[at : at + depth // 2] = (total + block.astype(F32)).astype(BF16)
-
-
-def update_call(place, x, k, pieces, own, which, other, name, after=()):
+    total = jnp.dot(turned[...], rhs, preferred_element_type=F32)
+    out_ref[...] = (total + blocks_ref[...].reshape(depth, cols).astype(F32)).astype(BF16)
+
+
+def update_call(place, x, k, pieces, gathered, name, after=()):
     half, width = pieces[4].shape
     blocks, _, groups, r, depth = x[0].shape
-    plane, _, n_rows, _ = other.shape
+    parts, n_rows, _ = gathered.shape
     return call(
         update_kernel,
         place,
         (width // CB,),
         [(a, (blocks, None, groups, r, depth), lambda j, s: (0, k, 0, 0, 0)) for a in x]
         + [col(a) for a in pieces]
-        + [
-            (own, (plane, 1, n_rows, CB), lambda j, s: (0, which, 0, j)),
-            (other, (plane, 1, n_rows, CB), lambda j, s: (0, which, 0, j)),
-        ],
+        + [(gathered, (parts, n_rows, CB), lambda j, s: (0, 0, j))],
         [col(sds((depth, width), BF16))],
         [pltpu.VMEM((depth, 8 * half), BF16)],
-        32,
+        50,
         (16 * half * depth * width, 16 * half * (depth + width) + 4 * depth * width),
         name,
         after,
@@ -446,40 +452,48 @@
     base = (wide * x_stash.shape[0]).astype(jnp.int32)
     place = jnp.concatenate([where, offsets.reshape(2), base[None]])
 
-    x, (own, over) = wide_gather(
+    x, (to_up, to_down), joined = wide_gather(
         pick(place, token_ids, x_stash, grad_out),
         lambda pair: relay(place, acc_up, acc_down, width, parts, (pair,)),
     )
     half = half_rows(x)
 
     far, far_done = far_sum(place, x, w_up, w_down, ())
+    up_blocks = exchange(hold(to_up, (joined,)))
     near_h, done = near_sum(place, x, 0, w_up, far, "hidden", (far_done,))
     near_b, done = near_sum(place, x, 1, w_down, far, "back", (done,))
-    over = lax.ppermute(hold(over, (far_done,)), WIDE, Z_SWAP)
-    own_blocks = lax.all_to_all(hold(own, (far_done,)), WIDE, 0, 0, tiled=True, axis_index_groups=PLANES)
+
     keep, other, done = own_sum(place, x, 0, w_up, near_h, "hidden", (done,))
     gelu_value, slope = gelu_parts(keep + other.astype(F32))
     mine = gelu_value.astype(BF16)
     act_other = lax.ppermute(mine, NARROW, ZHI_SWAP)
-    keep, other, done = own_sum(place, x, 1, w_down, near_b, "back", (act_other,))
-    held = hold(over, (done,))
-    other_blocks = lax.all_to_all(held, WIDE, 0, 0, tiled=True, axis_index_groups=PLANES)
-    act, act_far = narrow_gather(mine, act_other, "act", (done, own_blocks))
+    keep, other, done = own_sum(place, x, 1, w_down, near_b, "back", (act_other, up_blocks))
+    act, act_far = narrow_gather(mine, act_other, "act", (done,))
     hidden_grad = ((keep + other.astype(F32)) * slope).astype(BF16)
-    grad, grad_far = narrow_gather(hidden_grad, lax.ppermute(hidden_grad, NARROW, ZHI_SWAP), "grad", (act_far[0], act_far[1]))
-    k0, g0 = rows_call(place, act + act_far, half, w_down, "out_rows", (grad[0],))
-    k1, g1 = rows_call(place, grad + grad_far, half, w_up, "grad_rows", (g0, other_blocks))
+    grad_other = lax.ppermute(hidden_grad, NARROW, ZHI_SWAP)
+    to_down = hold(to_down, (grad_other,))
+    down_blocks = exchange(to_down)
+    grad, _ = narrow_gather(hidden_grad, grad_other, "grad", (act_far[0], act_far[1], to_down), False)
+    kept, given = rows_call(place, act + act_far, half, w_down, "out_rows", (grad[0],))
+    near_done = (grad[1], grad[2])
+    grad_far = far_gather(grad, (given, *near_done))
+    given = hold(given, near_done)
     results = {}
 
     def grad_first(own_out):
-        results["grad"] = wide_sum(place, k1, g1, "grad", lambda own: ())
-        return (results["grad"][1],)
-
-    out_y, _, out_sent = wide_sum(place, k0, g0, "out", grad_first)
-    grad_in, own, sent = results["grad"]
-    after = (own, out_sent)
-    new_up = update_call(place, x, 0, grad + grad_far, own_blocks, 0, other_blocks, "up_update", after)
-    new_down = update_call(place, x, 1, act + act_far, own_blocks, 1, other_blocks, "down_update", (new_up, sent))
+        results["rows"] = rows_call(place, grad + grad_far, half, w_up, "grad_rows", (own_out,))
+        return (results["rows"][1], down_blocks)
+
+    out_y, _, out_sent = wide_sum(place, kept, given, "out", grad_first)
+    kept, given = results["rows"]
+
+    def up_first(own):
+        results["up"] = update_call(place, x, 0, grad + grad_far, up_blocks, "up_update", (own,))
+        return (results["up"],)
+
+    grad_in, _, sent = wide_sum(place, kept, hold(given, (out_sent,)), "grad", up_first)
+    new_up = results["up"]
+    new_down = update_call(place, x, 1, act + act_far, down_blocks, "down_update", (sent,))
     return (out_y, grad_in, new_up, new_down)
 
 

time: 321 us -> 315 us (0.981)
  waiting for transfers between devices: 158 us -> 116 us
  Pallas kernels: 72.2 us -> 90.4 us
  local copies, waits for them, and re-layouts: 30.4 us -> 41 us
  starting transfers between devices: 56.9 us -> 63.3 us
    ppermute x2, waiting for transfers between devices: 35.6 us -> 14.3 us  [own_sum(): return (keep, lax.ppermute(send, NARROW, ZHI_SWAP), send)]
    ppermute x1, waiting for transfers between devices: 16.8 us -> 4.41 us  [far_sum(): lax.ppermute(b, NARROW, Y_LEFT)]
    pallas_call x9, Pallas kernels: 58.4 us -> 70.5 us  [call(): pl.pallas_call(run, out_shape=[shape for shape, _, _ in outs], grid_spec=...]
    ppermute x3, waiting for transfers between devices: 9.47 us -> 20.8 us  [wide_gather(): lax.ppermute(pair, WIDE, X_SHIFT[(4 - d) % 4])]
    ppermute x2, waiting for transfers between devices: 32.6 us -> 21.4 us  [narrow_gather(): lax.ppermute(own, NARROW, Y_RIGHT)]
    ppermute x1, waiting for transfers between devices: 13.1 us -> 3.52 us  [body(): act_other = lax.ppermute(mine, NARROW, ZHI_SWAP)]
    ppermute x6 -> x5, waiting for transfers between devices: 10.4 us -> 2.14 us  [the longest x2 1.13 us: far_gather(): lax.ppermute(near[0], NARROW, Y_RIGHT)]
    unnamed x100 -> x98, local copies, waits for them, and re-layouts: 29.5 us -> 37.6 us
  transfers between devices with their start and end apart: 36 -> 35, of which waited for: 15 -> 20; matrix products, arithmetic and copies ran while one was open for 0% -> 1% of each run, Pallas kernels for 20% -> 23%
where the time goes in v2:
time: 315 us; the launch traced here: 313 us
  waiting for transfers between devices  116 us (37%)
  Pallas kernels  90.4 us (29%)
  starting transfers between devices  63.3 us (20%)
  local copies, waits for them, and re-layouts  41 us (13%)
    pallas_call x9, Pallas kernels, call(): pl.pallas_call(run, out_shape=[shape for shape, _, _ in outs], grid_spec=...  70.5 us
    unnamed x98, local copies, waits for them, and re-layouts  37.6 us
    ppermute x2, waiting for transfers between devices, near_sum(): lax.ppermute(left, NARROW, Y_LEFT)  22 us
    ppermute x2, waiting for transfers between devices, narrow_gather(): lax.ppermute(own, NARROW, Y_RIGHT)  21.4 us
    ppermute x3, waiting for transfers between devices, wide_gather(): lax.ppermute(pair, WIDE, X_SHIFT[(4 - d) % 4])  20.8 us
    ppermute x2, waiting for transfers between devices, own_sum(): return (keep, lax.ppermute(send, NARROW, ZHI_SWAP), send)  14.3 us
    ppermute x6, starting transfers between devices, wide_sum(): lax.ppermute(block, WIDE, X_SHIFT[d])  13 us
    all_to_all x2, starting transfers between devices, exchange(): return lax.all_to_all(blocks, WIDE, 0, 0, tiled=True)  11.7 us
  transfers between devices with their start and end apart: 35, of which 20 were waited for; matrix products, arithmetic and copies ran while one was open for 1% of the time, Pallas kernels for 23%

profile of v2, /device:TPU:0, one launch (start us, length us, event | category | flops | bytes accessed | tf_op | source)
XLA Modules:
  0.0 313.3 jit_solution(13684782120418707608)
XLA Ops:
  6.7 6.3 %collective-permute-done = bf16[128,1024]{1,0:T(8,128)(2,1)S(1)} collective-permute-done((bf16[128,1024]{1,0:T(8,128)(2,1)S(1)}, bf16[128,1024]{1,0:T(8,128)(2,1)S(1)}, u32[]{:S(2)}, u32[]{:S(2)}) %collective-permute-start) | collective-permute-done | bytes 262176 | tf_op jit(solution)/shard_map/ppermute | solution.py:400
  18.8 9.6 %collective-permute-done.3.refs_3_ = bf16[2,128,1024]{2,1,0:T(8,128)(2,1)S(1)} collective-permute-done((bf16[2,128,1024]{2,1,0:T(8,128)(2,1)S(1)}, bf16[2,128,1024]{2,1,0:T(8,128)(2,1)S(1)}, u32[]{:S(2)}, u32[]{:S(2)}) %collective-permute-start.3) | collective-permute-done | bytes 524320 | tf_op jit(solution)/shard_map/ppermute | solution.py:402
  28.4 11.1 %collective-permute-done.2.refs_2_ = bf16[2,128,1024]{2,1,0:T(8,128)(2,1)S(1)} collective-permute-done((bf16[2,128,1024]{2,1,0:T(8,128)(2,1)S(1)}, bf16[2,128,1024]{2,1,0:T(8,128)(2,1)S(1)}, u32[]{:S(2)}, u32[]{:S(2)}) %collective-permute-start.2) | collective-permute-done | bytes 524320 | tf_op jit(solution)/shard_map/ppermute | solution.py:402
  41.0 4.4 %collective-permute-done.4 = bf16[8,128,1024]{2,1,0:T(8,128)(2,1)S(1)} collective-permute-done((bf16[8,128,1024]{2,1,0:T(8,128)(2,1)}, bf16[8,128,1024]{2,1,0:T(8,128)(2,1)S(1)}, u32[]{:S(2)}, u32[]{:S(2)}) %collective-permute-start.4) | collective-permute-done | bytes 2097184 | tf_op jit(solution)/shard_map/ppermute | solution.py:404
  49.8 5.9 %far.1 = (bf16[2,128,1920]{2,1,0:T(8,128)(2,1)}, bf16[2,128,1920]{2,1,0:T(8,128)(2,1)}) custom-call(s32[6]{0:T(128)S(1)} %concatenate.3.refs_0_.s_ref, bf16[8,2,4,16,1024]{4,3,2,1,0:T(8,128)(2,1)S(1)} %bitcast.11, bf16[8,2,4,16,1024]{4,3,2,1,0:T(8,128)(2,1)S(1)} %bitcast.19, bf16[8,2,4,16,1024]{4,3,2,1,0:T(8,128)(2,1)S(1)} %bitcast.12, ...), custom_call_target="tpu_custom_call" | custom-call | flops 2013265920 | bytes 5898240 | tf_op jit(solution)/shard_map/far/pallas_call | solution.py:53
  55.7 3.0 collective-permute-start.6
  58.8 8.1 %relay.1 = (bf16[16,64,1920]{2,1,0:T(8,128)(2,1)S(1)}, bf16[16,64,1920]{2,1,0:T(8,128)(2,1)S(1)}) custom-call(s32[6]{0:T(128)S(1)} %concatenate.3.refs_0_.s_ref, bf16[1,1,1966592]{2,1,0:T(2,128)(2,1)S(1)} %copy-done.16, bf16[1,1,1966592]{2,1,0:T(2,128)(2,1)} %down_ref.1, bf16[2,128,1024]{2,1,0:T(8,128)(2,1)S(1)} %pad_maximum_fusion.refs_0_), custom_call_target="tpu_custom_call" | custom-call | bytes 32000000 | tf_op jit(solution)/shard_map/relay/pallas_call | solution.py:185
  70.8 5.2 %all-to-all-start = ((bf16[16,64,1920]{2,1,0:T(8,128)(2,1)}), bf16[16,64,1920]{2,1,0:T(8,128)(2,1)}, u32[]{:S(2)}, u32[]{:S(2)}) async-start(bf16[16,64,1920]{2,1,0:T(8,128)(2,1)} %hold.6), calls=%async_computation | async-start | bytes 7864320 | tf_op jit(solution)/shard_map/all_to_all | solution.py:304
  76.0 4.4 %collective-permute-done.6.refs_6_ = bf16[2,128,1920]{2,1,0:T(8,128)(2,1)S(1)} collective-permute-done((bf16[2,128,1920]{2,1,0:T(8,128)(2,1)}, bf16[2,128,1920]{2,1,0:T(8,128)(2,1)S(1)}, u32[]{:S(2)}, u32[]{:S(2)}) %collective-permute-start.6) | collective-permute-done | bytes 983072 | tf_op jit(solution)/shard_map/ppermute | solution.py:269
  80.4 3.4 %collective-permute-done.5.refs_5_ = bf16[2,128,1920]{2,1,0:T(8,128)(2,1)} collective-permute-done((bf16[2,128,1920]{2,1,0:T(8,128)(2,1)}, bf16[2,128,1920]{2,1,0:T(8,128)(2,1)}, u32[]{:S(2)}, u32[]{:S(2)}) %collective-permute-start.5) | collective-permute-done | bytes 983072 | tf_op jit(solution)/shard_map/ppermute | solution.py:269
  87.5 6.1 %hidden_near.1 = (bf16[256,1920]{1,0:T(8,128)(2,1)S(1)}, bf16[256,1920]{1,0:T(8,128)(2,1)S(1)}) custom-call(s32[6]{0:T(128)S(1)} %concatenate.3.refs_0_.s_ref, bf16[8,2,4,16,1024]{4,3,2,1,0:T(8,128)(2,1)S(1)} %bitcast.13, bf16[8,2,4,16,1024]{4,3,2,1,0:T(8,128)(2,1)S(1)} %bitcast.23, bf16[8,2,4,16,1024]{4,3,2,1,0:T(8,128)(2,1)S(1)} %bitcast.14, ...), custom_call_target="tpu_custom_call" | custom-call | flops 2013265920 | bytes 5898240 | tf_op jit(solution)/shard_map/hidden_near/pallas_call | solution.py:53
  95.7 6.4 %back_near.1 = (bf16[256,1920]{1,0:T(8,128)(2,1)}, bf16[256,1920]{1,0:T(8,128)(2,1)}) custom-call(s32[6]{0:T(128)S(1)} %concatenate.3.refs_0_.s_ref, bf16[8,2,4,16,1024]{4,3,2,1,0:T(8,128)(2,1)S(1)} %bitcast.15, bf16[8,2,4,16,1024]{4,3,2,1,0:T(8,128)(2,1)S(1)} %bitcast.25, bf16[8,2,4,16,1024]{4,3,2,1,0:T(8,128)(2,1)S(1)} %bitcast.16, ...), custom_call_target="tpu_custom_call" | custom-call | flops 2013265920 | bytes 5898240 | tf_op jit(solution)/shard_map/back_near/pallas_call | solution.py:53
  102.0 14.3 %collective-permute-done.8.refs_4_ = bf16[256,1920]{1,0:T(8,128)(2,1)S(1)} collective-permute-done((bf16[256,1920]{1,0:T(8,128)(2,1)S(1)}, bf16[256,1920]{1,0:T(8,128)(2,1)S(1)}, u32[]{:S(2)}, u32[]{:S(2)}) %collective-permute-start.8) | collective-permute-done | bytes 983072 | tf_op jit(solution)/shard_map/ppermute | solution.py:277
  117.7 3.7 %hidden_own.1 = (f32[128,1920]{1,0:T(8,128)S(1)}, bf16[128,1920]{1,0:T(8,128)(2,1)S(1)}) custom-call(s32[6]{0:T(128)S(1)} %concatenate.3.refs_0_.s_ref, bf16[8,2,4,16,1024]{4,3,2,1,0:T(8,128)(2,1)S(1)} %bitcast.17, bf16[8,2,4,16,1024]{4,3,2,1,0:T(8,128)(2,1)S(1)} %bitcast.27, bf16[1024,1920]{1,0:T(8,128)(2,1)S(1)} %copy-done.11, ...), custom_call_target="tpu_custom_call" | custom-call | flops 1006632960 | bytes 4915200 | tf_op jit(solution)/shard_map/hidden_own/pallas_call | solution.py:53
  121.4 3.6 %collective-permute-start.9 = (bf16[128,1920]{1,0:T(8,128)(2,1)S(1)}, bf16[128,1920]{1,0:T(8,128)(2,1)S(1)}, u32[]{:S(2)}, u32[]{:S(2)}) collective-permute-start(bf16[128,1920]{1,0:T(8,128)(2,1)S(1)} %get-tuple-element.38), channel_id=1, source_target_pairs={{0,1},{1,0},{2,3},{3,2},{4,5},{5,4},{6,7},{7,6},{8,9},{9,8},{10,11... | collective-permute-start | bytes 1474568 | tf_op jit(solution)/shard_map/ppermute | solution.py:284
  128.3 7.7 %collective-permute-done.9 = bf16[128,1920]{1,0:T(8,128)(2,1)S(1)} collective-permute-done((bf16[128,1920]{1,0:T(8,128)(2,1)S(1)}, bf16[128,1920]{1,0:T(8,128)(2,1)S(1)}, u32[]{:S(2)}, u32[]{:S(2)}) %collective-permute-start.9) | collective-permute-done | bytes 491552 | tf_op jit(solution)/shard_map/ppermute | solution.py:284
  139.7 7.7 %collective-permute-done.12.refs_4_ = bf16[256,1920]{1,0:T(8,128)(2,1)} collective-permute-done((bf16[256,1920]{1,0:T(8,128)(2,1)}, bf16[256,1920]{1,0:T(8,128)(2,1)}, u32[]{:S(2)}, u32[]{:S(2)}) %collective-permute-start.12) | collective-permute-done | bytes 983072 | tf_op jit(solution)/shard_map/ppermute | solution.py:277
  148.1 3.5 %collective-permute-done.10.refs_5_.refs_1_ = bf16[128,1920]{1,0:T(8,128)(2,1)} collective-permute-done((bf16[128,1920]{1,0:T(8,128)(2,1)}, bf16[128,1920]{1,0:T(8,128)(2,1)}, u32[]{:S(2)}, u32[]{:S(2)}) %collective-permute-start.10) | collective-permute-done | bytes 491552 | tf_op jit(solution)/shard_map/ppermute | solution.py:469
  155.4 5.4 %back_own.1 = (f32[128,1920]{1,0:T(8,128)S(1)}, bf16[128,1920]{1,0:T(8,128)(2,1)S(1)}) custom-call(s32[6]{0:T(128)S(1)} %concatenate.3.refs_0_.s_ref, bf16[8,2,4,16,1024]{4,3,2,1,0:T(8,128)(2,1)S(1)} %bitcast.18, bf16[8,2,4,16,1024]{4,3,2,1,0:T(8,128)(2,1)S(1)} %bitcast.28, bf16[1024,1920]{1,0:T(8,128)(2,1)S(1)} %copy-done.7, ...), custom_call_target="tpu_custom_call" | custom-call | flops 1006632960 | bytes 4915200 | tf_op jit(solution)/shard_map/back_own/pallas_call | solution.py:53
  163.3 3.6 %collective-permute-start.13 = (bf16[256,1920]{1,0:T(8,128)(2,1)S(1)}, bf16[256,1920]{1,0:T(8,128)(2,1)S(1)}, u32[]{:S(2)}, u32[]{:S(2)}) collective-permute-start(bf16[256,1920]{1,0:T(8,128)(2,1)S(1)} %join_act.1.refs_0_.refs_2_), channel_id=1, source_target_pairs={{0,6},{1,7},{2,0},{3,1},{4,2},{5,3},{6,4},{7,5},{8,14},{9,15},{10,... | collective-permute-start | bytes 2949128 | tf_op jit(solution)/shard_map/ppermute | solution.py:298
  166.9 6.6 %collective-permute-done.17 = bf16[128,1920]{1,0:T(8,128)(2,1)S(1)} collective-permute-done((bf16[128,1920]{1,0:T(8,128)(2,1)S(1)}, bf16[128,1920]{1,0:T(8,128)(2,1)S(1)}, u32[]{:S(2)}, u32[]{:S(2)}) %collective-permute-start.17) | collective-permute-done | bytes 491552 | tf_op jit(solution)/shard_map/ppermute | solution.py:284
  174.5 13.4 %collective-permute-done.14.refs_2_.refs_4_ = bf16[256,1920]{1,0:T(8,128)(2,1)S(1)} collective-permute-done((bf16[256,1920]{1,0:T(8,128)(2,1)S(1)}, bf16[256,1920]{1,0:T(8,128)(2,1)S(1)}, u32[]{:S(2)}, u32[]{:S(2)}) %collective-permute-start.14) | collective-permute-done | bytes 983072 | tf_op jit(solution)/shard_map/ppermute | solution.py:298
  193.2 6.5 %all-to-all-start.1 = ((bf16[16,64,1920]{2,1,0:T(8,128)(2,1)}), bf16[16,64,1920]{2,1,0:T(8,128)(2,1)}, u32[]{:S(2)}, u32[]{:S(2)}) async-start(bf16[16,64,1920]{2,1,0:T(8,128)(2,1)} %hold.7.refs_4_), calls=%async_computation.1 | async-start | bytes 7864320 | tf_op jit(solution)/shard_map/all_to_all | solution.py:304
  203.8 3.3 %collective-permute-start.19 = (bf16[256,1920]{1,0:T(8,128)(2,1)S(1)}, bf16[256,1920]{1,0:T(8,128)(2,1)S(1)}, u32[]{:S(2)}, u32[]{:S(2)}) collective-permute-start(bf16[256,1920]{1,0:T(8,128)(2,1)S(1)} %join_grad.1.refs_6_.refs_0_.refs_2_), channel_id=1, source_target_pairs={{0,6},{1,7},{2,0},{3,1},{4,2},{5,3},{6,4},{7,5},{8,14},{9,15},{10,... | collective-permute-start | bytes 2949128 | tf_op jit(solution)/shard_map/ppermute | solution.py:298
  208.1 10.9 %out_rows.1 = (f32[4,128,1024]{2,1,0:T(8,128)}, f32[4,128,1024]{2,1,0:T(8,128)}) custom-call(s32[6]{0:T(128)S(1)} %concatenate.3.refs_0_.s_ref, bf16[256,1920]{1,0:T(8,128)(2,1)S(1)} %join_act.1.refs_0_.refs_2_, bf16[256,1920]{1,0:T(8,128)(2,1)S(1)} %copy-done.23, bf16[256,1920]{1,0:T(8,128)(2,1)S(1)} %copy-done.20, ...), custom_call_target="tpu_custom_call" | custom-call | flops 4026531840 | bytes 16252928 | tf_op jit(solution)/shard_map/out_rows/pallas_call | solution.py:53
  219.0 8.0 %collective-permute-done.20.refs_2_.refs_3_.refs_4_ = bf16[256,1920]{1,0:T(8,128)(2,1)S(1)} collective-permute-done((bf16[256,1920]{1,0:T(8,128)(2,1)S(1)}, bf16[256,1920]{1,0:T(8,128)(2,1)S(1)}, u32[]{:S(2)}, u32[]{:S(2)}) %collective-permute-start.20) | collective-permute-done | bytes 983072 | tf_op jit(solution)/shard_map/ppermute | solution.py:298
  229.3 3.2 %collective-permute-start.26 = (bf16[128,1920]{1,0:T(8,128)(2,1)}, bf16[128,1920]{1,0:T(8,128)(2,1)S(1)}, u32[]{:S(2)}, u32[]{:S(2)}) collective-permute-start(bf16[128,1920]{1,0:T(8,128)(2,1)} %hold.10), channel_id=1, source_target_pairs={{0,6},{1,7},{2,0},{3,1},{4,2},{5,3},{6,4},{7,5},{8,14},{9,15},{10,... | collective-permute-start | bytes 1474568 | tf_op jit(solution)/shard_map/ppermute | solution.py:293
  245.5 10.8 %grad_rows.1 = (f32[4,128,1024]{2,1,0:T(8,128)}, f32[4,128,1024]{2,1,0:T(8,128)}) custom-call(s32[6]{0:T(128)S(1)} %concatenate.3.refs_0_.s_ref, bf16[256,1920]{1,0:T(8,128)(2,1)S(1)} %copy-done.18, bf16[256,1920]{1,0:T(8,128)(2,1)S(1)} %copy-done.13, bf16[256,1920]{1,0:T(8,128)(2,1)} %copy-done.44, ...), custom_call_target="tpu_custom_call" | custom-call | flops 4026531840 | bytes 16252928 | tf_op jit(solution)/shard_map/grad_rows/pallas_call | solution.py:53
  258.7 5.3 %collective-permute-done.23.refs_2_ = bf16[4,32,1024]{2,1,0:T(8,128)(2,1)} collective-permute-done((bf16[4,32,1024]{2,1,0:T(8,128)(2,1)}, bf16[4,32,1024]{2,1,0:T(8,128)(2,1)}, u32[]{:S(2)}, u32[]{:S(2)}) %collective-permute-start.23) | collective-permute-done | bytes 262176 | tf_op jit(solution)/shard_map/ppermute | solution.py:391
  270.4 5.0 %collective-permute-done.27.refs_2_ = bf16[4,16,1024]{2,1,0:T(8,128)(2,1)S(1)} collective-permute-done((bf16[4,16,1024]{2,1,0:T(8,128)(2,1)}, bf16[4,16,1024]{2,1,0:T(8,128)(2,1)S(1)}, u32[]{:S(2)}, u32[]{:S(2)}) %collective-permute-start.27) | collective-permute-done | bytes 131104 | tf_op jit(solution)/shard_map/ppermute | solution.py:394
  289.0 10.8 %up_update.1.refs_4_ = bf16[1024,1920]{1,0:T(8,128)(2,1)} custom-call(s32[6]{0:T(128)S(1)} %concatenate.3.refs_0_.s_ref, bf16[8,2,4,16,1024]{4,3,2,1,0:T(8,128)(2,1)} %bitcast.9, bf16[8,2,4,16,1024]{4,3,2,1,0:T(8,128)(2,1)} %bitcast.21, bf16[256,1920]{1,0:T(8,128)(2,1)S(1)} %copy-done.18, bf16[256,1920]{1,0:T(8,128)(2,1)S(1)} %copy-done.13, ...), custom_call_target="tpu_custom_call" | custom-call | flops 4026531840 | bytes 13893632 | tf_op jit(solution)/shard_map/up_update/pallas_call | solution.py:53
  301.4 10.7 %down_update.1 = bf16[1024,1920]{1,0:T(8,128)(2,1)} custom-call(s32[6]{0:T(128)S(1)} %concatenate.3.refs_0_.s_ref, bf16[8,2,4,16,1024]{4,3,2,1,0:T(8,128)(2,1)} %bitcast.10, bf16[8,2,4,16,1024]{4,3,2,1,0:T(8,128)(2,1)} %bitcast.22, bf16[256,1920]{1,0:T(8,128)(2,1)S(1)} %join_act.1.refs_0_.refs_2_, bf16[256,1920]{1,0:T(8,128)(2,1)S(1)} %copy-done.24, ...), custom_call_target="tpu_custom_call" | custom-call | flops 4026531840 | bytes 13893632 | tf_op jit(solution)/shard_map/down_update/pallas_call | solution.py:53
  (170 shorter events, 94.5 us)
Async XLA Ops:
  4.6 8.4 %collective-permute-start = (bf16[128,1024]{1,0:T(8,128)(2,1)S(1)}, bf16[128,1024]{1,0:T(8,128)(2,1)S(1)}, u32[]{:S(2)}, u32[]{:S(2)}) collective-permute-start(bf16[128,1024]{1,0:T(8,128)(2,1)S(1)} %pick.1), channel_id=1, source_target_pairs={{0,64},{8,72},{16,80},{24,88},{32,96},{40,104},{48,112},{56,120},{... | collective-permute-start | bytes 786440 | tf_op jit(solution)/shard_map/ppermute | solution.py:400
  13.1 15.3 %collective-permute-start.3 = (bf16[2,128,1024]{2,1,0:T(8,128)(2,1)S(1)}, bf16[2,128,1024]{2,1,0:T(8,128)(2,1)S(1)}, u32[]{:S(2)}, u32[]{:S(2)}) collective-permute-start(bf16[2,128,1024]{2,1,0:T(8,128)(2,1)S(1)} %pad_maximum_fusion.refs_0_), channel_id=1, source_target_pairs={{0,16},{8,24},{16,32},{24,40},{32,48},{40,56},{48,0},{56,8},{64,80... | collective-permute-start | bytes 1572872 | tf_op jit(solution)/shard_map/ppermute | solution.py:402
  14.6 24.9 %collective-permute-start.2 = (bf16[2,128,1024]{2,1,0:T(8,128)(2,1)S(1)}, bf16[2,128,1024]{2,1,0:T(8,128)(2,1)S(1)}, u32[]{:S(2)}, u32[]{:S(2)}) collective-permute-start(bf16[2,128,1024]{2,1,0:T(8,128)(2,1)S(1)} %pad_maximum_fusion.refs_0_), channel_id=1, source_target_pairs={{0,32},{8,40},{16,48},{24,56},{32,0},{40,8},{48,16},{56,24},{64,96... | collective-permute-start | bytes 1572872 | tf_op jit(solution)/shard_map/ppermute | solution.py:402
  17.4 22.2 %collective-permute-start.1 = (bf16[2,128,1024]{2,1,0:T(8,128)(2,1)S(1)}, bf16[2,128,1024]{2,1,0:T(8,128)(2,1)S(1)}, u32[]{:S(2)}, u32[]{:S(2)}) collective-permute-start(bf16[2,128,1024]{2,1,0:T(8,128)(2,1)S(1)} %pad_maximum_fusion.refs_0_), channel_id=1, source_target_pairs={{0,48},{8,56},{16,0},{24,8},{32,16},{40,24},{48,32},{56,40},{64,11... | collective-permute-start | bytes 1572872 | tf_op jit(solution)/shard_map/ppermute | solution.py:402
  55.7 24.6 %collective-permute-start.6 = (bf16[2,128,1920]{2,1,0:T(8,128)(2,1)}, bf16[2,128,1920]{2,1,0:T(8,128)(2,1)S(1)}, u32[]{:S(2)}, u32[]{:S(2)}) collective-permute-start(bf16[2,128,1920]{2,1,0:T(8,128)(2,1)} %get-tuple-element.33), channel_id=1, source_target_pairs={{0,6},{1,7},{2,0},{3,1},{4,2},{5,3},{6,4},{7,5},{8,14},{9,15},{10,... | collective-permute-start | bytes 2949128 | tf_op jit(solution)/shard_map/ppermute | solution.py:269
  58.7 25.0 %collective-permute-start.5 = (bf16[2,128,1920]{2,1,0:T(8,128)(2,1)}, bf16[2,128,1920]{2,1,0:T(8,128)(2,1)}, u32[]{:S(2)}, u32[]{:S(2)}) collective-permute-start(bf16[2,128,1920]{2,1,0:T(8,128)(2,1)} %get-tuple-element.32.refs_7_), channel_id=1, source_target_pairs={{0,2},{1,3},{2,4},{3,5},{4,6},{5,7},{6,0},{7,1},{8,10},{9,11},{10,... | collective-permute-start | bytes 2949128 | tf_op jit(solution)/shard_map/ppermute | solution.py:269
  70.8 68.9 %all-to-all-start = ((bf16[16,64,1920]{2,1,0:T(8,128)(2,1)}), bf16[16,64,1920]{2,1,0:T(8,128)(2,1)}, u32[]{:S(2)}, u32[]{:S(2)}) async-start(bf16[16,64,1920]{2,1,0:T(8,128)(2,1)} %hold.6), calls=%async_computation | async-start | bytes 7864320 | tf_op jit(solution)/shard_map/all_to_all | solution.py:304
  93.6 22.7 %collective-permute-start.8 = (bf16[256,1920]{1,0:T(8,128)(2,1)S(1)}, bf16[256,1920]{1,0:T(8,128)(2,1)S(1)}, u32[]{:S(2)}, u32[]{:S(2)}) collective-permute-start(bf16[256,1920]{1,0:T(8,128)(2,1)S(1)} %get-tuple-element.35), channel_id=1, source_target_pairs={{0,6},{1,7},{2,0},{3,1},{4,2},{5,3},{6,4},{7,5},{8,14},{9,15},{10,... | collective-permute-start | bytes 2949128 | tf_op jit(solution)/shard_map/ppermute | solution.py:277
  93.8 23.9 %collective-permute-start.7 = (bf16[256,1920]{1,0:T(8,128)(2,1)S(1)}, bf16[256,1920]{1,0:T(8,128)(2,1)S(1)}, u32[]{:S(2)}, u32[]{:S(2)}) collective-permute-start(bf16[256,1920]{1,0:T(8,128)(2,1)S(1)} %get-tuple-element.34.refs_7_), channel_id=1, source_target_pairs={{0,2},{1,3},{2,4},{3,5},{4,6},{5,7},{6,0},{7,1},{8,10},{9,11},{10,... | collective-permute-start | bytes 2949128 | tf_op jit(solution)/shard_map/ppermute | solution.py:277
  121.4 14.5 %collective-permute-start.9 = (bf16[128,1920]{1,0:T(8,128)(2,1)S(1)}, bf16[128,1920]{1,0:T(8,128)(2,1)S(1)}, u32[]{:S(2)}, u32[]{:S(2)}) collective-permute-start(bf16[128,1920]{1,0:T(8,128)(2,1)S(1)} %get-tuple-element.38), channel_id=1, source_target_pairs={{0,1},{1,0},{2,3},{3,2},{4,5},{5,4},{6,7},{7,6},{8,9},{9,8},{10,11... | collective-permute-start | bytes 1474568 | tf_op jit(solution)/shard_map/ppermute | solution.py:284
  125.0 23.1 %collective-permute-start.11 = (bf16[256,1920]{1,0:T(8,128)(2,1)}, bf16[256,1920]{1,0:T(8,128)(2,1)}, u32[]{:S(2)}, u32[]{:S(2)}) collective-permute-start(bf16[256,1920]{1,0:T(8,128)(2,1)} %get-tuple-element.36.refs_5_), channel_id=1, source_target_pairs={{0,2},{1,3},{2,4},{3,5},{4,6},{5,7},{6,0},{7,1},{8,10},{9,11},{10,... | collective-permute-start | bytes 2949128 | tf_op jit(solution)/shard_map/ppermute | solution.py:277
  125.3 22.1 %collective-permute-start.12 = (bf16[256,1920]{1,0:T(8,128)(2,1)}, bf16[256,1920]{1,0:T(8,128)(2,1)}, u32[]{:S(2)}, u32[]{:S(2)}) collective-permute-start(bf16[256,1920]{1,0:T(8,128)(2,1)} %get-tuple-element.39), channel_id=1, source_target_pairs={{0,6},{1,7},{2,0},{3,1},{4,2},{5,3},{6,4},{7,5},{8,14},{9,15},{10,... | collective-permute-start | bytes 2949128 | tf_op jit(solution)/shard_map/ppermute | solution.py:277
  137.8 13.9 %collective-permute-start.10 = (bf16[128,1920]{1,0:T(8,128)(2,1)}, bf16[128,1920]{1,0:T(8,128)(2,1)}, u32[]{:S(2)}, u32[]{:S(2)}) collective-permute-start(bf16[128,1920]{1,0:T(8,128)(2,1)} %multiply_convert_fusion.refs_0_), channel_id=1, source_target_pairs={{0,1},{1,0},{2,3},{3,2},{4,5},{5,4},{6,7},{7,6},{8,9},{9,8},{10,11... | collective-permute-start | bytes 1474568 | tf_op jit(solution)/shard_map/ppermute | solution.py:469
  160.7 12.7 %collective-permute-start.17 = (bf16[128,1920]{1,0:T(8,128)(2,1)S(1)}, bf16[128,1920]{1,0:T(8,128)(2,1)S(1)}, u32[]{:S(2)}, u32[]{:S(2)}) collective-permute-start(bf16[128,1920]{1,0:T(8,128)(2,1)S(1)} %get-tuple-element.41.refs_2_), channel_id=1, source_target_pairs={{0,1},{1,0},{2,3},{3,2},{4,5},{5,4},{6,7},{7,6},{8,9},{9,8},{10,11... | collective-permute-start | bytes 1474568 | tf_op jit(solution)/shard_map/ppermute | solution.py:284
  162.4 25.5 %collective-permute-start.14 = (bf16[256,1920]{1,0:T(8,128)(2,1)S(1)}, bf16[256,1920]{1,0:T(8,128)(2,1)S(1)}, u32[]{:S(2)}, u32[]{:S(2)}) collective-permute-start(bf16[256,1920]{1,0:T(8,128)(2,1)S(1)} %join_act.1.refs_0_.refs_2_), channel_id=1, source_target_pairs={{0,2},{1,3},{2,4},{3,5},{4,6},{5,7},{6,0},{7,1},{8,10},{9,11},{10,... | collective-permute-start | bytes 2949128 | tf_op jit(solution)/shard_map/ppermute | solution.py:298
  163.3 24.7 %collective-permute-start.13 = (bf16[256,1920]{1,0:T(8,128)(2,1)S(1)}, bf16[256,1920]{1,0:T(8,128)(2,1)S(1)}, u32[]{:S(2)}, u32[]{:S(2)}) collective-permute-start(bf16[256,1920]{1,0:T(8,128)(2,1)S(1)} %join_act.1.refs_0_.refs_2_), channel_id=1, source_target_pairs={{0,6},{1,7},{2,0},{3,1},{4,2},{5,3},{6,4},{7,5},{8,14},{9,15},{10,... | collective-permute-start | bytes 2949128 | tf_op jit(solution)/shard_map/ppermute | solution.py:298
  174.0 18.4 %collective-permute-start.18 = (bf16[128,1920]{1,0:T(8,128)(2,1)S(1)}, bf16[128,1920]{1,0:T(8,128)(2,1)S(1)}, u32[]{:S(2)}, u32[]{:S(2)}) collective-permute-start(bf16[128,1920]{1,0:T(8,128)(2,1)S(1)} %fusion.5.refs_0_), channel_id=1, source_target_pairs={{0,1},{1,0},{2,3},{3,2},{4,5},{5,4},{6,7},{7,6},{8,9},{9,8},{10,11... | collective-permute-start | bytes 1474568 | tf_op jit(solution)/shard_map/ppermute | solution.py:473
  187.9 13.0 %collective-permute-start.15 = (bf16[128,1920]{1,0:T(8,128)(2,1)S(1)}, bf16[128,1920]{1,0:T(8,128)(2,1)S(1)}, u32[]{:S(2)}, u32[]{:S(2)}) collective-permute-start(bf16[128,1920]{1,0:T(8,128)(2,1)S(1)} %slice.16), channel_id=1, source_target_pairs={{0,2},{1,3},{2,4},{3,5},{4,6},{5,7},{6,0},{7,1},{8,10},{9,11},{10,... | collective-permute-start | bytes 1474568 | tf_op jit(solution)/shard_map/ppermute | solution.py:293
  190.0 11.9 %collective-permute-start.16 = (bf16[128,1920]{1,0:T(8,128)(2,1)}, bf16[128,1920]{1,0:T(8,128)(2,1)S(1)}, u32[]{:S(2)}, u32[]{:S(2)}) collective-permute-start(bf16[128,1920]{1,0:T(8,128)(2,1)} %slice.17), channel_id=1, source_target_pairs={{0,6},{1,7},{2,0},{3,1},{4,2},{5,3},{6,4},{7,5},{8,14},{9,15},{10,... | collective-permute-start | bytes 1474568 | tf_op jit(solution)/shard_map/ppermute | solution.py:293
  193.2 65.5 %all-to-all-start.1 = ((bf16[16,64,1920]{2,1,0:T(8,128)(2,1)}), bf16[16,64,1920]{2,1,0:T(8,128)(2,1)}, u32[]{:S(2)}, u32[]{:S(2)}) async-start(bf16[16,64,1920]{2,1,0:T(8,128)(2,1)} %hold.7.refs_4_), calls=%async_computation.1 | async-start | bytes 7864320 | tf_op jit(solution)/shard_map/all_to_all | solution.py:304
  203.7 23.3 %collective-permute-start.20 = (bf16[256,1920]{1,0:T(8,128)(2,1)S(1)}, bf16[256,1920]{1,0:T(8,128)(2,1)S(1)}, u32[]{:S(2)}, u32[]{:S(2)}) collective-permute-start(bf16[256,1920]{1,0:T(8,128)(2,1)S(1)} %join_grad.1.refs_6_.refs_0_.refs_2_), channel_id=1, source_target_pairs={{0,2},{1,3},{2,4},{3,5},{4,6},{5,7},{6,0},{7,1},{8,10},{9,11},{10,... | collective-permute-start | bytes 2949128 | tf_op jit(solution)/shard_map/ppermute | solution.py:298
  203.8 24.1 %collective-permute-start.19 = (bf16[256,1920]{1,0:T(8,128)(2,1)S(1)}, bf16[256,1920]{1,0:T(8,128)(2,1)S(1)}, u32[]{:S(2)}, u32[]{:S(2)}) collective-permute-start(bf16[256,1920]{1,0:T(8,128)(2,1)S(1)} %join_grad.1.refs_6_.refs_0_.refs_2_), channel_id=1, source_target_pairs={{0,6},{1,7},{2,0},{3,1},{4,2},{5,3},{6,4},{7,5},{8,14},{9,15},{10,... | collective-permute-start | bytes 2949128 | tf_op jit(solution)/shard_map/ppermute | solution.py:298
  229.3 16.2 %collective-permute-start.25 = (bf16[128,1920]{1,0:T(8,128)(2,1)}, bf16[128,1920]{1,0:T(8,128)(2,1)S(1)}, u32[]{:S(2)}, u32[]{:S(2)}) collective-permute-start(bf16[128,1920]{1,0:T(8,128)(2,1)} %hold.9), channel_id=1, source_target_pairs={{0,2},{1,3},{2,4},{3,5},{4,6},{5,7},{6,0},{7,1},{8,10},{9,11},{10,... | collective-permute-start | bytes 1474568 | tf_op jit(solution)/shard_map/ppermute | solution.py:293
  229.3 16.1 %collective-permute-start.26 = (bf16[128,1920]{1,0:T(8,128)(2,1)}, bf16[128,1920]{1,0:T(8,128)(2,1)S(1)}, u32[]{:S(2)}, u32[]{:S(2)}) collective-permute-start(bf16[128,1920]{1,0:T(8,128)(2,1)} %hold.10), channel_id=1, source_target_pairs={{0,6},{1,7},{2,0},{3,1},{4,2},{5,3},{6,4},{7,5},{8,14},{9,15},{10,... | collective-permute-start | bytes 1474568 | tf_op jit(solution)/shard_map/ppermute | solution.py:293
  239.1 19.6 %collective-permute-start.22 = (bf16[4,32,1024]{2,1,0:T(8,128)(2,1)}, bf16[4,32,1024]{2,1,0:T(8,128)(2,1)}, u32[]{:S(2)}, u32[]{:S(2)}) collective-permute-start(bf16[4,32,1024]{2,1,0:T(8,128)(2,1)} %get-tuple-element.47), channel_id=1, source_target_pairs={{0,16},{8,24},{16,32},{24,40},{32,48},{40,56},{48,0},{56,8},{64,80... | collective-permute-start | bytes 786440 | tf_op jit(solution)/shard_map/ppermute | solution.py:391
  240.8 23.2 %collective-permute-start.23 = (bf16[4,32,1024]{2,1,0:T(8,128)(2,1)}, bf16[4,32,1024]{2,1,0:T(8,128)(2,1)}, u32[]{:S(2)}, u32[]{:S(2)}) collective-permute-start(bf16[4,32,1024]{2,1,0:T(8,128)(2,1)} %get-tuple-element.48), channel_id=1, source_target_pairs={{0,32},{8,40},{16,48},{24,56},{32,0},{40,8},{48,16},{56,24},{64,96... | collective-permute-start | bytes 786440 | tf_op jit(solution)/shard_map/ppermute | solution.py:391
  243.5 20.5 %collective-permute-start.24 = (bf16[4,32,1024]{2,1,0:T(8,128)(2,1)}, bf16[4,32,1024]{2,1,0:T(8,128)(2,1)}, u32[]{:S(2)}, u32[]{:S(2)}) collective-permute-start(bf16[4,32,1024]{2,1,0:T(8,128)(2,1)} %get-tuple-element.49), channel_id=1, source_target_pairs={{0,48},{8,56},{16,0},{24,8},{32,16},{40,24},{48,32},{56,40},{64,11... | collective-permute-start | bytes 786440 | tf_op jit(solution)/shard_map/ppermute | solution.py:391
  269.2 8.3 %collective-permute-start.28 = (f32[4,128,1024]{2,1,0:T(8,128)}, f32[4,128,1024]{2,1,0:T(8,128)S(1)}, u32[]{:S(2)}, u32[]{:S(2)}) collective-permute-start(f32[4,128,1024]{2,1,0:T(8,128)} %hold.11), channel_id=1, source_target_pairs={{0,8},{8,0},{16,24},{24,16},{32,40},{40,32},{48,56},{56,48},{64,72... | collective-permute-start | bytes 6291464 | tf_op jit(solution)/shard_map/ppermute | solution.py:386
  282.3 17.5 %collective-permute-start.29 = (bf16[4,32,1024]{2,1,0:T(8,128)(2,1)S(1)}, bf16[4,32,1024]{2,1,0:T(8,128)(2,1)S(1)}, u32[]{:S(2)}, u32[]{:S(2)}) collective-permute-start(bf16[4,32,1024]{2,1,0:T(8,128)(2,1)S(1)} %get-tuple-element.55), channel_id=1, source_target_pairs={{0,16},{8,24},{16,32},{24,40},{32,48},{40,56},{48,0},{56,8},{64,80... | collective-permute-start | bytes 786440 | tf_op jit(solution)/shard_map/ppermute | solution.py:391
  283.6 16.2 %collective-permute-start.30 = (bf16[4,32,1024]{2,1,0:T(8,128)(2,1)S(1)}, bf16[4,32,1024]{2,1,0:T(8,128)(2,1)S(1)}, u32[]{:S(2)}, u32[]{:S(2)}) collective-permute-start(bf16[4,32,1024]{2,1,0:T(8,128)(2,1)S(1)} %get-tuple-element.56), channel_id=1, source_target_pairs={{0,32},{8,40},{16,48},{24,56},{32,0},{40,8},{48,16},{56,24},{64,96... | collective-permute-start | bytes 786440 | tf_op jit(solution)/shard_map/ppermute | solution.py:391
  286.4 13.4 %collective-permute-start.31 = (bf16[4,32,1024]{2,1,0:T(8,128)(2,1)S(1)}, bf16[4,32,1024]{2,1,0:T(8,128)(2,1)S(1)}, u32[]{:S(2)}, u32[]{:S(2)}) collective-permute-start(bf16[4,32,1024]{2,1,0:T(8,128)(2,1)S(1)} %get-tuple-element.57), channel_id=1, source_target_pairs={{0,48},{8,56},{16,0},{24,8},{32,16},{40,24},{48,32},{56,40},{64,11... | collective-permute-start | bytes 786440 | tf_op jit(solution)/shard_map/ppermute | solution.py:391
  300.0 12.2 %collective-permute-start.32 = (bf16[4,16,1024]{2,1,0:T(8,128)(2,1)S(1)}, bf16[4,16,1024]{2,1,0:T(8,128)(2,1)S(1)}, u32[]{:S(2)}, u32[]{:S(2)}) collective-permute-start(bf16[4,16,1024]{2,1,0:T(8,128)(2,1)S(1)} %get-tuple-element.59.refs_8_), channel_id=1, source_target_pairs={{0,64},{8,72},{16,80},{24,88},{32,96},{40,104},{48,112},{56,120},{... | collective-permute-start | bytes 393224 | tf_op jit(solution)/shard_map/ppermute | solution.py:394
  (52 other events, 262.3 us)

commit v3 on v2

--- a/solution.py
+++ b/solution.py
@@ -9,6 +9,8 @@
 
 SLACK = 512
 MIB = 2**20
+SMALL = 16
+WIDE_GRANT = 62
 BF16 = jnp.bfloat16
 F32 = jnp.float32
 WIDE = "wide"
@@ -89,7 +91,7 @@
     out_ref[:tokens] = rows[...].astype(BF16)
 
 
-def simple_call(kernel, ins, outs, scratch, nbytes, name, after=(), mib=50):
+def simple_call(kernel, ins, outs, scratch, nbytes, name, after=(), mib=SMALL):
     n, m = len(ins), len(after)
 
     def run(*refs):
@@ -382,18 +384,28 @@
         out_ref[pl.ds(at, r)] = (keep_ref[i] + other_ref[i].astype(F32)).astype(BF16)
 
 
-def wide_sum(place, kept, given, tag, later):
+def core_sum(kept, given, tag, after=()):
     taken = lax.ppermute(given, WIDE, CORE_SWAP)
     groups, rows, depth = kept.shape
-    b, r = rows // 4, rows // 8
+    b = rows // 4
     outs = [sds((groups, b, depth), F32)] + [sds((groups, b, depth), BF16)] * 3
-    own, *blocks = simple_call(merge_kernel, [kept, taken], outs, [], 8e6, "merge_" + tag)
-    got = [lax.ppermute(block, WIDE, X_SHIFT[d]) for d, block in zip((1, 2, 3), blocks)]
-    outs = [sds((groups, r, depth), F32), sds((groups, r, depth), BF16)]
-    keep, send = simple_call(cross_kernel, [own, *got], outs, [], 2e6, "cross_" + tag, later(own))
+    return simple_call(merge_kernel, [kept, taken], outs, [], 8e6, "merge_" + tag, after, WIDE_GRANT)
+
+
+def x_exchange(blocks):
+    return [lax.ppermute(block, WIDE, X_SHIFT[d]) for d, block in zip((1, 2, 3), blocks)]
+
+
+def x_sum(own, got, tag, after=()):
+    groups, b, depth = own.shape
+    outs = [sds((groups, b // 2, depth), F32), sds((groups, b // 2, depth), BF16)]
+    return simple_call(cross_kernel, [own, *got], outs, [], 2e6, "cross_" + tag, after, WIDE_GRANT)
+
+
+def z_sum(place, keep, send, tag, after=()):
     other = lax.ppermute(send, WIDE, Z_SWAP)
-    outs = [sds((groups * r, depth), BF16)]
-    return simple_call(finish_kernel, [place, keep, other], outs, [], 1e6, "finish_" + tag)[0], own, send
+    outs = [sds((keep.shape[0] * keep.shape[1], keep.shape[2]), BF16)]
+    return simple_call(finish_kernel, [place, keep, other], outs, [], 1e6, "finish_" + tag, after, WIDE_GRANT)[0]
 
 
 def wide_gather(rows, work):
@@ -477,23 +489,17 @@
     kept, given = rows_call(place, act + act_far, half, w_down, "out_rows", (grad[0],))
     near_done = (grad[1], grad[2])
     grad_far = far_gather(grad, (given, *near_done))
-    given = hold(given, near_done)
-    results = {}
-
-    def grad_first(own_out):
-        results["rows"] = rows_call(place, grad + grad_far, half, w_up, "grad_rows", (own_out,))
-        return (results["rows"][1], down_blocks)
-
-    out_y, _, out_sent = wide_sum(place, kept, given, "out", grad_first)
-    kept, given = results["rows"]
-
-    def up_first(own):
-        results["up"] = update_call(place, x, 0, grad + grad_far, up_blocks, "up_update", (own,))
-        return (results["up"],)
-
-    grad_in, _, sent = wide_sum(place, kept, hold(given, (out_sent,)), "grad", up_first)
-    new_up = results["up"]
-    new_down = update_call(place, x, 1, act + act_far, down_blocks, "down_update", (sent,))
+    own_out, *out_blocks = core_sum(kept, hold(given, near_done), "out")
+    kept, given = rows_call(place, grad + grad_far, half, w_up, "grad_rows", (own_out,))
+    out_got = x_exchange(out_blocks)
+    own, *blocks = core_sum(kept, hold(given, (*out_got, down_blocks)), "grad")
+    got = x_exchange(blocks)
+    out_keep, out_send = x_sum(own_out, out_got, "out", (own,))
+    new_up = update_call(place, x, 0, grad + grad_far, up_blocks, "up_update", (own, out_send))
+    keep, send = x_sum(own, got, "grad", (new_up,))
+    out_y = z_sum(place, out_keep, out_send, "out", (send,))
+    new_down = update_call(place, x, 1, act + act_far, down_blocks, "down_update", (send, out_y))
+    grad_in = z_sum(place, keep, send, "grad", (new_down,))
     return (out_y, grad_in, new_up, new_down)
 
 

time: 315 us -> 318 us (level)
  Pallas kernels: 90.4 us -> 94.8 us
    pallas_call x10, Pallas kernels: 11.7 us -> 15.4 us  [simple_call(): pl.pallas_call(run, out_shape=outs, in_specs=[spec(a) for a in ins] + [HB...]
    unnamed x98 -> x106, local copies, waits for them, and re-layouts: 37.6 us -> 36.8 us
  transfers between devices with their start and end apart: 35 -> 35, of which waited for: 20 -> 21; matrix products, arithmetic and copies ran while one was open for 1% -> 1% of each run, Pallas kernels for 23% -> 24%
where the time goes in v3:
time: 318 us; the launch traced here: 316 us
  waiting for transfers between devices  115 us (36%)
  Pallas kernels  94.8 us (30%)
  starting transfers between devices  63.9 us (20%)
  local copies, waits for them, and re-layouts  41 us (13%)
    pallas_call x9, Pallas kernels, call(): pl.pallas_call(run, out_shape=[shape for shape, _, _ in outs], grid_spec=...  71.2 us
    unnamed x106, local copies, waits for them, and re-layouts  36.8 us
    ppermute x2, waiting for transfers between devices, near_sum(): lax.ppermute(left, NARROW, Y_LEFT)  22.7 us
    ppermute x2, waiting for transfers between devices, narrow_gather(): lax.ppermute(own, NARROW, Y_RIGHT)  22.3 us
    ppermute x3, waiting for transfers between devices, wide_gather(): lax.ppermute(pair, WIDE, X_SHIFT[(4 - d) % 4])  20.8 us
    pallas_call x10, Pallas kernels, simple_call(): pl.pallas_call(run, out_shape=outs, in_specs=[spec(a) for a in ins] + [HB...  15.4 us
    ppermute x2, waiting for transfers between devices, own_sum(): return (keep, lax.ppermute(send, NARROW, ZHI_SWAP), send)  13.4 us
    ppermute x6, starting transfers between devices, x_exchange(): lax.ppermute(block, WIDE, X_SHIFT[d])  12.8 us
  transfers between devices with their start and end apart: 35, of which 21 were waited for; matrix products, arithmetic and copies ran while one was open for 1% of the time, Pallas kernels for 24%

profile of v3, /device:TPU:0, one launch (start us, length us, event | category | flops | bytes accessed | tf_op | source)
XLA Modules:
  0.0 316.2 jit_solution(2909591458622146493)
XLA Ops:
  6.7 6.3 %collective-permute-done = bf16[128,1024]{1,0:T(8,128)(2,1)S(1)} collective-permute-done((bf16[128,1024]{1,0:T(8,128)(2,1)S(1)}, bf16[128,1024]{1,0:T(8,128)(2,1)S(1)}, u32[]{:S(2)}, u32[]{:S(2)}) %collective-permute-start) | collective-permute-done | bytes 262176 | tf_op jit(solution)/shard_map/ppermute | solution.py:412
  18.8 9.6 %collective-permute-done.3.refs_3_ = bf16[2,128,1024]{2,1,0:T(8,128)(2,1)S(1)} collective-permute-done((bf16[2,128,1024]{2,1,0:T(8,128)(2,1)S(1)}, bf16[2,128,1024]{2,1,0:T(8,128)(2,1)S(1)}, u32[]{:S(2)}, u32[]{:S(2)}) %collective-permute-start.3) | collective-permute-done | bytes 524320 | tf_op jit(solution)/shard_map/ppermute | solution.py:414
  28.4 11.1 %collective-permute-done.2.refs_2_ = bf16[2,128,1024]{2,1,0:T(8,128)(2,1)S(1)} collective-permute-done((bf16[2,128,1024]{2,1,0:T(8,128)(2,1)S(1)}, bf16[2,128,1024]{2,1,0:T(8,128)(2,1)S(1)}, u32[]{:S(2)}, u32[]{:S(2)}) %collective-permute-start.2) | collective-permute-done | bytes 524320 | tf_op jit(solution)/shard_map/ppermute | solution.py:414
  39.8 4.1 %collective-permute-done.4 = bf16[8,128,1024]{2,1,0:T(8,128)(2,1)S(1)} collective-permute-done((bf16[8,128,1024]{2,1,0:T(8,128)(2,1)S(1)}, bf16[8,128,1024]{2,1,0:T(8,128)(2,1)S(1)}, u32[]{:S(2)}, u32[]{:S(2)}) %collective-permute-start.4) | collective-permute-done | bytes 2097184 | tf_op jit(solution)/shard_map/ppermute | solution.py:416
  46.8 5.8 %far.1 = (bf16[2,128,1920]{2,1,0:T(8,128)(2,1)}, bf16[2,128,1920]{2,1,0:T(8,128)(2,1)}) custom-call(s32[6]{0:T(128)S(1)} %concatenate.3.refs_0_.s_ref, bf16[8,2,4,16,1024]{4,3,2,1,0:T(8,128)(2,1)S(1)} %bitcast.9, bf16[8,2,4,16,1024]{4,3,2,1,0:T(8,128)(2,1)S(1)} %bitcast.19, bf16[8,2,4,16,1024]{4,3,2,1,0:T(8,128)(2,1)S(1)} %bitcast.10, ...), custom_call_target="tpu_custom_call" | custom-call | flops 2013265920 | bytes 5898240 | tf_op jit(solution)/shard_map/far/pallas_call | solution.py:55
  55.7 8.1 %relay.1 = (bf16[16,64,1920]{2,1,0:T(8,128)(2,1)S(1)}, bf16[16,64,1920]{2,1,0:T(8,128)(2,1)S(1)}) custom-call(s32[6]{0:T(128)S(1)} %concatenate.3.refs_0_.s_ref, bf16[1,1,1966592]{2,1,0:T(2,128)(2,1)S(1)} %copy-done.16, bf16[1,1,1966592]{2,1,0:T(2,128)(2,1)} %down_ref.1, bf16[2,128,1024]{2,1,0:T(8,128)(2,1)S(1)} %pad_maximum_fusion.refs_0_), custom_call_target="tpu_custom_call" | custom-call | bytes 32000000 | tf_op jit(solution)/shard_map/relay/pallas_call | solution.py:187
  67.7 5.2 %all-to-all-start = ((bf16[16,64,1920]{2,1,0:T(8,128)(2,1)}), bf16[16,64,1920]{2,1,0:T(8,128)(2,1)}, u32[]{:S(2)}, u32[]{:S(2)}) async-start(bf16[16,64,1920]{2,1,0:T(8,128)(2,1)} %hold.6), calls=%async_computation | async-start | bytes 7864320 | tf_op jit(solution)/shard_map/all_to_all | solution.py:306
  72.9 4.4 %collective-permute-done.6.refs_6_ = bf16[2,128,1920]{2,1,0:T(8,128)(2,1)S(1)} collective-permute-done((bf16[2,128,1920]{2,1,0:T(8,128)(2,1)}, bf16[2,128,1920]{2,1,0:T(8,128)(2,1)S(1)}, u32[]{:S(2)}, u32[]{:S(2)}) %collective-permute-start.6) | collective-permute-done | bytes 983072 | tf_op jit(solution)/shard_map/ppermute | solution.py:271
  77.3 3.4 %collective-permute-done.5.refs_5_ = bf16[2,128,1920]{2,1,0:T(8,128)(2,1)} collective-permute-done((bf16[2,128,1920]{2,1,0:T(8,128)(2,1)}, bf16[2,128,1920]{2,1,0:T(8,128)(2,1)}, u32[]{:S(2)}, u32[]{:S(2)}) %collective-permute-start.5) | collective-permute-done | bytes 983072 | tf_op jit(solution)/shard_map/ppermute | solution.py:271
  84.5 6.1 %hidden_near.1 = (bf16[256,1920]{1,0:T(8,128)(2,1)S(1)}, bf16[256,1920]{1,0:T(8,128)(2,1)S(1)}) custom-call(s32[6]{0:T(128)S(1)} %concatenate.3.refs_0_.s_ref, bf16[8,2,4,16,1024]{4,3,2,1,0:T(8,128)(2,1)S(1)} %bitcast.13, bf16[8,2,4,16,1024]{4,3,2,1,0:T(8,128)(2,1)S(1)} %bitcast.23, bf16[8,2,4,16,1024]{4,3,2,1,0:T(8,128)(2,1)S(1)} %bitcast.14, ...), custom_call_target="tpu_custom_call" | custom-call | flops 2013265920 | bytes 5898240 | tf_op jit(solution)/shard_map/hidden_near/pallas_call | solution.py:55
  92.6 6.4 %back_near.1 = (bf16[256,1920]{1,0:T(8,128)(2,1)}, bf16[256,1920]{1,0:T(8,128)(2,1)}) custom-call(s32[6]{0:T(128)S(1)} %concatenate.3.refs_0_.s_ref, bf16[8,2,4,16,1024]{4,3,2,1,0:T(8,128)(2,1)S(1)} %bitcast.15, bf16[8,2,4,16,1024]{4,3,2,1,0:T(8,128)(2,1)S(1)} %bitcast.25, bf16[8,2,4,16,1024]{4,3,2,1,0:T(8,128)(2,1)S(1)} %bitcast.16, ...), custom_call_target="tpu_custom_call" | custom-call | flops 2013265920 | bytes 5898240 | tf_op jit(solution)/shard_map/back_near/pallas_call | solution.py:55
  99.0 14.3 %collective-permute-done.8.refs_4_ = bf16[256,1920]{1,0:T(8,128)(2,1)S(1)} collective-permute-done((bf16[256,1920]{1,0:T(8,128)(2,1)S(1)}, bf16[256,1920]{1,0:T(8,128)(2,1)S(1)}, u32[]{:S(2)}, u32[]{:S(2)}) %collective-permute-start.8) | collective-permute-done | bytes 983072 | tf_op jit(solution)/shard_map/ppermute | solution.py:279
  114.7 3.7 %hidden_own.1 = (f32[128,1920]{1,0:T(8,128)S(1)}, bf16[128,1920]{1,0:T(8,128)(2,1)S(1)}) custom-call(s32[6]{0:T(128)S(1)} %concatenate.3.refs_0_.s_ref, bf16[8,2,4,16,1024]{4,3,2,1,0:T(8,128)(2,1)S(1)} %bitcast.17, bf16[8,2,4,16,1024]{4,3,2,1,0:T(8,128)(2,1)S(1)} %bitcast.27, bf16[1024,1920]{1,0:T(8,128)(2,1)S(1)} %copy-done.12, ...), custom_call_target="tpu_custom_call" | custom-call | flops 1006632960 | bytes 4915200 | tf_op jit(solution)/shard_map/hidden_own/pallas_call | solution.py:55
  118.4 3.6 %collective-permute-start.9 = (bf16[128,1920]{1,0:T(8,128)(2,1)S(1)}, bf16[128,1920]{1,0:T(8,128)(2,1)S(1)}, u32[]{:S(2)}, u32[]{:S(2)}) collective-permute-start(bf16[128,1920]{1,0:T(8,128)(2,1)S(1)} %get-tuple-element.38), channel_id=1, source_target_pairs={{0,1},{1,0},{2,3},{3,2},{4,5},{5,4},{6,7},{7,6},{8,9},{9,8},{10,11... | collective-permute-start | bytes 1474568 | tf_op jit(solution)/shard_map/ppermute | solution.py:286
  125.2 7.7 %collective-permute-done.9 = bf16[128,1920]{1,0:T(8,128)(2,1)S(1)} collective-permute-done((bf16[128,1920]{1,0:T(8,128)(2,1)S(1)}, bf16[128,1920]{1,0:T(8,128)(2,1)S(1)}, u32[]{:S(2)}, u32[]{:S(2)}) %collective-permute-start.9) | collective-permute-done | bytes 491552 | tf_op jit(solution)/shard_map/ppermute | solution.py:286
  136.0 8.4 %collective-permute-done.12.refs_4_ = bf16[256,1920]{1,0:T(8,128)(2,1)} collective-permute-done((bf16[256,1920]{1,0:T(8,128)(2,1)}, bf16[256,1920]{1,0:T(8,128)(2,1)}, u32[]{:S(2)}, u32[]{:S(2)}) %collective-permute-start.12) | collective-permute-done | bytes 983072 | tf_op jit(solution)/shard_map/ppermute | solution.py:279
  151.3 5.4 %back_own.1 = (f32[128,1920]{1,0:T(8,128)S(1)}, bf16[128,1920]{1,0:T(8,128)(2,1)S(1)}) custom-call(s32[6]{0:T(128)S(1)} %concatenate.3.refs_0_.s_ref, bf16[8,2,4,16,1024]{4,3,2,1,0:T(8,128)(2,1)S(1)} %bitcast.18, bf16[8,2,4,16,1024]{4,3,2,1,0:T(8,128)(2,1)S(1)} %bitcast.28, bf16[1024,1920]{1,0:T(8,128)(2,1)S(1)} %copy-done.7, ...), custom_call_target="tpu_custom_call" | custom-call | flops 1006632960 | bytes 4915200 | tf_op jit(solution)/shard_map/back_own/pallas_call | solution.py:55
  160.1 3.6 %collective-permute-start.13 = (bf16[256,1920]{1,0:T(8,128)(2,1)S(1)}, bf16[256,1920]{1,0:T(8,128)(2,1)S(1)}, u32[]{:S(2)}, u32[]{:S(2)}) collective-permute-start(bf16[256,1920]{1,0:T(8,128)(2,1)S(1)} %join_act.1.refs_0_.refs_2_), channel_id=1, source_target_pairs={{0,6},{1,7},{2,0},{3,1},{4,2},{5,3},{6,4},{7,5},{8,14},{9,15},{10,... | collective-permute-start | bytes 2949128 | tf_op jit(solution)/shard_map/ppermute | solution.py:300
  163.7 5.7 %collective-permute-done.17 = bf16[128,1920]{1,0:T(8,128)(2,1)S(1)} collective-permute-done((bf16[128,1920]{1,0:T(8,128)(2,1)S(1)}, bf16[128,1920]{1,0:T(8,128)(2,1)S(1)}, u32[]{:S(2)}, u32[]{:S(2)}) %collective-permute-start.17) | collective-permute-done | bytes 491552 | tf_op jit(solution)/shard_map/ppermute | solution.py:286
  170.5 14.3 %collective-permute-done.14.refs_2_.refs_4_ = bf16[256,1920]{1,0:T(8,128)(2,1)S(1)} collective-permute-done((bf16[256,1920]{1,0:T(8,128)(2,1)S(1)}, bf16[256,1920]{1,0:T(8,128)(2,1)S(1)}, u32[]{:S(2)}, u32[]{:S(2)}) %collective-permute-start.14) | collective-permute-done | bytes 983072 | tf_op jit(solution)/shard_map/ppermute | solution.py:300
  187.5 3.2 %collective-permute-start.16 = (bf16[128,1920]{1,0:T(8,128)(2,1)}, bf16[128,1920]{1,0:T(8,128)(2,1)S(1)}, u32[]{:S(2)}, u32[]{:S(2)}) collective-permute-start(bf16[128,1920]{1,0:T(8,128)(2,1)} %slice.17), channel_id=1, source_target_pairs={{0,6},{1,7},{2,0},{3,1},{4,2},{5,3},{6,4},{7,5},{8,14},{9,15},{10,... | collective-permute-start | bytes 1474568 | tf_op jit(solution)/shard_map/ppermute | solution.py:295
  191.5 6.5 %all-to-all-start.1 = ((bf16[16,64,1920]{2,1,0:T(8,128)(2,1)}), bf16[16,64,1920]{2,1,0:T(8,128)(2,1)}, u32[]{:S(2)}, u32[]{:S(2)}) async-start(bf16[16,64,1920]{2,1,0:T(8,128)(2,1)} %hold.7.refs_4_), calls=%async_computation.1 | async-start | bytes 7864320 | tf_op jit(solution)/shard_map/all_to_all | solution.py:306
  204.1 3.3 %collective-permute-start.19 = (bf16[256,1920]{1,0:T(8,128)(2,1)S(1)}, bf16[256,1920]{1,0:T(8,128)(2,1)S(1)}, u32[]{:S(2)}, u32[]{:S(2)}) collective-permute-start(bf16[256,1920]{1,0:T(8,128)(2,1)S(1)} %join_grad.1.refs_6_.refs_0_.refs_2_), channel_id=1, source_target_pairs={{0,6},{1,7},{2,0},{3,1},{4,2},{5,3},{6,4},{7,5},{8,14},{9,15},{10,... | collective-permute-start | bytes 2949128 | tf_op jit(solution)/shard_map/ppermute | solution.py:300
  208.5 10.8 %out_rows.1 = (f32[4,128,1024]{2,1,0:T(8,128)}, f32[4,128,1024]{2,1,0:T(8,128)}) custom-call(s32[6]{0:T(128)S(1)} %concatenate.3.refs_0_.s_ref, bf16[256,1920]{1,0:T(8,128)(2,1)S(1)} %join_act.1.refs_0_.refs_2_, bf16[256,1920]{1,0:T(8,128)(2,1)S(1)} %copy-done.25, bf16[256,1920]{1,0:T(8,128)(2,1)S(1)} %collective-permute-done.14.refs_2_.refs_4_, ...), custom_call_target="tpu_custom_call" | custom-call | flops 4026531840 | bytes 16252928 | tf_op jit(solution)/shard_map/out_rows/pallas_call | solution.py:55
  219.4 8.0 %collective-permute-done.20.refs_2_.refs_3_.refs_4_ = bf16[256,1920]{1,0:T(8,128)(2,1)S(1)} collective-permute-done((bf16[256,1920]{1,0:T(8,128)(2,1)S(1)}, bf16[256,1920]{1,0:T(8,128)(2,1)S(1)}, u32[]{:S(2)}, u32[]{:S(2)}) %collective-permute-start.20) | collective-permute-done | bytes 983072 | tf_op jit(solution)/shard_map/ppermute | solution.py:300
  234.2 3.4 %merge_out.1 = (f32[4,32,1024]{2,1,0:T(8,128)}, bf16[4,32,1024]{2,1,0:T(8,128)(2,1)}, bf16[4,32,1024]{2,1,0:T(8,128)(2,1)}, bf16[4,32,1024]{2,1,0:T(8,128)(2,1)}) custom-call(f32[4,128,1024]{2,1,0:T(8,128)} %get-tuple-element.44.refs_0_, f32[4,128,1024]{2,1,0:T(8,128)} %collective-permute-done.21.refs_1_), custom_call_target="tpu_custom_call" | custom-call | bytes 8000000 | tf_op jit(solution)/shard_map/merge_out/pallas_call | solution.py:103
  247.2 11.0 %grad_rows.1 = (f32[4,128,1024]{2,1,0:T(8,128)}, f32[4,128,1024]{2,1,0:T(8,128)}) custom-call(s32[6]{0:T(128)S(1)} %concatenate.3.refs_0_.s_ref, bf16[256,1920]{1,0:T(8,128)(2,1)S(1)} %copy-done.19, bf16[256,1920]{1,0:T(8,128)(2,1)S(1)} %copy-done.14, bf16[256,1920]{1,0:T(8,128)(2,1)} %copy-done.47, ...), custom_call_target="tpu_custom_call" | custom-call | flops 4026531840 | bytes 16252928 | tf_op jit(solution)/shard_map/grad_rows/pallas_call | solution.py:55
  258.2 4.0 %collective-permute-done.23.refs_2_ = bf16[4,32,1024]{2,1,0:T(8,128)(2,1)S(1)} collective-permute-done((bf16[4,32,1024]{2,1,0:T(8,128)(2,1)}, bf16[4,32,1024]{2,1,0:T(8,128)(2,1)S(1)}, u32[]{:S(2)}, u32[]{:S(2)}) %collective-permute-start.23) | collective-permute-done | bytes 262176 | tf_op jit(solution)/shard_map/ppermute | solution.py:396
  263.1 4.5 %collective-permute-done.27.refs_1_ = f32[4,128,1024]{2,1,0:T(8,128)} collective-permute-done((f32[4,128,1024]{2,1,0:T(8,128)}, f32[4,128,1024]{2,1,0:T(8,128)}, u32[]{:S(2)}, u32[]{:S(2)}) %collective-permute-start.27) | collective-permute-done | bytes 2097184 | tf_op jit(solution)/shard_map/ppermute | solution.py:388
  267.6 3.3 %merge_grad.1 = (f32[4,32,1024]{2,1,0:T(8,128)}, bf16[4,32,1024]{2,1,0:T(8,128)(2,1)}, bf16[4,32,1024]{2,1,0:T(8,128)(2,1)}, bf16[4,32,1024]{2,1,0:T(8,128)(2,1)}) custom-call(f32[4,128,1024]{2,1,0:T(8,128)} %get-tuple-element.50.refs_0_, f32[4,128,1024]{2,1,0:T(8,128)} %collective-permute-done.27.refs_1_), custom_call_target="tpu_custom_call" | custom-call | bytes 8000000 | tf_op jit(solution)/shard_map/merge_grad/pallas_call | solution.py:103
  283.8 11.2 %up_update.1.refs_4_ = bf16[1024,1920]{1,0:T(8,128)(2,1)} custom-call(s32[6]{0:T(128)S(1)} %concatenate.3.refs_0_.s_ref, bf16[8,2,4,16,1024]{4,3,2,1,0:T(8,128)(2,1)} %bitcast.11, bf16[8,2,4,16,1024]{4,3,2,1,0:T(8,128)(2,1)} %bitcast.21, bf16[256,1920]{1,0:T(8,128)(2,1)S(1)} %copy-done.20, bf16[256,1920]{1,0:T(8,128)(2,1)S(1)} %copy-done.14, ...), custom_call_target="tpu_custom_call" | custom-call | flops 4026531840 | bytes 13893632 | tf_op jit(solution)/shard_map/up_update/pallas_call | solution.py:55
  303.7 10.8 %down_update.1.refs_3_ = bf16[1024,1920]{1,0:T(8,128)(2,1)} custom-call(s32[6]{0:T(128)S(1)} %copy-done.45, bf16[8,2,4,16,1024]{4,3,2,1,0:T(8,128)(2,1)} %bitcast.12, bf16[8,2,4,16,1024]{4,3,2,1,0:T(8,128)(2,1)} %bitcast.22, bf16[256,1920]{1,0:T(8,128)(2,1)S(1)} %join_act.1.refs_0_.refs_2_, bf16[256,1920]{1,0:T(8,128)(2,1)S(1)} %copy-done.26, ...), custom_call_target="tpu_custom_call" | custom-call | flops 4026531840 | bytes 13893632 | tf_op jit(solution)/shard_map/down_update/pallas_call | solution.py:55
  (178 shorter events, 97.8 us)
Async XLA Ops:
  4.6 8.4 %collective-permute-start = (bf16[128,1024]{1,0:T(8,128)(2,1)S(1)}, bf16[128,1024]{1,0:T(8,128)(2,1)S(1)}, u32[]{:S(2)}, u32[]{:S(2)}) collective-permute-start(bf16[128,1024]{1,0:T(8,128)(2,1)S(1)} %pick.1), channel_id=1, source_target_pairs={{0,64},{8,72},{16,80},{24,88},{32,96},{40,104},{48,112},{56,120},{... | collective-permute-start | bytes 786440 | tf_op jit(solution)/shard_map/ppermute | solution.py:412
  13.1 15.3 %collective-permute-start.3 = (bf16[2,128,1024]{2,1,0:T(8,128)(2,1)S(1)}, bf16[2,128,1024]{2,1,0:T(8,128)(2,1)S(1)}, u32[]{:S(2)}, u32[]{:S(2)}) collective-permute-start(bf16[2,128,1024]{2,1,0:T(8,128)(2,1)S(1)} %pad_maximum_fusion.refs_0_), channel_id=1, source_target_pairs={{0,16},{8,24},{16,32},{24,40},{32,48},{40,56},{48,0},{56,8},{64,80... | collective-permute-start | bytes 1572872 | tf_op jit(solution)/shard_map/ppermute | solution.py:414
  14.6 24.9 %collective-permute-start.2 = (bf16[2,128,1024]{2,1,0:T(8,128)(2,1)S(1)}, bf16[2,128,1024]{2,1,0:T(8,128)(2,1)S(1)}, u32[]{:S(2)}, u32[]{:S(2)}) collective-permute-start(bf16[2,128,1024]{2,1,0:T(8,128)(2,1)S(1)} %pad_maximum_fusion.refs_0_), channel_id=1, source_target_pairs={{0,32},{8,40},{16,48},{24,56},{32,0},{40,8},{48,16},{56,24},{64,96... | collective-permute-start | bytes 1572872 | tf_op jit(solution)/shard_map/ppermute | solution.py:414
  17.4 22.2 %collective-permute-start.1 = (bf16[2,128,1024]{2,1,0:T(8,128)(2,1)S(1)}, bf16[2,128,1024]{2,1,0:T(8,128)(2,1)S(1)}, u32[]{:S(2)}, u32[]{:S(2)}) collective-permute-start(bf16[2,128,1024]{2,1,0:T(8,128)(2,1)S(1)} %pad_maximum_fusion.refs_0_), channel_id=1, source_target_pairs={{0,48},{8,56},{16,0},{24,8},{32,16},{40,24},{48,32},{56,40},{64,11... | collective-permute-start | bytes 1572872 | tf_op jit(solution)/shard_map/ppermute | solution.py:414
  52.7 24.7 %collective-permute-start.6 = (bf16[2,128,1920]{2,1,0:T(8,128)(2,1)}, bf16[2,128,1920]{2,1,0:T(8,128)(2,1)S(1)}, u32[]{:S(2)}, u32[]{:S(2)}) collective-permute-start(bf16[2,128,1920]{2,1,0:T(8,128)(2,1)} %get-tuple-element.33), channel_id=1, source_target_pairs={{0,6},{1,7},{2,0},{3,1},{4,2},{5,3},{6,4},{7,5},{8,14},{9,15},{10,... | collective-permute-start | bytes 2949128 | tf_op jit(solution)/shard_map/ppermute | solution.py:271
  55.7 25.0 %collective-permute-start.5 = (bf16[2,128,1920]{2,1,0:T(8,128)(2,1)}, bf16[2,128,1920]{2,1,0:T(8,128)(2,1)}, u32[]{:S(2)}, u32[]{:S(2)}) collective-permute-start(bf16[2,128,1920]{2,1,0:T(8,128)(2,1)} %get-tuple-element.32.refs_7_), channel_id=1, source_target_pairs={{0,2},{1,3},{2,4},{3,5},{4,6},{5,7},{6,0},{7,1},{8,10},{9,11},{10,... | collective-permute-start | bytes 2949128 | tf_op jit(solution)/shard_map/ppermute | solution.py:271
  67.7 68.3 %all-to-all-start = ((bf16[16,64,1920]{2,1,0:T(8,128)(2,1)}), bf16[16,64,1920]{2,1,0:T(8,128)(2,1)}, u32[]{:S(2)}, u32[]{:S(2)}) async-start(bf16[16,64,1920]{2,1,0:T(8,128)(2,1)} %hold.6), calls=%async_computation | async-start | bytes 7864320 | tf_op jit(solution)/shard_map/all_to_all | solution.py:306
  90.5 22.7 %collective-permute-start.8 = (bf16[256,1920]{1,0:T(8,128)(2,1)S(1)}, bf16[256,1920]{1,0:T(8,128)(2,1)S(1)}, u32[]{:S(2)}, u32[]{:S(2)}) collective-permute-start(bf16[256,1920]{1,0:T(8,128)(2,1)S(1)} %get-tuple-element.35), channel_id=1, source_target_pairs={{0,6},{1,7},{2,0},{3,1},{4,2},{5,3},{6,4},{7,5},{8,14},{9,15},{10,... | collective-permute-start | bytes 2949128 | tf_op jit(solution)/shard_map/ppermute | solution.py:279
  90.8 23.9 %collective-permute-start.7 = (bf16[256,1920]{1,0:T(8,128)(2,1)S(1)}, bf16[256,1920]{1,0:T(8,128)(2,1)S(1)}, u32[]{:S(2)}, u32[]{:S(2)}) collective-permute-start(bf16[256,1920]{1,0:T(8,128)(2,1)S(1)} %get-tuple-element.34.refs_7_), channel_id=1, source_target_pairs={{0,2},{1,3},{2,4},{3,5},{4,6},{5,7},{6,0},{7,1},{8,10},{9,11},{10,... | collective-permute-start | bytes 2949128 | tf_op jit(solution)/shard_map/ppermute | solution.py:279
  118.4 14.5 %collective-permute-start.9 = (bf16[128,1920]{1,0:T(8,128)(2,1)S(1)}, bf16[128,1920]{1,0:T(8,128)(2,1)S(1)}, u32[]{:S(2)}, u32[]{:S(2)}) collective-permute-start(bf16[128,1920]{1,0:T(8,128)(2,1)S(1)} %get-tuple-element.38), channel_id=1, source_target_pairs={{0,1},{1,0},{2,3},{3,2},{4,5},{5,4},{6,7},{7,6},{8,9},{9,8},{10,11... | collective-permute-start | bytes 1474568 | tf_op jit(solution)/shard_map/ppermute | solution.py:286
  122.0 23.1 %collective-permute-start.11 = (bf16[256,1920]{1,0:T(8,128)(2,1)}, bf16[256,1920]{1,0:T(8,128)(2,1)}, u32[]{:S(2)}, u32[]{:S(2)}) collective-permute-start(bf16[256,1920]{1,0:T(8,128)(2,1)} %get-tuple-element.36.refs_5_), channel_id=1, source_target_pairs={{0,2},{1,3},{2,4},{3,5},{4,6},{5,7},{6,0},{7,1},{8,10},{9,11},{10,... | collective-permute-start | bytes 2949128 | tf_op jit(solution)/shard_map/ppermute | solution.py:279
  122.3 22.1 %collective-permute-start.12 = (bf16[256,1920]{1,0:T(8,128)(2,1)}, bf16[256,1920]{1,0:T(8,128)(2,1)}, u32[]{:S(2)}, u32[]{:S(2)}) collective-permute-start(bf16[256,1920]{1,0:T(8,128)(2,1)} %get-tuple-element.39), channel_id=1, source_target_pairs={{0,6},{1,7},{2,0},{3,1},{4,2},{5,3},{6,4},{7,5},{8,14},{9,15},{10,... | collective-permute-start | bytes 2949128 | tf_op jit(solution)/shard_map/ppermute | solution.py:279
  134.0 13.6 %collective-permute-start.10 = (bf16[128,1920]{1,0:T(8,128)(2,1)S(1)}, bf16[128,1920]{1,0:T(8,128)(2,1)S(1)}, u32[]{:S(2)}, u32[]{:S(2)}) collective-permute-start(bf16[128,1920]{1,0:T(8,128)(2,1)S(1)} %multiply_convert_fusion.refs_0_), channel_id=1, source_target_pairs={{0,1},{1,0},{2,3},{3,2},{4,5},{5,4},{6,7},{7,6},{8,9},{9,8},{10,11... | collective-permute-start | bytes 1474568 | tf_op jit(solution)/shard_map/ppermute | solution.py:481
  156.7 12.7 %collective-permute-start.17 = (bf16[128,1920]{1,0:T(8,128)(2,1)S(1)}, bf16[128,1920]{1,0:T(8,128)(2,1)S(1)}, u32[]{:S(2)}, u32[]{:S(2)}) collective-permute-start(bf16[128,1920]{1,0:T(8,128)(2,1)S(1)} %get-tuple-element.41.refs_2_), channel_id=1, source_target_pairs={{0,1},{1,0},{2,3},{3,2},{4,5},{5,4},{6,7},{7,6},{8,9},{9,8},{10,11... | collective-permute-start | bytes 1474568 | tf_op jit(solution)/shard_map/ppermute | solution.py:286
  159.3 25.5 %collective-permute-start.14 = (bf16[256,1920]{1,0:T(8,128)(2,1)S(1)}, bf16[256,1920]{1,0:T(8,128)(2,1)S(1)}, u32[]{:S(2)}, u32[]{:S(2)}) collective-permute-start(bf16[256,1920]{1,0:T(8,128)(2,1)S(1)} %join_act.1.refs_0_.refs_2_), channel_id=1, source_target_pairs={{0,2},{1,3},{2,4},{3,5},{4,6},{5,7},{6,0},{7,1},{8,10},{9,11},{10,... | collective-permute-start | bytes 2949128 | tf_op jit(solution)/shard_map/ppermute | solution.py:300
  160.1 25.5 %collective-permute-start.13 = (bf16[256,1920]{1,0:T(8,128)(2,1)S(1)}, bf16[256,1920]{1,0:T(8,128)(2,1)S(1)}, u32[]{:S(2)}, u32[]{:S(2)}) collective-permute-start(bf16[256,1920]{1,0:T(8,128)(2,1)S(1)} %join_act.1.refs_0_.refs_2_), channel_id=1, source_target_pairs={{0,6},{1,7},{2,0},{3,1},{4,2},{5,3},{6,4},{7,5},{8,14},{9,15},{10,... | collective-permute-start | bytes 2949128 | tf_op jit(solution)/shard_map/ppermute | solution.py:300
  170.0 20.7 %collective-permute-start.18 = (bf16[128,1920]{1,0:T(8,128)(2,1)S(1)}, bf16[128,1920]{1,0:T(8,128)(2,1)S(1)}, u32[]{:S(2)}, u32[]{:S(2)}) collective-permute-start(bf16[128,1920]{1,0:T(8,128)(2,1)S(1)} %fusion.5.refs_0_), channel_id=1, source_target_pairs={{0,1},{1,0},{2,3},{3,2},{4,5},{5,4},{6,7},{7,6},{8,9},{9,8},{10,11... | collective-permute-start | bytes 1474568 | tf_op jit(solution)/shard_map/ppermute | solution.py:485
  185.7 13.1 %collective-permute-start.15 = (bf16[128,1920]{1,0:T(8,128)(2,1)}, bf16[128,1920]{1,0:T(8,128)(2,1)S(1)}, u32[]{:S(2)}, u32[]{:S(2)}) collective-permute-start(bf16[128,1920]{1,0:T(8,128)(2,1)} %slice.16), channel_id=1, source_target_pairs={{0,2},{1,3},{2,4},{3,5},{4,6},{5,7},{6,0},{7,1},{8,10},{9,11},{10,... | collective-permute-start | bytes 1474568 | tf_op jit(solution)/shard_map/ppermute | solution.py:295
  187.5 12.5 %collective-permute-start.16 = (bf16[128,1920]{1,0:T(8,128)(2,1)}, bf16[128,1920]{1,0:T(8,128)(2,1)S(1)}, u32[]{:S(2)}, u32[]{:S(2)}) collective-permute-start(bf16[128,1920]{1,0:T(8,128)(2,1)} %slice.17), channel_id=1, source_target_pairs={{0,6},{1,7},{2,0},{3,1},{4,2},{5,3},{6,4},{7,5},{8,14},{9,15},{10,... | collective-permute-start | bytes 1474568 | tf_op jit(solution)/shard_map/ppermute | solution.py:295
  191.5 66.7 %all-to-all-start.1 = ((bf16[16,64,1920]{2,1,0:T(8,128)(2,1)}), bf16[16,64,1920]{2,1,0:T(8,128)(2,1)}, u32[]{:S(2)}, u32[]{:S(2)}) async-start(bf16[16,64,1920]{2,1,0:T(8,128)(2,1)} %hold.7.refs_4_), calls=%async_computation.1 | async-start | bytes 7864320 | tf_op jit(solution)/shard_map/all_to_all | solution.py:306
  203.9 23.5 %collective-permute-start.20 = (bf16[256,1920]{1,0:T(8,128)(2,1)S(1)}, bf16[256,1920]{1,0:T(8,128)(2,1)S(1)}, u32[]{:S(2)}, u32[]{:S(2)}) collective-permute-start(bf16[256,1920]{1,0:T(8,128)(2,1)S(1)} %join_grad.1.refs_6_.refs_0_.refs_2_), channel_id=1, source_target_pairs={{0,2},{1,3},{2,4},{3,5},{4,6},{5,7},{6,0},{7,1},{8,10},{9,11},{10,... | collective-permute-start | bytes 2949128 | tf_op jit(solution)/shard_map/ppermute | solution.py:300
  204.1 24.1 %collective-permute-start.19 = (bf16[256,1920]{1,0:T(8,128)(2,1)S(1)}, bf16[256,1920]{1,0:T(8,128)(2,1)S(1)}, u32[]{:S(2)}, u32[]{:S(2)}) collective-permute-start(bf16[256,1920]{1,0:T(8,128)(2,1)S(1)} %join_grad.1.refs_6_.refs_0_.refs_2_), channel_id=1, source_target_pairs={{0,6},{1,7},{2,0},{3,1},{4,2},{5,3},{6,4},{7,5},{8,14},{9,15},{10,... | collective-permute-start | bytes 2949128 | tf_op jit(solution)/shard_map/ppermute | solution.py:300
  229.7 15.2 %collective-permute-start.25 = (bf16[128,1920]{1,0:T(8,128)(2,1)}, bf16[128,1920]{1,0:T(8,128)(2,1)}, u32[]{:S(2)}, u32[]{:S(2)}) collective-permute-start(bf16[128,1920]{1,0:T(8,128)(2,1)} %hold.9), channel_id=1, source_target_pairs={{0,2},{1,3},{2,4},{3,5},{4,6},{5,7},{6,0},{7,1},{8,10},{9,11},{10,... | collective-permute-start | bytes 1474568 | tf_op jit(solution)/shard_map/ppermute | solution.py:295
  229.8 15.1 %collective-permute-start.26 = (bf16[128,1920]{1,0:T(8,128)(2,1)}, bf16[128,1920]{1,0:T(8,128)(2,1)}, u32[]{:S(2)}, u32[]{:S(2)}) collective-permute-start(bf16[128,1920]{1,0:T(8,128)(2,1)} %hold.10), channel_id=1, source_target_pairs={{0,6},{1,7},{2,0},{3,1},{4,2},{5,3},{6,4},{7,5},{8,14},{9,15},{10,... | collective-permute-start | bytes 1474568 | tf_op jit(solution)/shard_map/ppermute | solution.py:295
  237.6 20.6 %collective-permute-start.22 = (bf16[4,32,1024]{2,1,0:T(8,128)(2,1)}, bf16[4,32,1024]{2,1,0:T(8,128)(2,1)S(1)}, u32[]{:S(2)}, u32[]{:S(2)}) collective-permute-start(bf16[4,32,1024]{2,1,0:T(8,128)(2,1)} %get-tuple-element.47), channel_id=1, source_target_pairs={{0,16},{8,24},{16,32},{24,40},{32,48},{40,56},{48,0},{56,8},{64,80... | collective-permute-start | bytes 786440 | tf_op jit(solution)/shard_map/ppermute | solution.py:396
  239.3 23.0 %collective-permute-start.23 = (bf16[4,32,1024]{2,1,0:T(8,128)(2,1)}, bf16[4,32,1024]{2,1,0:T(8,128)(2,1)S(1)}, u32[]{:S(2)}, u32[]{:S(2)}) collective-permute-start(bf16[4,32,1024]{2,1,0:T(8,128)(2,1)} %get-tuple-element.48), channel_id=1, source_target_pairs={{0,32},{8,40},{16,48},{24,56},{32,0},{40,8},{48,16},{56,24},{64,96... | collective-permute-start | bytes 786440 | tf_op jit(solution)/shard_map/ppermute | solution.py:396
  241.9 20.3 %collective-permute-start.24 = (bf16[4,32,1024]{2,1,0:T(8,128)(2,1)}, bf16[4,32,1024]{2,1,0:T(8,128)(2,1)S(1)}, u32[]{:S(2)}, u32[]{:S(2)}) collective-permute-start(bf16[4,32,1024]{2,1,0:T(8,128)(2,1)} %get-tuple-element.49), channel_id=1, source_target_pairs={{0,48},{8,56},{16,0},{24,8},{32,16},{40,24},{48,32},{56,40},{64,11... | collective-permute-start | bytes 786440 | tf_op jit(solution)/shard_map/ppermute | solution.py:396
  273.0 25.1 %collective-permute-start.28 = (bf16[4,16,1024]{2,1,0:T(8,128)(2,1)}, bf16[4,16,1024]{2,1,0:T(8,128)(2,1)}, u32[]{:S(2)}, u32[]{:S(2)}) collective-permute-start(bf16[4,16,1024]{2,1,0:T(8,128)(2,1)} %get-tuple-element.54.refs_9_), channel_id=1, source_target_pairs={{0,64},{8,72},{16,80},{24,88},{32,96},{40,104},{48,112},{56,120},{... | collective-permute-start | bytes 393224 | tf_op jit(solution)/shard_map/ppermute | solution.py:406
  274.2 20.9 %collective-permute-start.29 = (bf16[4,32,1024]{2,1,0:T(8,128)(2,1)}, bf16[4,32,1024]{2,1,0:T(8,128)(2,1)}, u32[]{:S(2)}, u32[]{:S(2)}) collective-permute-start(bf16[4,32,1024]{2,1,0:T(8,128)(2,1)} %get-tuple-element.55), channel_id=1, source_target_pairs={{0,16},{8,24},{16,32},{24,40},{32,48},{40,56},{48,0},{56,8},{64,80... | collective-permute-start | bytes 786440 | tf_op jit(solution)/shard_map/ppermute | solution.py:396
  275.5 19.6 %collective-permute-start.30 = (bf16[4,32,1024]{2,1,0:T(8,128)(2,1)}, bf16[4,32,1024]{2,1,0:T(8,128)(2,1)}, u32[]{:S(2)}, u32[]{:S(2)}) collective-permute-start(bf16[4,32,1024]{2,1,0:T(8,128)(2,1)} %get-tuple-element.56), channel_id=1, source_target_pairs={{0,32},{8,40},{16,48},{24,56},{32,0},{40,8},{48,16},{56,24},{64,96... | collective-permute-start | bytes 786440 | tf_op jit(solution)/shard_map/ppermute | solution.py:396
  278.0 17.0 %collective-permute-start.31 = (bf16[4,32,1024]{2,1,0:T(8,128)(2,1)}, bf16[4,32,1024]{2,1,0:T(8,128)(2,1)}, u32[]{:S(2)}, u32[]{:S(2)}) collective-permute-start(bf16[4,32,1024]{2,1,0:T(8,128)(2,1)} %get-tuple-element.57), channel_id=1, source_target_pairs={{0,48},{8,56},{16,0},{24,8},{32,16},{40,24},{48,32},{56,40},{64,11... | collective-permute-start | bytes 786440 | tf_op jit(solution)/shard_map/ppermute | solution.py:396
  297.2 17.3 %collective-permute-start.32 = (bf16[4,16,1024]{2,1,0:T(8,128)(2,1)}, bf16[4,16,1024]{2,1,0:T(8,128)(2,1)}, u32[]{:S(2)}, u32[]{:S(2)}) collective-permute-start(bf16[4,16,1024]{2,1,0:T(8,128)(2,1)} %get-tuple-element.58.refs_3_.refs_8_), channel_id=1, source_target_pairs={{0,64},{8,72},{16,80},{24,88},{32,96},{40,104},{48,112},{56,120},{... | collective-permute-start | bytes 393224 | tf_op jit(solution)/shard_map/ppermute | solution.py:406
  (56 other events, 604.0 us)

commit v4 on v3

--- a/solution.py
+++ b/solution.py
@@ -449,7 +449,7 @@
         + [(gathered, (parts, n_rows, CB), lambda j, s: (0, 0, j))],
         [col(sds((depth, width), BF16))],
         [pltpu.VMEM((depth, 8 * half), BF16)],
-        50,
+        62,
         (16 * half * depth * width, 16 * half * (depth + width) + 4 * depth * width),
         name,
         after,
@@ -471,7 +471,7 @@
     half = half_rows(x)
 
     far, far_done = far_sum(place, x, w_up, w_down, ())
-    up_blocks = exchange(hold(to_up, (joined,)))
+    down_blocks = exchange(hold(to_down, (joined,)))
     near_h, done = near_sum(place, x, 0, w_up, far, "hidden", (far_done,))
     near_b, done = near_sum(place, x, 1, w_down, far, "back", (done,))
 
@@ -479,27 +479,27 @@
     gelu_value, slope = gelu_parts(keep + other.astype(F32))
     mine = gelu_value.astype(BF16)
     act_other = lax.ppermute(mine, NARROW, ZHI_SWAP)
-    keep, other, done = own_sum(place, x, 1, w_down, near_b, "back", (act_other, up_blocks))
+    keep, other, done = own_sum(place, x, 1, w_down, near_b, "back", (act_other, down_blocks))
     act, act_far = narrow_gather(mine, act_other, "act", (done,))
     hidden_grad = ((keep + other.astype(F32)) * slope).astype(BF16)
     grad_other = lax.ppermute(hidden_grad, NARROW, ZHI_SWAP)
-    to_down = hold(to_down, (grad_other,))
-    down_blocks = exchange(to_down)
-    grad, _ = narrow_gather(hidden_grad, grad_other, "grad", (act_far[0], act_far[1], to_down), False)
+    to_up = hold(to_up, (grad_other,))
+    up_blocks = exchange(to_up)
+    grad, _ = narrow_gather(hidden_grad, grad_other, "grad", (act_far[0], act_far[1], to_up), False)
     kept, given = rows_call(place, act + act_far, half, w_down, "out_rows", (grad[0],))
     near_done = (grad[1], grad[2])
-    grad_far = far_gather(grad, (given, *near_done))
+    new_down = update_call(place, x, 1, act + act_far, down_blocks, "down_update", (given,))
+    grad_far = far_gather(grad, (new_down, *near_done))
     own_out, *out_blocks = core_sum(kept, hold(given, near_done), "out")
     kept, given = rows_call(place, grad + grad_far, half, w_up, "grad_rows", (own_out,))
     out_got = x_exchange(out_blocks)
-    own, *blocks = core_sum(kept, hold(given, (*out_got, down_blocks)), "grad")
+    own, *blocks = core_sum(kept, hold(given, (*out_got, up_blocks)), "grad")
     got = x_exchange(blocks)
     out_keep, out_send = x_sum(own_out, out_got, "out", (own,))
     new_up = update_call(place, x, 0, grad + grad_far, up_blocks, "up_update", (own, out_send))
     keep, send = x_sum(own, got, "grad", (new_up,))
     out_y = z_sum(place, out_keep, out_send, "out", (send,))
-    new_down = update_call(place, x, 1, act + act_far, down_blocks, "down_update", (send, out_y))
-    grad_in = z_sum(place, keep, send, "grad", (new_down,))
+    grad_in = z_sum(place, keep, send, "grad", (out_y,))
     return (out_y, grad_in, new_up, new_down)
 
 

time: 318 us -> 308 us (0.969)
  waiting for transfers between devices: 115 us -> 106 us
  local copies, waits for them, and re-layouts: 41 us -> 37 us
    ppermute x2, waiting for transfers between devices: 22.7 us -> 0.01 us  [near_sum(): lax.ppermute(left, NARROW, Y_LEFT)]
    ppermute x2, waiting for transfers between devices: 2.16 us -> 22.8 us  [near_sum(): lax.ppermute(right, NARROW, Y_RIGHT)]
    ppermute x2, waiting for transfers between devices: 22.3 us -> 10.5 us  [narrow_gather(): lax.ppermute(own, NARROW, Y_RIGHT)]
    ppermute x2, waiting for transfers between devices: 13.4 us -> 18.8 us  [own_sum(): return (keep, lax.ppermute(send, NARROW, ZHI_SWAP), send)]
    unnamed x106 -> x100, local copies, waits for them, and re-layouts: 36.8 us -> 31.8 us
    ppermute x1, waiting for transfers between devices: 4.42 us -> 0.13 us  [far_sum(): lax.ppermute(b, NARROW, Y_LEFT)]
    ppermute x1, waiting for transfers between devices: 2.51 us -> 6.58 us  [body(): act_other = lax.ppermute(mine, NARROW, ZHI_SWAP)]
    ppermute x6, waiting for transfers between devices: 4.01 us -> 0.02 us  [x_exchange(): lax.ppermute(block, WIDE, X_SHIFT[d])]
  transfers between devices with their start and end apart: 35 -> 35, of which waited for: 21 -> 18; matrix products, arithmetic and copies ran while one was open for 1% -> 2% of each run, Pallas kernels for 24% -> 26%
where the time goes in v4:
time: 308 us; the launch traced here: 306 us
  waiting for transfers between devices  106 us (34%)
  Pallas kernels  97.6 us (32%)
  starting transfers between devices  62.7 us (20%)
  local copies, waits for them, and re-layouts  37 us (12%)
    pallas_call x9, Pallas kernels, call(): pl.pallas_call(run, out_shape=[shape for shape, _, _ in outs], grid_spec=...  72.9 us
    unnamed x100, local copies, waits for them, and re-layouts  31.8 us
    ppermute x3, waiting for transfers between devices, wide_gather(): lax.ppermute(pair, WIDE, X_SHIFT[(4 - d) % 4])  23.8 us
    ppermute x2, waiting for transfers between devices, near_sum(): lax.ppermute(right, NARROW, Y_RIGHT)  22.8 us
    ppermute x2, waiting for transfers between devices, own_sum(): return (keep, lax.ppermute(send, NARROW, ZHI_SWAP), send)  18.8 us
    pallas_call x10, Pallas kernels, simple_call(): pl.pallas_call(run, out_shape=outs, in_specs=[spec(a) for a in ins] + [HB...  16.5 us
    ppermute x6, starting transfers between devices, x_exchange(): lax.ppermute(block, WIDE, X_SHIFT[d])  14.4 us
    all_to_all x2, starting transfers between devices, exchange(): return lax.all_to_all(blocks, WIDE, 0, 0, tiled=True)  11.5 us
  transfers between devices with their start and end apart: 35, of which 18 were waited for; matrix products, arithmetic and copies ran while one was open for 2% of the time, Pallas kernels for 26%

profile of v4, /device:TPU:0, one launch (start us, length us, event | category | flops | bytes accessed | tf_op | source)
XLA Modules:
  0.0 305.9 jit_solution(747338445936809849)
XLA Ops:
  6.7 6.3 %collective-permute-done = bf16[128,1024]{1,0:T(8,128)(2,1)S(1)} collective-permute-done((bf16[128,1024]{1,0:T(8,128)(2,1)S(1)}, bf16[128,1024]{1,0:T(8,128)(2,1)S(1)}, u32[]{:S(2)}, u32[]{:S(2)}) %collective-permute-start) | collective-permute-done | bytes 262176 | tf_op jit(solution)/shard_map/ppermute | solution.py:412
  17.6 20.1 %collective-permute-done.1.refs_1_ = bf16[2,128,1024]{2,1,0:T(8,128)(2,1)S(1)} collective-permute-done((bf16[2,128,1024]{2,1,0:T(8,128)(2,1)S(1)}, bf16[2,128,1024]{2,1,0:T(8,128)(2,1)S(1)}, u32[]{:S(2)}, u32[]{:S(2)}) %collective-permute-start.1) | collective-permute-done | bytes 524320 | tf_op jit(solution)/shard_map/ppermute | solution.py:414
  37.7 3.7 %collective-permute-done.3.refs_3_ = bf16[2,128,1024]{2,1,0:T(8,128)(2,1)S(1)} collective-permute-done((bf16[2,128,1024]{2,1,0:T(8,128)(2,1)S(1)}, bf16[2,128,1024]{2,1,0:T(8,128)(2,1)S(1)}, u32[]{:S(2)}, u32[]{:S(2)}) %collective-permute-start.3) | collective-permute-done | bytes 524320 | tf_op jit(solution)/shard_map/ppermute | solution.py:414
  41.6 4.1 %collective-permute-done.4 = bf16[8,128,1024]{2,1,0:T(8,128)(2,1)S(1)} collective-permute-done((bf16[8,128,1024]{2,1,0:T(8,128)(2,1)S(1)}, bf16[8,128,1024]{2,1,0:T(8,128)(2,1)S(1)}, u32[]{:S(2)}, u32[]{:S(2)}) %collective-permute-start.4) | collective-permute-done | bytes 2097184 | tf_op jit(solution)/shard_map/ppermute | solution.py:416
  48.6 5.8 %far.1 = (bf16[2,128,1920]{2,1,0:T(8,128)(2,1)}, bf16[2,128,1920]{2,1,0:T(8,128)(2,1)}) custom-call(s32[6]{0:T(128)S(1)} %concatenate.3.refs_0_.s_ref, bf16[8,2,4,16,1024]{4,3,2,1,0:T(8,128)(2,1)S(1)} %bitcast.9, bf16[8,2,4,16,1024]{4,3,2,1,0:T(8,128)(2,1)S(1)} %bitcast.19, bf16[8,2,4,16,1024]{4,3,2,1,0:T(8,128)(2,1)S(1)} %bitcast.10, ...), custom_call_target="tpu_custom_call" | custom-call | flops 2013265920 | bytes 5898240 | tf_op jit(solution)/shard_map/far/pallas_call | solution.py:55
  57.7 8.1 %relay.1 = (bf16[16,64,1920]{2,1,0:T(8,128)(2,1)S(1)}, bf16[16,64,1920]{2,1,0:T(8,128)(2,1)S(1)}) custom-call(s32[6]{0:T(128)S(1)} %concatenate.3.refs_0_.s_ref, bf16[1,1,1966592]{2,1,0:T(2,128)(2,1)S(1)} %copy-done.17, bf16[1,1,1966592]{2,1,0:T(2,128)(2,1)} %down_ref.1, bf16[2,128,1024]{2,1,0:T(8,128)(2,1)S(1)} %pad_maximum_fusion.refs_0_), custom_call_target="tpu_custom_call" | custom-call | bytes 32000000 | tf_op jit(solution)/shard_map/relay/pallas_call | solution.py:187
  69.8 4.7 %all-to-all-start = ((bf16[16,64,1920]{2,1,0:T(8,128)(2,1)}), bf16[16,64,1920]{2,1,0:T(8,128)(2,1)}, u32[]{:S(2)}, u32[]{:S(2)}) async-start(bf16[16,64,1920]{2,1,0:T(8,128)(2,1)} %hold.6), calls=%async_computation | async-start | bytes 7864320 | tf_op jit(solution)/shard_map/all_to_all | solution.py:306
  74.5 5.3 %collective-permute-done.5.refs_5_ = bf16[2,128,1920]{2,1,0:T(8,128)(2,1)S(1)} collective-permute-done((bf16[2,128,1920]{2,1,0:T(8,128)(2,1)}, bf16[2,128,1920]{2,1,0:T(8,128)(2,1)S(1)}, u32[]{:S(2)}, u32[]{:S(2)}) %collective-permute-start.5) | collective-permute-done | bytes 983072 | tf_op jit(solution)/shard_map/ppermute | solution.py:271
  83.6 6.1 %hidden_near.1 = (bf16[256,1920]{1,0:T(8,128)(2,1)S(1)}, bf16[256,1920]{1,0:T(8,128)(2,1)S(1)}) custom-call(s32[6]{0:T(128)S(1)} %concatenate.3.refs_0_.s_ref, bf16[8,2,4,16,1024]{4,3,2,1,0:T(8,128)(2,1)S(1)} %bitcast.13, bf16[8,2,4,16,1024]{4,3,2,1,0:T(8,128)(2,1)S(1)} %bitcast.23, bf16[8,2,4,16,1024]{4,3,2,1,0:T(8,128)(2,1)S(1)} %bitcast.14, ...), custom_call_target="tpu_custom_call" | custom-call | flops 2013265920 | bytes 5898240 | tf_op jit(solution)/shard_map/hidden_near/pallas_call | solution.py:55
  93.0 6.4 %back_near.1 = (bf16[256,1920]{1,0:T(8,128)(2,1)}, bf16[256,1920]{1,0:T(8,128)(2,1)}) custom-call(s32[6]{0:T(128)S(1)} %concatenate.3.refs_0_.s_ref, bf16[8,2,4,16,1024]{4,3,2,1,0:T(8,128)(2,1)S(1)} %bitcast.15, bf16[8,2,4,16,1024]{4,3,2,1,0:T(8,128)(2,1)S(1)} %bitcast.25, bf16[8,2,4,16,1024]{4,3,2,1,0:T(8,128)(2,1)S(1)} %bitcast.16, ...), custom_call_target="tpu_custom_call" | custom-call | flops 2013265920 | bytes 5898240 | tf_op jit(solution)/shard_map/back_near/pallas_call | solution.py:55
  99.4 14.5 %collective-permute-done.7.refs_3_ = bf16[256,1920]{1,0:T(8,128)(2,1)S(1)} collective-permute-done((bf16[256,1920]{1,0:T(8,128)(2,1)S(1)}, bf16[256,1920]{1,0:T(8,128)(2,1)S(1)}, u32[]{:S(2)}, u32[]{:S(2)}) %collective-permute-start.7) | collective-permute-done | bytes 983072 | tf_op jit(solution)/shard_map/ppermute | solution.py:279
  113.9 3.7 %hidden_own.1 = (f32[128,1920]{1,0:T(8,128)S(1)}, bf16[128,1920]{1,0:T(8,128)(2,1)S(1)}) custom-call(s32[6]{0:T(128)S(1)} %concatenate.3.refs_0_.s_ref, bf16[8,2,4,16,1024]{4,3,2,1,0:T(8,128)(2,1)S(1)} %bitcast.17, bf16[8,2,4,16,1024]{4,3,2,1,0:T(8,128)(2,1)S(1)} %bitcast.27, bf16[1024,1920]{1,0:T(8,128)(2,1)S(1)} %copy-done.12, ...), custom_call_target="tpu_custom_call" | custom-call | flops 1006632960 | bytes 4915200 | tf_op jit(solution)/shard_map/hidden_own/pallas_call | solution.py:55
  117.6 3.6 %collective-permute-start.9 = (bf16[128,1920]{1,0:T(8,128)(2,1)S(1)}, bf16[128,1920]{1,0:T(8,128)(2,1)S(1)}, u32[]{:S(2)}, u32[]{:S(2)}) collective-permute-start(bf16[128,1920]{1,0:T(8,128)(2,1)S(1)} %get-tuple-element.38), channel_id=1, source_target_pairs={{0,1},{1,0},{2,3},{3,2},{4,5},{5,4},{6,7},{7,6},{8,9},{9,8},{10,11... | collective-permute-start | bytes 1474568 | tf_op jit(solution)/shard_map/ppermute | solution.py:286
  124.4 9.9 %collective-permute-done.9 = bf16[128,1920]{1,0:T(8,128)(2,1)S(1)} collective-permute-done((bf16[128,1920]{1,0:T(8,128)(2,1)S(1)}, bf16[128,1920]{1,0:T(8,128)(2,1)S(1)}, u32[]{:S(2)}, u32[]{:S(2)}) %collective-permute-start.9) | collective-permute-done | bytes 491552 | tf_op jit(solution)/shard_map/ppermute | solution.py:286
  136.2 8.4 %collective-permute-done.11.refs_3_ = bf16[256,1920]{1,0:T(8,128)(2,1)} collective-permute-done((bf16[256,1920]{1,0:T(8,128)(2,1)}, bf16[256,1920]{1,0:T(8,128)(2,1)}, u32[]{:S(2)}, u32[]{:S(2)}) %collective-permute-start.11) | collective-permute-done | bytes 983072 | tf_op jit(solution)/shard_map/ppermute | solution.py:279
  144.5 6.6 %collective-permute-done.10.refs_5_.refs_1_ = bf16[128,1920]{1,0:T(8,128)(2,1)} collective-permute-done((bf16[128,1920]{1,0:T(8,128)(2,1)}, bf16[128,1920]{1,0:T(8,128)(2,1)}, u32[]{:S(2)}, u32[]{:S(2)}) %collective-permute-start.10) | collective-permute-done | bytes 491552 | tf_op jit(solution)/shard_map/ppermute | solution.py:481
  154.8 5.4 %back_own.1 = (f32[128,1920]{1,0:T(8,128)S(1)}, bf16[128,1920]{1,0:T(8,128)(2,1)S(1)}) custom-call(s32[6]{0:T(128)S(1)} %concatenate.3.refs_0_.s_ref, bf16[8,2,4,16,1024]{4,3,2,1,0:T(8,128)(2,1)S(1)} %bitcast.18, bf16[8,2,4,16,1024]{4,3,2,1,0:T(8,128)(2,1)S(1)} %bitcast.28, bf16[1024,1920]{1,0:T(8,128)(2,1)S(1)} %copy-done.7, ...), custom_call_target="tpu_custom_call" | custom-call | flops 1006632960 | bytes 4915200 | tf_op jit(solution)/shard_map/back_own/pallas_call | solution.py:55
  165.1 9.0 %collective-permute-done.17 = bf16[128,1920]{1,0:T(8,128)(2,1)S(1)} collective-permute-done((bf16[128,1920]{1,0:T(8,128)(2,1)S(1)}, bf16[128,1920]{1,0:T(8,128)(2,1)S(1)}, u32[]{:S(2)}, u32[]{:S(2)}) %collective-permute-start.17) | collective-permute-done | bytes 491552 | tf_op jit(solution)/shard_map/ppermute | solution.py:286
  175.5 10.5 %collective-permute-done.14.refs_2_.refs_4_ = bf16[256,1920]{1,0:T(8,128)(2,1)S(1)} collective-permute-done((bf16[256,1920]{1,0:T(8,128)(2,1)S(1)}, bf16[256,1920]{1,0:T(8,128)(2,1)S(1)}, u32[]{:S(2)}, u32[]{:S(2)}) %collective-permute-start.14) | collective-permute-done | bytes 983072 | tf_op jit(solution)/shard_map/ppermute | solution.py:300
  188.6 3.2 %collective-permute-start.16 = (bf16[128,1920]{1,0:T(8,128)(2,1)}, bf16[128,1920]{1,0:T(8,128)(2,1)S(1)}, u32[]{:S(2)}, u32[]{:S(2)}) collective-permute-start(bf16[128,1920]{1,0:T(8,128)(2,1)} %slice.17), channel_id=1, source_target_pairs={{0,6},{1,7},{2,0},{3,1},{4,2},{5,3},{6,4},{7,5},{8,14},{9,15},{10,... | collective-permute-start | bytes 1474568 | tf_op jit(solution)/shard_map/ppermute | solution.py:295
  192.7 6.8 %all-to-all-start.1 = ((bf16[16,64,1920]{2,1,0:T(8,128)(2,1)}), bf16[16,64,1920]{2,1,0:T(8,128)(2,1)}, u32[]{:S(2)}, u32[]{:S(2)}) async-start(bf16[16,64,1920]{2,1,0:T(8,128)(2,1)} %hold.7.refs_4_), calls=%async_computation.1 | async-start | bytes 7864320 | tf_op jit(solution)/shard_map/all_to_all | solution.py:306
  206.9 3.7 %collective-permute-start.19 = (bf16[256,1920]{1,0:T(8,128)(2,1)S(1)}, bf16[256,1920]{1,0:T(8,128)(2,1)S(1)}, u32[]{:S(2)}, u32[]{:S(2)}) collective-permute-start(bf16[256,1920]{1,0:T(8,128)(2,1)S(1)} %join_grad.1.refs_6_.refs_0_.refs_2_), channel_id=1, source_target_pairs={{0,6},{1,7},{2,0},{3,1},{4,2},{5,3},{6,4},{7,5},{8,14},{9,15},{10,... | collective-permute-start | bytes 2949128 | tf_op jit(solution)/shard_map/ppermute | solution.py:300
  210.6 10.9 %out_rows.1 = (f32[4,128,1024]{2,1,0:T(8,128)}, f32[4,128,1024]{2,1,0:T(8,128)}) custom-call(s32[6]{0:T(128)S(1)} %concatenate.3.refs_0_.s_ref, bf16[256,1920]{1,0:T(8,128)(2,1)S(1)} %join_act.1.refs_0_.refs_2_, bf16[256,1920]{1,0:T(8,128)(2,1)S(1)} %copy-done.24, bf16[256,1920]{1,0:T(8,128)(2,1)S(1)} %copy-done.22, bf16[128,1920]{1,0:T(8,128)(2,1)S(1)} %copy-done.31, ...), custom_call_target="tpu_custom_call" | custom-call | flops 4026531840 | bytes 16252928 | tf_op jit(solution)/shard_map/out_rows/pallas_call | solution.py:55
  221.5 11.8 %down_update.1.refs_1_ = bf16[1024,1920]{1,0:T(8,128)(2,1)} custom-call(s32[6]{0:T(128)} %copy-done.37, bf16[8,2,4,16,1024]{4,3,2,1,0:T(8,128)(2,1)} %bitcast.11, bf16[8,2,4,16,1024]{4,3,2,1,0:T(8,128)(2,1)} %bitcast.21, bf16[256,1920]{1,0:T(8,128)(2,1)} %copy-done.20, bf16[256,1920]{1,0:T(8,128)(2,1)} %copy-done.23, bf16[256,1920]{1,0:T(8,128)(2,1)} %copy-done.21, ...), custom_call_target="tpu_custom_call" | custom-call | flops 4026531840 | bytes 13893632 | tf_op jit(solution)/shard_map/down_update/pallas_call | solution.py:55
  237.1 3.2 %collective-permute-start.26 = (bf16[128,1920]{1,0:T(8,128)(2,1)}, bf16[128,1920]{1,0:T(8,128)(2,1)}, u32[]{:S(2)}, u32[]{:S(2)}) collective-permute-start(bf16[128,1920]{1,0:T(8,128)(2,1)} %hold.10), channel_id=1, source_target_pairs={{0,6},{1,7},{2,0},{3,1},{4,2},{5,3},{6,4},{7,5},{8,14},{9,15},{10,... | collective-permute-start | bytes 1474568 | tf_op jit(solution)/shard_map/ppermute | solution.py:295
  240.4 3.4 %merge_out.1 = (f32[4,32,1024]{2,1,0:T(8,128)}, bf16[4,32,1024]{2,1,0:T(8,128)(2,1)}, bf16[4,32,1024]{2,1,0:T(8,128)(2,1)}, bf16[4,32,1024]{2,1,0:T(8,128)(2,1)}) custom-call(f32[4,128,1024]{2,1,0:T(8,128)} %get-tuple-element.44.refs_0_, f32[4,128,1024]{2,1,0:T(8,128)} %collective-permute-done.21.refs_1_), custom_call_target="tpu_custom_call" | custom-call | bytes 8000000 | tf_op jit(solution)/shard_map/merge_out/pallas_call | solution.py:103
  243.8 4.6 %collective-permute-start.23 = (bf16[4,32,1024]{2,1,0:T(8,128)(2,1)}, bf16[4,32,1024]{2,1,0:T(8,128)(2,1)S(1)}, u32[]{:S(2)}, u32[]{:S(2)}) collective-permute-start(bf16[4,32,1024]{2,1,0:T(8,128)(2,1)} %get-tuple-element.48), channel_id=1, source_target_pairs={{0,32},{8,40},{16,48},{24,56},{32,0},{40,8},{48,16},{56,24},{64,96... | collective-permute-start | bytes 786440 | tf_op jit(solution)/shard_map/ppermute | solution.py:396
  252.8 11.0 %grad_rows.1 = (f32[4,128,1024]{2,1,0:T(8,128)}, f32[4,128,1024]{2,1,0:T(8,128)}) custom-call(s32[6]{0:T(128)S(1)} %copy-done.38, bf16[256,1920]{1,0:T(8,128)(2,1)S(1)} %copy-done.19, bf16[256,1920]{1,0:T(8,128)(2,1)S(1)} %copy-done.15, bf16[256,1920]{1,0:T(8,128)(2,1)} %collective-permute-done.20.refs_2_.refs_3_.refs_4_, ...), custom_call_target="tpu_custom_call" | custom-call | flops 4026531840 | bytes 16252928 | tf_op jit(solution)/shard_map/grad_rows/pallas_call | solution.py:55
  264.8 4.5 %collective-permute-done.27.refs_1_ = f32[4,128,1024]{2,1,0:T(8,128)} collective-permute-done((f32[4,128,1024]{2,1,0:T(8,128)}, f32[4,128,1024]{2,1,0:T(8,128)}, u32[]{:S(2)}, u32[]{:S(2)}) %collective-permute-start.27) | collective-permute-done | bytes 2097184 | tf_op jit(solution)/shard_map/ppermute | solution.py:388
  269.3 3.4 %merge_grad.1 = (f32[4,32,1024]{2,1,0:T(8,128)}, bf16[4,32,1024]{2,1,0:T(8,128)(2,1)}, bf16[4,32,1024]{2,1,0:T(8,128)(2,1)}, bf16[4,32,1024]{2,1,0:T(8,128)(2,1)}) custom-call(f32[4,128,1024]{2,1,0:T(8,128)} %get-tuple-element.50.refs_0_, f32[4,128,1024]{2,1,0:T(8,128)} %collective-permute-done.27.refs_1_), custom_call_target="tpu_custom_call" | custom-call | bytes 8000000 | tf_op jit(solution)/shard_map/merge_grad/pallas_call | solution.py:103
  277.0 3.3 %collective-permute-start.30 = (bf16[4,32,1024]{2,1,0:T(8,128)(2,1)}, bf16[4,32,1024]{2,1,0:T(8,128)(2,1)S(1)}, u32[]{:S(2)}, u32[]{:S(2)}) collective-permute-start(bf16[4,32,1024]{2,1,0:T(8,128)(2,1)} %get-tuple-element.56), channel_id=1, source_target_pairs={{0,32},{8,40},{16,48},{24,56},{32,0},{40,8},{48,16},{56,24},{64,96... | collective-permute-start | bytes 786440 | tf_op jit(solution)/shard_map/ppermute | solution.py:396
  282.9 11.8 %up_update.1.refs_4_ = bf16[1024,1920]{1,0:T(8,128)(2,1)} custom-call(s32[6]{0:T(128)} %copy-done.37, bf16[8,2,4,16,1024]{4,3,2,1,0:T(8,128)(2,1)} %bitcast.12, bf16[8,2,4,16,1024]{4,3,2,1,0:T(8,128)(2,1)} %bitcast.22, bf16[256,1920]{1,0:T(8,128)(2,1)} %copy-done.18, bf16[256,1920]{1,0:T(8,128)(2,1)} %copy-done.13, ...), custom_call_target="tpu_custom_call" | custom-call | flops 4026531840 | bytes 13893632 | tf_op jit(solution)/shard_map/up_update/pallas_call | solution.py:55
  (172 shorter events, 81.3 us)
Async XLA Ops:
  4.6 8.4 %collective-permute-start = (bf16[128,1024]{1,0:T(8,128)(2,1)S(1)}, bf16[128,1024]{1,0:T(8,128)(2,1)S(1)}, u32[]{:S(2)}, u32[]{:S(2)}) collective-permute-start(bf16[128,1024]{1,0:T(8,128)(2,1)S(1)} %pick.1), channel_id=1, source_target_pairs={{0,64},{8,72},{16,80},{24,88},{32,96},{40,104},{48,112},{56,120},{... | collective-permute-start | bytes 786440 | tf_op jit(solution)/shard_map/ppermute | solution.py:412
  13.1 24.6 %collective-permute-start.1 = (bf16[2,128,1024]{2,1,0:T(8,128)(2,1)S(1)}, bf16[2,128,1024]{2,1,0:T(8,128)(2,1)S(1)}, u32[]{:S(2)}, u32[]{:S(2)}) collective-permute-start(bf16[2,128,1024]{2,1,0:T(8,128)(2,1)S(1)} %pad_maximum_fusion.refs_0_), channel_id=1, source_target_pairs={{0,48},{8,56},{16,0},{24,8},{32,16},{40,24},{48,32},{56,40},{64,11... | collective-permute-start | bytes 1572872 | tf_op jit(solution)/shard_map/ppermute | solution.py:414
  15.9 21.8 %collective-permute-start.2 = (bf16[2,128,1024]{2,1,0:T(8,128)(2,1)S(1)}, bf16[2,128,1024]{2,1,0:T(8,128)(2,1)S(1)}, u32[]{:S(2)}, u32[]{:S(2)}) collective-permute-start(bf16[2,128,1024]{2,1,0:T(8,128)(2,1)S(1)} %pad_maximum_fusion.refs_0_), channel_id=1, source_target_pairs={{0,32},{8,40},{16,48},{24,56},{32,0},{40,8},{48,16},{56,24},{64,96... | collective-permute-start | bytes 1572872 | tf_op jit(solution)/shard_map/ppermute | solution.py:414
  16.7 24.6 %collective-permute-start.3 = (bf16[2,128,1024]{2,1,0:T(8,128)(2,1)S(1)}, bf16[2,128,1024]{2,1,0:T(8,128)(2,1)S(1)}, u32[]{:S(2)}, u32[]{:S(2)}) collective-permute-start(bf16[2,128,1024]{2,1,0:T(8,128)(2,1)S(1)} %pad_maximum_fusion.refs_0_), channel_id=1, source_target_pairs={{0,16},{8,24},{16,32},{24,40},{32,48},{40,56},{48,0},{56,8},{64,80... | collective-permute-start | bytes 1572872 | tf_op jit(solution)/shard_map/ppermute | solution.py:414
  54.4 25.3 %collective-permute-start.5 = (bf16[2,128,1920]{2,1,0:T(8,128)(2,1)}, bf16[2,128,1920]{2,1,0:T(8,128)(2,1)S(1)}, u32[]{:S(2)}, u32[]{:S(2)}) collective-permute-start(bf16[2,128,1920]{2,1,0:T(8,128)(2,1)} %get-tuple-element.32.refs_7_), channel_id=1, source_target_pairs={{0,2},{1,3},{2,4},{3,5},{4,6},{5,7},{6,0},{7,1},{8,10},{9,11},{10,... | collective-permute-start | bytes 2949128 | tf_op jit(solution)/shard_map/ppermute | solution.py:271
  56.0 23.8 %collective-permute-start.6 = (bf16[2,128,1920]{2,1,0:T(8,128)(2,1)}, bf16[2,128,1920]{2,1,0:T(8,128)(2,1)}, u32[]{:S(2)}, u32[]{:S(2)}) collective-permute-start(bf16[2,128,1920]{2,1,0:T(8,128)(2,1)} %get-tuple-element.33), channel_id=1, source_target_pairs={{0,6},{1,7},{2,0},{3,1},{4,2},{5,3},{6,4},{7,5},{8,14},{9,15},{10,... | collective-permute-start | bytes 2949128 | tf_op jit(solution)/shard_map/ppermute | solution.py:271
  69.8 66.4 %all-to-all-start = ((bf16[16,64,1920]{2,1,0:T(8,128)(2,1)}), bf16[16,64,1920]{2,1,0:T(8,128)(2,1)}, u32[]{:S(2)}, u32[]{:S(2)}) async-start(bf16[16,64,1920]{2,1,0:T(8,128)(2,1)} %hold.6), calls=%async_computation | async-start | bytes 7864320 | tf_op jit(solution)/shard_map/all_to_all | solution.py:306
  89.7 24.2 %collective-permute-start.7 = (bf16[256,1920]{1,0:T(8,128)(2,1)S(1)}, bf16[256,1920]{1,0:T(8,128)(2,1)S(1)}, u32[]{:S(2)}, u32[]{:S(2)}) collective-permute-start(bf16[256,1920]{1,0:T(8,128)(2,1)S(1)} %get-tuple-element.34.refs_7_), channel_id=1, source_target_pairs={{0,2},{1,3},{2,4},{3,5},{4,6},{5,7},{6,0},{7,1},{8,10},{9,11},{10,... | collective-permute-start | bytes 2949128 | tf_op jit(solution)/shard_map/ppermute | solution.py:279
  91.3 22.5 %collective-permute-start.8 = (bf16[256,1920]{1,0:T(8,128)(2,1)S(1)}, bf16[256,1920]{1,0:T(8,128)(2,1)S(1)}, u32[]{:S(2)}, u32[]{:S(2)}) collective-permute-start(bf16[256,1920]{1,0:T(8,128)(2,1)S(1)} %get-tuple-element.35), channel_id=1, source_target_pairs={{0,6},{1,7},{2,0},{3,1},{4,2},{5,3},{6,4},{7,5},{8,14},{9,15},{10,... | collective-permute-start | bytes 2949128 | tf_op jit(solution)/shard_map/ppermute | solution.py:279
  117.6 16.7 %collective-permute-start.9 = (bf16[128,1920]{1,0:T(8,128)(2,1)S(1)}, bf16[128,1920]{1,0:T(8,128)(2,1)S(1)}, u32[]{:S(2)}, u32[]{:S(2)}) collective-permute-start(bf16[128,1920]{1,0:T(8,128)(2,1)S(1)} %get-tuple-element.38), channel_id=1, source_target_pairs={{0,1},{1,0},{2,3},{3,2},{4,5},{5,4},{6,7},{7,6},{8,9},{9,8},{10,11... | collective-permute-start | bytes 1474568 | tf_op jit(solution)/shard_map/ppermute | solution.py:286
  121.2 23.3 %collective-permute-start.11 = (bf16[256,1920]{1,0:T(8,128)(2,1)}, bf16[256,1920]{1,0:T(8,128)(2,1)}, u32[]{:S(2)}, u32[]{:S(2)}) collective-permute-start(bf16[256,1920]{1,0:T(8,128)(2,1)} %get-tuple-element.36.refs_5_), channel_id=1, source_target_pairs={{0,2},{1,3},{2,4},{3,5},{4,6},{5,7},{6,0},{7,1},{8,10},{9,11},{10,... | collective-permute-start | bytes 2949128 | tf_op jit(solution)/shard_map/ppermute | solution.py:279
  122.3 22.2 %collective-permute-start.12 = (bf16[256,1920]{1,0:T(8,128)(2,1)}, bf16[256,1920]{1,0:T(8,128)(2,1)}, u32[]{:S(2)}, u32[]{:S(2)}) collective-permute-start(bf16[256,1920]{1,0:T(8,128)(2,1)} %get-tuple-element.39), channel_id=1, source_target_pairs={{0,6},{1,7},{2,0},{3,1},{4,2},{5,3},{6,4},{7,5},{8,14},{9,15},{10,... | collective-permute-start | bytes 2949128 | tf_op jit(solution)/shard_map/ppermute | solution.py:279
  136.1 15.0 %collective-permute-start.10 = (bf16[128,1920]{1,0:T(8,128)(2,1)}, bf16[128,1920]{1,0:T(8,128)(2,1)}, u32[]{:S(2)}, u32[]{:S(2)}) collective-permute-start(bf16[128,1920]{1,0:T(8,128)(2,1)} %multiply_convert_fusion.refs_0_), channel_id=1, source_target_pairs={{0,1},{1,0},{2,3},{3,2},{4,5},{5,4},{6,7},{7,6},{8,9},{9,8},{10,11... | collective-permute-start | bytes 1474568 | tf_op jit(solution)/shard_map/ppermute | solution.py:481
  160.2 13.9 %collective-permute-start.17 = (bf16[128,1920]{1,0:T(8,128)(2,1)S(1)}, bf16[128,1920]{1,0:T(8,128)(2,1)S(1)}, u32[]{:S(2)}, u32[]{:S(2)}) collective-permute-start(bf16[128,1920]{1,0:T(8,128)(2,1)S(1)} %get-tuple-element.41.refs_2_), channel_id=1, source_target_pairs={{0,1},{1,0},{2,3},{3,2},{4,5},{5,4},{6,7},{7,6},{8,9},{9,8},{10,11... | collective-permute-start | bytes 1474568 | tf_op jit(solution)/shard_map/ppermute | solution.py:286
  161.8 24.1 %collective-permute-start.14 = (bf16[256,1920]{1,0:T(8,128)(2,1)S(1)}, bf16[256,1920]{1,0:T(8,128)(2,1)S(1)}, u32[]{:S(2)}, u32[]{:S(2)}) collective-permute-start(bf16[256,1920]{1,0:T(8,128)(2,1)S(1)} %join_act.1.refs_0_.refs_2_), channel_id=1, source_target_pairs={{0,2},{1,3},{2,4},{3,5},{4,6},{5,7},{6,0},{7,1},{8,10},{9,11},{10,... | collective-permute-start | bytes 2949128 | tf_op jit(solution)/shard_map/ppermute | solution.py:300
  162.3 24.6 %collective-permute-start.13 = (bf16[256,1920]{1,0:T(8,128)(2,1)S(1)}, bf16[256,1920]{1,0:T(8,128)(2,1)S(1)}, u32[]{:S(2)}, u32[]{:S(2)}) collective-permute-start(bf16[256,1920]{1,0:T(8,128)(2,1)S(1)} %join_act.1.refs_0_.refs_2_), channel_id=1, source_target_pairs={{0,6},{1,7},{2,0},{3,1},{4,2},{5,3},{6,4},{7,5},{8,14},{9,15},{10,... | collective-permute-start | bytes 2949128 | tf_op jit(solution)/shard_map/ppermute | solution.py:300
  174.6 17.2 %collective-permute-start.18 = (bf16[128,1920]{1,0:T(8,128)(2,1)S(1)}, bf16[128,1920]{1,0:T(8,128)(2,1)S(1)}, u32[]{:S(2)}, u32[]{:S(2)}) collective-permute-start(bf16[128,1920]{1,0:T(8,128)(2,1)S(1)} %fusion.5.refs_0_), channel_id=1, source_target_pairs={{0,1},{1,0},{2,3},{3,2},{4,5},{5,4},{6,7},{7,6},{8,9},{9,8},{10,11... | collective-permute-start | bytes 1474568 | tf_op jit(solution)/shard_map/ppermute | solution.py:485
  186.8 12.8 %collective-permute-start.15 = (bf16[128,1920]{1,0:T(8,128)(2,1)}, bf16[128,1920]{1,0:T(8,128)(2,1)S(1)}, u32[]{:S(2)}, u32[]{:S(2)}) collective-permute-start(bf16[128,1920]{1,0:T(8,128)(2,1)} %slice.16), channel_id=1, source_target_pairs={{0,2},{1,3},{2,4},{3,5},{4,6},{5,7},{6,0},{7,1},{8,10},{9,11},{10,... | collective-permute-start | bytes 1474568 | tf_op jit(solution)/shard_map/ppermute | solution.py:295
  188.6 12.2 %collective-permute-start.16 = (bf16[128,1920]{1,0:T(8,128)(2,1)}, bf16[128,1920]{1,0:T(8,128)(2,1)S(1)}, u32[]{:S(2)}, u32[]{:S(2)}) collective-permute-start(bf16[128,1920]{1,0:T(8,128)(2,1)} %slice.17), channel_id=1, source_target_pairs={{0,6},{1,7},{2,0},{3,1},{4,2},{5,3},{6,4},{7,5},{8,14},{9,15},{10,... | collective-permute-start | bytes 1474568 | tf_op jit(solution)/shard_map/ppermute | solution.py:295
  192.7 71.2 %all-to-all-start.1 = ((bf16[16,64,1920]{2,1,0:T(8,128)(2,1)}), bf16[16,64,1920]{2,1,0:T(8,128)(2,1)}, u32[]{:S(2)}, u32[]{:S(2)}) async-start(bf16[16,64,1920]{2,1,0:T(8,128)(2,1)} %hold.7.refs_4_), calls=%async_computation.1 | async-start | bytes 7864320 | tf_op jit(solution)/shard_map/all_to_all | solution.py:306
  206.9 26.4 %collective-permute-start.19 = (bf16[256,1920]{1,0:T(8,128)(2,1)S(1)}, bf16[256,1920]{1,0:T(8,128)(2,1)S(1)}, u32[]{:S(2)}, u32[]{:S(2)}) collective-permute-start(bf16[256,1920]{1,0:T(8,128)(2,1)S(1)} %join_grad.1.refs_6_.refs_0_.refs_2_), channel_id=1, source_target_pairs={{0,6},{1,7},{2,0},{3,1},{4,2},{5,3},{6,4},{7,5},{8,14},{9,15},{10,... | collective-permute-start | bytes 2949128 | tf_op jit(solution)/shard_map/ppermute | solution.py:300
  210.6 22.7 %collective-permute-start.20 = (bf16[256,1920]{1,0:T(8,128)(2,1)S(1)}, bf16[256,1920]{1,0:T(8,128)(2,1)}, u32[]{:S(2)}, u32[]{:S(2)}) collective-permute-start(bf16[256,1920]{1,0:T(8,128)(2,1)S(1)} %join_grad.1.refs_6_.refs_0_.refs_2_), channel_id=1, source_target_pairs={{0,2},{1,3},{2,4},{3,5},{4,6},{5,7},{6,0},{7,1},{8,10},{9,11},{10,... | collective-permute-start | bytes 2949128 | tf_op jit(solution)/shard_map/ppermute | solution.py:300
  234.3 6.0 %collective-permute-start.21 = (f32[4,128,1024]{2,1,0:T(8,128)}, f32[4,128,1024]{2,1,0:T(8,128)}, u32[]{:S(2)}, u32[]{:S(2)}) collective-permute-start(f32[4,128,1024]{2,1,0:T(8,128)} %hold.8), channel_id=1, source_target_pairs={{0,8},{8,0},{16,24},{24,16},{32,40},{40,32},{48,56},{56,48},{64,72... | collective-permute-start | bytes 6291464 | tf_op jit(solution)/shard_map/ppermute | solution.py:388
  236.2 15.3 %collective-permute-start.25 = (bf16[128,1920]{1,0:T(8,128)(2,1)}, bf16[128,1920]{1,0:T(8,128)(2,1)}, u32[]{:S(2)}, u32[]{:S(2)}) collective-permute-start(bf16[128,1920]{1,0:T(8,128)(2,1)} %hold.9), channel_id=1, source_target_pairs={{0,2},{1,3},{2,4},{3,5},{4,6},{5,7},{6,0},{7,1},{8,10},{9,11},{10,... | collective-permute-start | bytes 1474568 | tf_op jit(solution)/shard_map/ppermute | solution.py:295
  237.1 14.6 %collective-permute-start.26 = (bf16[128,1920]{1,0:T(8,128)(2,1)}, bf16[128,1920]{1,0:T(8,128)(2,1)}, u32[]{:S(2)}, u32[]{:S(2)}) collective-permute-start(bf16[128,1920]{1,0:T(8,128)(2,1)} %hold.10), channel_id=1, source_target_pairs={{0,6},{1,7},{2,0},{3,1},{4,2},{5,3},{6,4},{7,5},{8,14},{9,15},{10,... | collective-permute-start | bytes 1474568 | tf_op jit(solution)/shard_map/ppermute | solution.py:295
  243.8 20.1 %collective-permute-start.22 = (bf16[4,32,1024]{2,1,0:T(8,128)(2,1)}, bf16[4,32,1024]{2,1,0:T(8,128)(2,1)S(1)}, u32[]{:S(2)}, u32[]{:S(2)}) collective-permute-start(bf16[4,32,1024]{2,1,0:T(8,128)(2,1)} %get-tuple-element.47), channel_id=1, source_target_pairs={{0,16},{8,24},{16,32},{24,40},{32,48},{40,56},{48,0},{56,8},{64,80... | collective-permute-start | bytes 786440 | tf_op jit(solution)/shard_map/ppermute | solution.py:396
  243.8 20.1 %collective-permute-start.23 = (bf16[4,32,1024]{2,1,0:T(8,128)(2,1)}, bf16[4,32,1024]{2,1,0:T(8,128)(2,1)S(1)}, u32[]{:S(2)}, u32[]{:S(2)}) collective-permute-start(bf16[4,32,1024]{2,1,0:T(8,128)(2,1)} %get-tuple-element.48), channel_id=1, source_target_pairs={{0,32},{8,40},{16,48},{24,56},{32,0},{40,8},{48,16},{56,24},{64,96... | collective-permute-start | bytes 786440 | tf_op jit(solution)/shard_map/ppermute | solution.py:396
  248.3 15.6 %collective-permute-start.24 = (bf16[4,32,1024]{2,1,0:T(8,128)(2,1)}, bf16[4,32,1024]{2,1,0:T(8,128)(2,1)S(1)}, u32[]{:S(2)}, u32[]{:S(2)}) collective-permute-start(bf16[4,32,1024]{2,1,0:T(8,128)(2,1)} %get-tuple-element.49), channel_id=1, source_target_pairs={{0,48},{8,56},{16,0},{24,8},{32,16},{40,24},{48,32},{56,40},{64,11... | collective-permute-start | bytes 786440 | tf_op jit(solution)/shard_map/ppermute | solution.py:396
  274.7 24.7 %collective-permute-start.28 = (bf16[4,16,1024]{2,1,0:T(8,128)(2,1)}, bf16[4,16,1024]{2,1,0:T(8,128)(2,1)S(1)}, u32[]{:S(2)}, u32[]{:S(2)}) collective-permute-start(bf16[4,16,1024]{2,1,0:T(8,128)(2,1)} %get-tuple-element.54.refs_9_), channel_id=1, source_target_pairs={{0,64},{8,72},{16,80},{24,88},{32,96},{40,104},{48,112},{56,120},{... | collective-permute-start | bytes 393224 | tf_op jit(solution)/shard_map/ppermute | solution.py:406
  275.7 19.0 %collective-permute-start.29 = (bf16[4,32,1024]{2,1,0:T(8,128)(2,1)}, bf16[4,32,1024]{2,1,0:T(8,128)(2,1)S(1)}, u32[]{:S(2)}, u32[]{:S(2)}) collective-permute-start(bf16[4,32,1024]{2,1,0:T(8,128)(2,1)} %get-tuple-element.55), channel_id=1, source_target_pairs={{0,16},{8,24},{16,32},{24,40},{32,48},{40,56},{48,0},{56,8},{64,80... | collective-permute-start | bytes 786440 | tf_op jit(solution)/shard_map/ppermute | solution.py:396
  277.0 17.7 %collective-permute-start.30 = (bf16[4,32,1024]{2,1,0:T(8,128)(2,1)}, bf16[4,32,1024]{2,1,0:T(8,128)(2,1)S(1)}, u32[]{:S(2)}, u32[]{:S(2)}) collective-permute-start(bf16[4,32,1024]{2,1,0:T(8,128)(2,1)} %get-tuple-element.56), channel_id=1, source_target_pairs={{0,32},{8,40},{16,48},{24,56},{32,0},{40,8},{48,16},{56,24},{64,96... | collective-permute-start | bytes 786440 | tf_op jit(solution)/shard_map/ppermute | solution.py:396
  280.3 14.5 %collective-permute-start.31 = (bf16[4,32,1024]{2,1,0:T(8,128)(2,1)}, bf16[4,32,1024]{2,1,0:T(8,128)(2,1)S(1)}, u32[]{:S(2)}, u32[]{:S(2)}) collective-permute-start(bf16[4,32,1024]{2,1,0:T(8,128)(2,1)} %get-tuple-element.57), channel_id=1, source_target_pairs={{0,48},{8,56},{16,0},{24,8},{32,16},{40,24},{48,32},{56,40},{64,11... | collective-permute-start | bytes 786440 | tf_op jit(solution)/shard_map/ppermute | solution.py:396
  (53 other events, 526.9 us)

commit v5 on v4

--- a/solution.py
+++ b/solution.py
@@ -47,7 +47,7 @@
     n, m = len(ins), len(after)
 
     def spec(block, index):
-        return pl.BlockSpec(memory_space=pltpu.HBM) if block is None else pl.BlockSpec(block, index)
+        return HBM if block is None else pl.BlockSpec(block, index)
 
     def run(s_ref, *refs):
         kernel(s_ref, *refs[:n], *refs[n + m :])
@@ -347,7 +347,7 @@
         [(a, None, None) for a in pieces] + [(w, (DB, width), lambda j, s: (j, 0))],
         [out(), out()],
         [pltpu.VMEM((groups, 2, half, width), BF16), pltpu.SemaphoreType.DMA((2 * groups,))],
-        50,
+        62,
         (4 * groups * half * depth * width, 2 * depth * width + 4 * groups * half * (width + 4 * depth)),
         name,
         after,

time: 308 us -> 305 us (level)
  local copies, waits for them, and re-layouts: 37 us -> 30.2 us
  waiting for transfers between devices: 106 us -> 112 us
    unnamed x100 -> x78, local copies, waits for them, and re-layouts: 31.8 us -> 24.7 us
    ppermute x6, waiting for transfers between devices: 0.02 us -> 4.74 us  [x_exchange(): lax.ppermute(block, WIDE, X_SHIFT[d])]
where the time goes in v5:
time: 305 us; the launch traced here: 303 us
  waiting for transfers between devices  112 us (37%)
  Pallas kernels  96.9 us (32%)
  starting transfers between devices  61.9 us (20%)
  local copies, waits for them, and re-layouts  30.2 us (10%)
    pallas_call x9, Pallas kernels, call(): pl.pallas_call(run, out_shape=[shape for shape, _, _ in outs], grid_spec=...  72.3 us
    unnamed x78, local copies, waits for them, and re-layouts  24.7 us
    ppermute x3, waiting for transfers between devices, wide_gather(): lax.ppermute(pair, WIDE, X_SHIFT[(4 - d) % 4])  23.8 us
    ppermute x2, waiting for transfers between devices, near_sum(): lax.ppermute(right, NARROW, Y_RIGHT)  22.8 us
    ppermute x2, waiting for transfers between devices, own_sum(): return (keep, lax.ppermute(send, NARROW, ZHI_SWAP), send)  18.8 us
    pallas_call x10, Pallas kernels, simple_call(): pl.pallas_call(run, out_shape=outs, in_specs=[spec(a) for a in ins] + [HB...  16.5 us
    ppermute x6, starting transfers between devices, x_exchange(): lax.ppermute(block, WIDE, X_SHIFT[d])  13.7 us
    all_to_all x2, starting transfers between devices, exchange(): return lax.all_to_all(blocks, WIDE, 0, 0, tiled=True)  11.5 us
  transfers between devices with their start and end apart: 35, of which 18 were waited for; matrix products, arithmetic and copies ran while one was open for 2% of the time, Pallas kernels for 26%

profile of v5, /device:TPU:0, one launch (start us, length us, event | category | flops | bytes accessed | tf_op | source)
XLA Modules:
  0.0 303.3 jit_solution(14502184867926624565)
XLA Ops:
  6.7 6.3 %collective-permute-done = bf16[128,1024]{1,0:T(8,128)(2,1)S(1)} collective-permute-done((bf16[128,1024]{1,0:T(8,128)(2,1)S(1)}, bf16[128,1024]{1,0:T(8,128)(2,1)S(1)}, u32[]{:S(2)}, u32[]{:S(2)}) %collective-permute-start) | collective-permute-done | bytes 262176 | tf_op jit(solution)/shard_map/ppermute | solution.py:412
  17.6 20.1 %collective-permute-done.1.refs_1_ = bf16[2,128,1024]{2,1,0:T(8,128)(2,1)S(1)} collective-permute-done((bf16[2,128,1024]{2,1,0:T(8,128)(2,1)S(1)}, bf16[2,128,1024]{2,1,0:T(8,128)(2,1)S(1)}, u32[]{:S(2)}, u32[]{:S(2)}) %collective-permute-start.1) | collective-permute-done | bytes 524320 | tf_op jit(solution)/shard_map/ppermute | solution.py:414
  37.7 3.7 %collective-permute-done.3.refs_3_ = bf16[2,128,1024]{2,1,0:T(8,128)(2,1)S(1)} collective-permute-done((bf16[2,128,1024]{2,1,0:T(8,128)(2,1)S(1)}, bf16[2,128,1024]{2,1,0:T(8,128)(2,1)S(1)}, u32[]{:S(2)}, u32[]{:S(2)}) %collective-permute-start.3) | collective-permute-done | bytes 524320 | tf_op jit(solution)/shard_map/ppermute | solution.py:414
  41.6 4.1 %collective-permute-done.4 = bf16[8,128,1024]{2,1,0:T(8,128)(2,1)S(1)} collective-permute-done((bf16[8,128,1024]{2,1,0:T(8,128)(2,1)S(1)}, bf16[8,128,1024]{2,1,0:T(8,128)(2,1)S(1)}, u32[]{:S(2)}, u32[]{:S(2)}) %collective-permute-start.4) | collective-permute-done | bytes 2097184 | tf_op jit(solution)/shard_map/ppermute | solution.py:416
  48.6 5.9 %far.1 = (bf16[2,128,1920]{2,1,0:T(8,128)(2,1)}, bf16[2,128,1920]{2,1,0:T(8,128)(2,1)}) custom-call(s32[6]{0:T(128)S(1)} %concatenate.3.refs_0_.s_ref, bf16[8,2,4,16,1024]{4,3,2,1,0:T(8,128)(2,1)S(1)} %bitcast.9, bf16[8,2,4,16,1024]{4,3,2,1,0:T(8,128)(2,1)S(1)} %bitcast.19, bf16[8,2,4,16,1024]{4,3,2,1,0:T(8,128)(2,1)S(1)} %bitcast.10, ...), custom_call_target="tpu_custom_call" | custom-call | flops 2013265920 | bytes 5898240 | tf_op jit(solution)/shard_map/far/pallas_call | solution.py:55
  57.7 8.1 %relay.1 = (bf16[16,64,1920]{2,1,0:T(8,128)(2,1)S(1)}, bf16[16,64,1920]{2,1,0:T(8,128)(2,1)S(1)}) custom-call(s32[6]{0:T(128)S(1)} %concatenate.3.refs_0_.s_ref, bf16[1,1,1966592]{2,1,0:T(2,128)(2,1)S(1)} %copy-done.14, bf16[1,1,1966592]{2,1,0:T(2,128)(2,1)} %down_ref.1, bf16[2,128,1024]{2,1,0:T(8,128)(2,1)S(1)} %pad_maximum_fusion.refs_0_), custom_call_target="tpu_custom_call" | custom-call | bytes 32000000 | tf_op jit(solution)/shard_map/relay/pallas_call | solution.py:187
  69.8 4.7 %all-to-all-start = ((bf16[16,64,1920]{2,1,0:T(8,128)(2,1)}), bf16[16,64,1920]{2,1,0:T(8,128)(2,1)}, u32[]{:S(2)}, u32[]{:S(2)}) async-start(bf16[16,64,1920]{2,1,0:T(8,128)(2,1)} %hold.6), calls=%async_computation | async-start | bytes 7864320 | tf_op jit(solution)/shard_map/all_to_all | solution.py:306
  74.4 5.4 %collective-permute-done.5.refs_5_ = bf16[2,128,1920]{2,1,0:T(8,128)(2,1)S(1)} collective-permute-done((bf16[2,128,1920]{2,1,0:T(8,128)(2,1)}, bf16[2,128,1920]{2,1,0:T(8,128)(2,1)S(1)}, u32[]{:S(2)}, u32[]{:S(2)}) %collective-permute-start.5) | collective-permute-done | bytes 983072 | tf_op jit(solution)/shard_map/ppermute | solution.py:271
  83.6 6.1 %hidden_near.1 = (bf16[256,1920]{1,0:T(8,128)(2,1)S(1)}, bf16[256,1920]{1,0:T(8,128)(2,1)S(1)}) custom-call(s32[6]{0:T(128)S(1)} %concatenate.3.refs_0_.s_ref, bf16[8,2,4,16,1024]{4,3,2,1,0:T(8,128)(2,1)S(1)} %bitcast.13, bf16[8,2,4,16,1024]{4,3,2,1,0:T(8,128)(2,1)S(1)} %bitcast.23, bf16[8,2,4,16,1024]{4,3,2,1,0:T(8,128)(2,1)S(1)} %bitcast.14, ...), custom_call_target="tpu_custom_call" | custom-call | flops 2013265920 | bytes 5898240 | tf_op jit(solution)/shard_map/hidden_near/pallas_call | solution.py:55
  93.0 6.4 %back_near.1 = (bf16[256,1920]{1,0:T(8,128)(2,1)}, bf16[256,1920]{1,0:T(8,128)(2,1)}) custom-call(s32[6]{0:T(128)S(1)} %concatenate.3.refs_0_.s_ref, bf16[8,2,4,16,1024]{4,3,2,1,0:T(8,128)(2,1)S(1)} %bitcast.15, bf16[8,2,4,16,1024]{4,3,2,1,0:T(8,128)(2,1)S(1)} %bitcast.25, bf16[8,2,4,16,1024]{4,3,2,1,0:T(8,128)(2,1)S(1)} %bitcast.16, ...), custom_call_target="tpu_custom_call" | custom-call | flops 2013265920 | bytes 5898240 | tf_op jit(solution)/shard_map/back_near/pallas_call | solution.py:55
  99.5 14.4 %collective-permute-done.7.refs_3_ = bf16[256,1920]{1,0:T(8,128)(2,1)S(1)} collective-permute-done((bf16[256,1920]{1,0:T(8,128)(2,1)S(1)}, bf16[256,1920]{1,0:T(8,128)(2,1)S(1)}, u32[]{:S(2)}, u32[]{:S(2)}) %collective-permute-start.7) | collective-permute-done | bytes 983072 | tf_op jit(solution)/shard_map/ppermute | solution.py:279
  113.9 3.7 %hidden_own.1 = (f32[128,1920]{1,0:T(8,128)S(1)}, bf16[128,1920]{1,0:T(8,128)(2,1)S(1)}) custom-call(s32[6]{0:T(128)S(1)} %concatenate.3.refs_0_.s_ref, bf16[8,2,4,16,1024]{4,3,2,1,0:T(8,128)(2,1)S(1)} %bitcast.17, bf16[8,2,4,16,1024]{4,3,2,1,0:T(8,128)(2,1)S(1)} %bitcast.27, bf16[1024,1920]{1,0:T(8,128)(2,1)S(1)} %copy-done.12, ...), custom_call_target="tpu_custom_call" | custom-call | flops 1006632960 | bytes 4915200 | tf_op jit(solution)/shard_map/hidden_own/pallas_call | solution.py:55
  117.6 3.6 %collective-permute-start.9 = (bf16[128,1920]{1,0:T(8,128)(2,1)S(1)}, bf16[128,1920]{1,0:T(8,128)(2,1)S(1)}, u32[]{:S(2)}, u32[]{:S(2)}) collective-permute-start(bf16[128,1920]{1,0:T(8,128)(2,1)S(1)} %get-tuple-element.38), channel_id=1, source_target_pairs={{0,1},{1,0},{2,3},{3,2},{4,5},{5,4},{6,7},{7,6},{8,9},{9,8},{10,11... | collective-permute-start | bytes 1474568 | tf_op jit(solution)/shard_map/ppermute | solution.py:286
  124.5 9.8 %collective-permute-done.9 = bf16[128,1920]{1,0:T(8,128)(2,1)S(1)} collective-permute-done((bf16[128,1920]{1,0:T(8,128)(2,1)S(1)}, bf16[128,1920]{1,0:T(8,128)(2,1)S(1)}, u32[]{:S(2)}, u32[]{:S(2)}) %collective-permute-start.9) | collective-permute-done | bytes 491552 | tf_op jit(solution)/shard_map/ppermute | solution.py:286
  136.1 8.4 %collective-permute-done.11.refs_3_ = bf16[256,1920]{1,0:T(8,128)(2,1)} collective-permute-done((bf16[256,1920]{1,0:T(8,128)(2,1)}, bf16[256,1920]{1,0:T(8,128)(2,1)}, u32[]{:S(2)}, u32[]{:S(2)}) %collective-permute-start.11) | collective-permute-done | bytes 983072 | tf_op jit(solution)/shard_map/ppermute | solution.py:279
  144.6 6.5 %collective-permute-done.10.refs_5_.refs_1_ = bf16[128,1920]{1,0:T(8,128)(2,1)} collective-permute-done((bf16[128,1920]{1,0:T(8,128)(2,1)}, bf16[128,1920]{1,0:T(8,128)(2,1)}, u32[]{:S(2)}, u32[]{:S(2)}) %collective-permute-start.10) | collective-permute-done | bytes 491552 | tf_op jit(solution)/shard_map/ppermute | solution.py:481
  154.8 5.4 %back_own.1 = (f32[128,1920]{1,0:T(8,128)S(1)}, bf16[128,1920]{1,0:T(8,128)(2,1)S(1)}) custom-call(s32[6]{0:T(128)S(1)} %concatenate.3.refs_0_.s_ref, bf16[8,2,4,16,1024]{4,3,2,1,0:T(8,128)(2,1)S(1)} %bitcast.18, bf16[8,2,4,16,1024]{4,3,2,1,0:T(8,128)(2,1)S(1)} %bitcast.28, bf16[1024,1920]{1,0:T(8,128)(2,1)S(1)} %copy-done.7, ...), custom_call_target="tpu_custom_call" | custom-call | flops 1006632960 | bytes 4915200 | tf_op jit(solution)/shard_map/back_own/pallas_call | solution.py:55
  165.1 9.0 %collective-permute-done.17 = bf16[128,1920]{1,0:T(8,128)(2,1)S(1)} collective-permute-done((bf16[128,1920]{1,0:T(8,128)(2,1)S(1)}, bf16[128,1920]{1,0:T(8,128)(2,1)S(1)}, u32[]{:S(2)}, u32[]{:S(2)}) %collective-permute-start.17) | collective-permute-done | bytes 491552 | tf_op jit(solution)/shard_map/ppermute | solution.py:286
  175.4 10.5 %collective-permute-done.14.refs_2_.refs_4_ = bf16[256,1920]{1,0:T(8,128)(2,1)S(1)} collective-permute-done((bf16[256,1920]{1,0:T(8,128)(2,1)S(1)}, bf16[256,1920]{1,0:T(8,128)(2,1)S(1)}, u32[]{:S(2)}, u32[]{:S(2)}) %collective-permute-start.14) | collective-permute-done | bytes 983072 | tf_op jit(solution)/shard_map/ppermute | solution.py:300
  187.0 3.1 %collective-permute-start.16 = (bf16[128,1920]{1,0:T(8,128)(2,1)}, bf16[128,1920]{1,0:T(8,128)(2,1)S(1)}, u32[]{:S(2)}, u32[]{:S(2)}) collective-permute-start(bf16[128,1920]{1,0:T(8,128)(2,1)} %slice.17), channel_id=1, source_target_pairs={{0,6},{1,7},{2,0},{3,1},{4,2},{5,3},{6,4},{7,5},{8,14},{9,15},{10,... | collective-permute-start | bytes 1474568 | tf_op jit(solution)/shard_map/ppermute | solution.py:295
  190.9 6.8 %all-to-all-start.1 = ((bf16[16,64,1920]{2,1,0:T(8,128)(2,1)}), bf16[16,64,1920]{2,1,0:T(8,128)(2,1)}, u32[]{:S(2)}, u32[]{:S(2)}) async-start(bf16[16,64,1920]{2,1,0:T(8,128)(2,1)} %hold.7.refs_4_), calls=%async_computation.1 | async-start | bytes 7864320 | tf_op jit(solution)/shard_map/all_to_all | solution.py:306
  201.3 3.7 %collective-permute-start.19 = (bf16[256,1920]{1,0:T(8,128)(2,1)S(1)}, bf16[256,1920]{1,0:T(8,128)(2,1)}, u32[]{:S(2)}, u32[]{:S(2)}) collective-permute-start(bf16[256,1920]{1,0:T(8,128)(2,1)S(1)} %join_grad.1.refs_6_.refs_0_.refs_2_), channel_id=1, source_target_pairs={{0,6},{1,7},{2,0},{3,1},{4,2},{5,3},{6,4},{7,5},{8,14},{9,15},{10,... | collective-permute-start | bytes 2949128 | tf_op jit(solution)/shard_map/ppermute | solution.py:300
  204.9 10.6 %out_rows.1 = (f32[4,128,1024]{2,1,0:T(8,128)}, f32[4,128,1024]{2,1,0:T(8,128)}) custom-call(s32[6]{0:T(128)} %copy-done.23, bf16[256,1920]{1,0:T(8,128)(2,1)} %copy-done.16, bf16[256,1920]{1,0:T(8,128)(2,1)} %copy-done.26, bf16[256,1920]{1,0:T(8,128)(2,1)} %copy-done.25, bf16[128,1920]{1,0:T(8,128)(2,1)} %copy-done.19, bf16[128,1920]{1,0:T(8,128)(2,1)} %copy-done.20, ...), custom_call_target="tpu_custom_call" | custom-call | flops 4026531840 | bytes 16252928 | tf_op jit(solution)/shard_map/out_rows/pallas_call | solution.py:55
  215.5 11.8 %down_update.1.refs_1_ = bf16[1024,1920]{1,0:T(8,128)(2,1)} custom-call(s32[6]{0:T(128)} %copy-done.23, bf16[8,2,4,16,1024]{4,3,2,1,0:T(8,128)(2,1)} %bitcast.11, bf16[8,2,4,16,1024]{4,3,2,1,0:T(8,128)(2,1)} %bitcast.21, bf16[256,1920]{1,0:T(8,128)(2,1)} %copy-done.16, bf16[256,1920]{1,0:T(8,128)(2,1)} %copy-done.26, bf16[256,1920]{1,0:T(8,128)(2,1)} %copy-done.25, ...), custom_call_target="tpu_custom_call" | custom-call | flops 4026531840 | bytes 13893632 | tf_op jit(solution)/shard_map/down_update/pallas_call | solution.py:55
  231.2 3.2 %collective-permute-start.26 = (bf16[128,1920]{1,0:T(8,128)(2,1)}, bf16[128,1920]{1,0:T(8,128)(2,1)S(1)}, u32[]{:S(2)}, u32[]{:S(2)}) collective-permute-start(bf16[128,1920]{1,0:T(8,128)(2,1)} %hold.10), channel_id=1, source_target_pairs={{0,6},{1,7},{2,0},{3,1},{4,2},{5,3},{6,4},{7,5},{8,14},{9,15},{10,... | collective-permute-start | bytes 1474568 | tf_op jit(solution)/shard_map/ppermute | solution.py:295
  234.4 3.4 %merge_out.1 = (f32[4,32,1024]{2,1,0:T(8,128)}, bf16[4,32,1024]{2,1,0:T(8,128)(2,1)}, bf16[4,32,1024]{2,1,0:T(8,128)(2,1)}, bf16[4,32,1024]{2,1,0:T(8,128)(2,1)}) custom-call(f32[4,128,1024]{2,1,0:T(8,128)} %get-tuple-element.44.refs_0_, f32[4,128,1024]{2,1,0:T(8,128)} %collective-permute-done.21.refs_1_), custom_call_target="tpu_custom_call" | custom-call | bytes 8000000 | tf_op jit(solution)/shard_map/merge_out/pallas_call | solution.py:103
  237.8 4.6 %collective-permute-start.23 = (bf16[4,32,1024]{2,1,0:T(8,128)(2,1)}, bf16[4,32,1024]{2,1,0:T(8,128)(2,1)S(1)}, u32[]{:S(2)}, u32[]{:S(2)}) collective-permute-start(bf16[4,32,1024]{2,1,0:T(8,128)(2,1)} %get-tuple-element.48), channel_id=1, source_target_pairs={{0,32},{8,40},{16,48},{24,56},{32,0},{40,8},{48,16},{56,24},{64,96... | collective-permute-start | bytes 786440 | tf_op jit(solution)/shard_map/ppermute | solution.py:396
  246.6 10.6 %grad_rows.1 = (f32[4,128,1024]{2,1,0:T(8,128)}, f32[4,128,1024]{2,1,0:T(8,128)}) custom-call(s32[6]{0:T(128)} %copy-done.23, bf16[256,1920]{1,0:T(8,128)(2,1)} %copy-done.15, bf16[256,1920]{1,0:T(8,128)(2,1)} %collective-permute-done.19.refs_1_.refs_2_.refs_3_, bf16[256,1920]{1,0:T(8,128)(2,1)} %collective-permute-done.20.refs_2_.refs_3_.refs_4_, ...), custom_call_target="tpu_custom_call" | custom-call | flops 4026531840 | bytes 16252928 | tf_op jit(solution)/shard_map/grad_rows/pallas_call | solution.py:55
  257.3 4.7 %collective-permute-done.23.refs_2_ = bf16[4,32,1024]{2,1,0:T(8,128)(2,1)S(1)} collective-permute-done((bf16[4,32,1024]{2,1,0:T(8,128)(2,1)}, bf16[4,32,1024]{2,1,0:T(8,128)(2,1)S(1)}, u32[]{:S(2)}, u32[]{:S(2)}) %collective-permute-start.23) | collective-permute-done | bytes 262176 | tf_op jit(solution)/shard_map/ppermute | solution.py:396
  262.8 4.5 %collective-permute-done.27.refs_1_ = f32[4,128,1024]{2,1,0:T(8,128)} collective-permute-done((f32[4,128,1024]{2,1,0:T(8,128)}, f32[4,128,1024]{2,1,0:T(8,128)}, u32[]{:S(2)}, u32[]{:S(2)}) %collective-permute-start.27) | collective-permute-done | bytes 2097184 | tf_op jit(solution)/shard_map/ppermute | solution.py:388
  267.3 3.4 %merge_grad.1 = (f32[4,32,1024]{2,1,0:T(8,128)}, bf16[4,32,1024]{2,1,0:T(8,128)(2,1)}, bf16[4,32,1024]{2,1,0:T(8,128)(2,1)}, bf16[4,32,1024]{2,1,0:T(8,128)(2,1)}) custom-call(f32[4,128,1024]{2,1,0:T(8,128)} %get-tuple-element.50.refs_0_, f32[4,128,1024]{2,1,0:T(8,128)} %collective-permute-done.27.refs_1_), custom_call_target="tpu_custom_call" | custom-call | bytes 8000000 | tf_op jit(solution)/shard_map/merge_grad/pallas_call | solution.py:103
  280.4 11.8 %up_update.1.refs_4_ = bf16[1024,1920]{1,0:T(8,128)(2,1)} custom-call(s32[6]{0:T(128)} %copy-done.23, bf16[8,2,4,16,1024]{4,3,2,1,0:T(8,128)(2,1)} %bitcast.12, bf16[8,2,4,16,1024]{4,3,2,1,0:T(8,128)(2,1)} %bitcast.22, bf16[256,1920]{1,0:T(8,128)(2,1)} %copy-done.15, bf16[256,1920]{1,0:T(8,128)(2,1)} %collective-permute-done.19.refs_1_.refs_2_.refs_3_, ...), custom_call_target="tpu_custom_call" | custom-call | flops 4026531840 | bytes 13893632 | tf_op jit(solution)/shard_map/up_update/pallas_call | solution.py:55
  (150 shorter events, 78.2 us)
Async XLA Ops:
  4.6 8.4 %collective-permute-start = (bf16[128,1024]{1,0:T(8,128)(2,1)S(1)}, bf16[128,1024]{1,0:T(8,128)(2,1)S(1)}, u32[]{:S(2)}, u32[]{:S(2)}) collective-permute-start(bf16[128,1024]{1,0:T(8,128)(2,1)S(1)} %pick.1), channel_id=1, source_target_pairs={{0,64},{8,72},{16,80},{24,88},{32,96},{40,104},{48,112},{56,120},{... | collective-permute-start | bytes 786440 | tf_op jit(solution)/shard_map/ppermute | solution.py:412
  13.1 24.6 %collective-permute-start.1 = (bf16[2,128,1024]{2,1,0:T(8,128)(2,1)S(1)}, bf16[2,128,1024]{2,1,0:T(8,128)(2,1)S(1)}, u32[]{:S(2)}, u32[]{:S(2)}) collective-permute-start(bf16[2,128,1024]{2,1,0:T(8,128)(2,1)S(1)} %pad_maximum_fusion.refs_0_), channel_id=1, source_target_pairs={{0,48},{8,56},{16,0},{24,8},{32,16},{40,24},{48,32},{56,40},{64,11... | collective-permute-start | bytes 1572872 | tf_op jit(solution)/shard_map/ppermute | solution.py:414
  15.9 21.8 %collective-permute-start.2 = (bf16[2,128,1024]{2,1,0:T(8,128)(2,1)S(1)}, bf16[2,128,1024]{2,1,0:T(8,128)(2,1)S(1)}, u32[]{:S(2)}, u32[]{:S(2)}) collective-permute-start(bf16[2,128,1024]{2,1,0:T(8,128)(2,1)S(1)} %pad_maximum_fusion.refs_0_), channel_id=1, source_target_pairs={{0,32},{8,40},{16,48},{24,56},{32,0},{40,8},{48,16},{56,24},{64,96... | collective-permute-start | bytes 1572872 | tf_op jit(solution)/shard_map/ppermute | solution.py:414
  16.7 24.6 %collective-permute-start.3 = (bf16[2,128,1024]{2,1,0:T(8,128)(2,1)S(1)}, bf16[2,128,1024]{2,1,0:T(8,128)(2,1)S(1)}, u32[]{:S(2)}, u32[]{:S(2)}) collective-permute-start(bf16[2,128,1024]{2,1,0:T(8,128)(2,1)S(1)} %pad_maximum_fusion.refs_0_), channel_id=1, source_target_pairs={{0,16},{8,24},{16,32},{24,40},{32,48},{40,56},{48,0},{56,8},{64,80... | collective-permute-start | bytes 1572872 | tf_op jit(solution)/shard_map/ppermute | solution.py:414
  54.5 25.3 %collective-permute-start.5 = (bf16[2,128,1920]{2,1,0:T(8,128)(2,1)}, bf16[2,128,1920]{2,1,0:T(8,128)(2,1)S(1)}, u32[]{:S(2)}, u32[]{:S(2)}) collective-permute-start(bf16[2,128,1920]{2,1,0:T(8,128)(2,1)} %get-tuple-element.32.refs_7_), channel_id=1, source_target_pairs={{0,2},{1,3},{2,4},{3,5},{4,6},{5,7},{6,0},{7,1},{8,10},{9,11},{10,... | collective-permute-start | bytes 2949128 | tf_op jit(solution)/shard_map/ppermute | solution.py:271
  56.1 23.8 %collective-permute-start.6 = (bf16[2,128,1920]{2,1,0:T(8,128)(2,1)}, bf16[2,128,1920]{2,1,0:T(8,128)(2,1)}, u32[]{:S(2)}, u32[]{:S(2)}) collective-permute-start(bf16[2,128,1920]{2,1,0:T(8,128)(2,1)} %get-tuple-element.33), channel_id=1, source_target_pairs={{0,6},{1,7},{2,0},{3,1},{4,2},{5,3},{6,4},{7,5},{8,14},{9,15},{10,... | collective-permute-start | bytes 2949128 | tf_op jit(solution)/shard_map/ppermute | solution.py:271
  69.8 66.4 %all-to-all-start = ((bf16[16,64,1920]{2,1,0:T(8,128)(2,1)}), bf16[16,64,1920]{2,1,0:T(8,128)(2,1)}, u32[]{:S(2)}, u32[]{:S(2)}) async-start(bf16[16,64,1920]{2,1,0:T(8,128)(2,1)} %hold.6), calls=%async_computation | async-start | bytes 7864320 | tf_op jit(solution)/shard_map/all_to_all | solution.py:306
  89.7 24.2 %collective-permute-start.7 = (bf16[256,1920]{1,0:T(8,128)(2,1)S(1)}, bf16[256,1920]{1,0:T(8,128)(2,1)S(1)}, u32[]{:S(2)}, u32[]{:S(2)}) collective-permute-start(bf16[256,1920]{1,0:T(8,128)(2,1)S(1)} %get-tuple-element.34.refs_7_), channel_id=1, source_target_pairs={{0,2},{1,3},{2,4},{3,5},{4,6},{5,7},{6,0},{7,1},{8,10},{9,11},{10,... | collective-permute-start | bytes 2949128 | tf_op jit(solution)/shard_map/ppermute | solution.py:279
  91.4 22.5 %collective-permute-start.8 = (bf16[256,1920]{1,0:T(8,128)(2,1)S(1)}, bf16[256,1920]{1,0:T(8,128)(2,1)S(1)}, u32[]{:S(2)}, u32[]{:S(2)}) collective-permute-start(bf16[256,1920]{1,0:T(8,128)(2,1)S(1)} %get-tuple-element.35), channel_id=1, source_target_pairs={{0,6},{1,7},{2,0},{3,1},{4,2},{5,3},{6,4},{7,5},{8,14},{9,15},{10,... | collective-permute-start | bytes 2949128 | tf_op jit(solution)/shard_map/ppermute | solution.py:279
  117.6 16.6 %collective-permute-start.9 = (bf16[128,1920]{1,0:T(8,128)(2,1)S(1)}, bf16[128,1920]{1,0:T(8,128)(2,1)S(1)}, u32[]{:S(2)}, u32[]{:S(2)}) collective-permute-start(bf16[128,1920]{1,0:T(8,128)(2,1)S(1)} %get-tuple-element.38), channel_id=1, source_target_pairs={{0,1},{1,0},{2,3},{3,2},{4,5},{5,4},{6,7},{7,6},{8,9},{9,8},{10,11... | collective-permute-start | bytes 1474568 | tf_op jit(solution)/shard_map/ppermute | solution.py:286
  121.2 23.3 %collective-permute-start.11 = (bf16[256,1920]{1,0:T(8,128)(2,1)}, bf16[256,1920]{1,0:T(8,128)(2,1)}, u32[]{:S(2)}, u32[]{:S(2)}) collective-permute-start(bf16[256,1920]{1,0:T(8,128)(2,1)} %get-tuple-element.36.refs_5_), channel_id=1, source_target_pairs={{0,2},{1,3},{2,4},{3,5},{4,6},{5,7},{6,0},{7,1},{8,10},{9,11},{10,... | collective-permute-start | bytes 2949128 | tf_op jit(solution)/shard_map/ppermute | solution.py:279
  122.3 22.2 %collective-permute-start.12 = (bf16[256,1920]{1,0:T(8,128)(2,1)}, bf16[256,1920]{1,0:T(8,128)(2,1)}, u32[]{:S(2)}, u32[]{:S(2)}) collective-permute-start(bf16[256,1920]{1,0:T(8,128)(2,1)} %get-tuple-element.39), channel_id=1, source_target_pairs={{0,6},{1,7},{2,0},{3,1},{4,2},{5,3},{6,4},{7,5},{8,14},{9,15},{10,... | collective-permute-start | bytes 2949128 | tf_op jit(solution)/shard_map/ppermute | solution.py:279
  136.1 15.0 %collective-permute-start.10 = (bf16[128,1920]{1,0:T(8,128)(2,1)}, bf16[128,1920]{1,0:T(8,128)(2,1)}, u32[]{:S(2)}, u32[]{:S(2)}) collective-permute-start(bf16[128,1920]{1,0:T(8,128)(2,1)} %multiply_convert_fusion.refs_0_), channel_id=1, source_target_pairs={{0,1},{1,0},{2,3},{3,2},{4,5},{5,4},{6,7},{7,6},{8,9},{9,8},{10,11... | collective-permute-start | bytes 1474568 | tf_op jit(solution)/shard_map/ppermute | solution.py:481
  160.2 13.9 %collective-permute-start.17 = (bf16[128,1920]{1,0:T(8,128)(2,1)S(1)}, bf16[128,1920]{1,0:T(8,128)(2,1)S(1)}, u32[]{:S(2)}, u32[]{:S(2)}) collective-permute-start(bf16[128,1920]{1,0:T(8,128)(2,1)S(1)} %get-tuple-element.41.refs_2_), channel_id=1, source_target_pairs={{0,1},{1,0},{2,3},{3,2},{4,5},{5,4},{6,7},{7,6},{8,9},{9,8},{10,11... | collective-permute-start | bytes 1474568 | tf_op jit(solution)/shard_map/ppermute | solution.py:286
  161.8 24.1 %collective-permute-start.14 = (bf16[256,1920]{1,0:T(8,128)(2,1)S(1)}, bf16[256,1920]{1,0:T(8,128)(2,1)S(1)}, u32[]{:S(2)}, u32[]{:S(2)}) collective-permute-start(bf16[256,1920]{1,0:T(8,128)(2,1)S(1)} %join_act.1.refs_0_.refs_2_), channel_id=1, source_target_pairs={{0,2},{1,3},{2,4},{3,5},{4,6},{5,7},{6,0},{7,1},{8,10},{9,11},{10,... | collective-permute-start | bytes 2949128 | tf_op jit(solution)/shard_map/ppermute | solution.py:300
  162.2 23.8 %collective-permute-start.13 = (bf16[256,1920]{1,0:T(8,128)(2,1)S(1)}, bf16[256,1920]{1,0:T(8,128)(2,1)S(1)}, u32[]{:S(2)}, u32[]{:S(2)}) collective-permute-start(bf16[256,1920]{1,0:T(8,128)(2,1)S(1)} %join_act.1.refs_0_.refs_2_), channel_id=1, source_target_pairs={{0,6},{1,7},{2,0},{3,1},{4,2},{5,3},{6,4},{7,5},{8,14},{9,15},{10,... | collective-permute-start | bytes 2949128 | tf_op jit(solution)/shard_map/ppermute | solution.py:300
  174.6 15.5 %collective-permute-start.18 = (bf16[128,1920]{1,0:T(8,128)(2,1)S(1)}, bf16[128,1920]{1,0:T(8,128)(2,1)S(1)}, u32[]{:S(2)}, u32[]{:S(2)}) collective-permute-start(bf16[128,1920]{1,0:T(8,128)(2,1)S(1)} %fusion.5.refs_0_), channel_id=1, source_target_pairs={{0,1},{1,0},{2,3},{3,2},{4,5},{5,4},{6,7},{7,6},{8,9},{9,8},{10,11... | collective-permute-start | bytes 1474568 | tf_op jit(solution)/shard_map/ppermute | solution.py:485
  185.9 12.7 %collective-permute-start.15 = (bf16[128,1920]{1,0:T(8,128)(2,1)S(1)}, bf16[128,1920]{1,0:T(8,128)(2,1)S(1)}, u32[]{:S(2)}, u32[]{:S(2)}) collective-permute-start(bf16[128,1920]{1,0:T(8,128)(2,1)S(1)} %slice.16), channel_id=1, source_target_pairs={{0,2},{1,3},{2,4},{3,5},{4,6},{5,7},{6,0},{7,1},{8,10},{9,11},{10,... | collective-permute-start | bytes 1474568 | tf_op jit(solution)/shard_map/ppermute | solution.py:295
  187.0 12.0 %collective-permute-start.16 = (bf16[128,1920]{1,0:T(8,128)(2,1)}, bf16[128,1920]{1,0:T(8,128)(2,1)S(1)}, u32[]{:S(2)}, u32[]{:S(2)}) collective-permute-start(bf16[128,1920]{1,0:T(8,128)(2,1)} %slice.17), channel_id=1, source_target_pairs={{0,6},{1,7},{2,0},{3,1},{4,2},{5,3},{6,4},{7,5},{8,14},{9,15},{10,... | collective-permute-start | bytes 1474568 | tf_op jit(solution)/shard_map/ppermute | solution.py:295
  190.9 66.3 %all-to-all-start.1 = ((bf16[16,64,1920]{2,1,0:T(8,128)(2,1)}), bf16[16,64,1920]{2,1,0:T(8,128)(2,1)}, u32[]{:S(2)}, u32[]{:S(2)}) async-start(bf16[16,64,1920]{2,1,0:T(8,128)(2,1)} %hold.7.refs_4_), calls=%async_computation.1 | async-start | bytes 7864320 | tf_op jit(solution)/shard_map/all_to_all | solution.py:306
  201.3 26.1 %collective-permute-start.19 = (bf16[256,1920]{1,0:T(8,128)(2,1)S(1)}, bf16[256,1920]{1,0:T(8,128)(2,1)}, u32[]{:S(2)}, u32[]{:S(2)}) collective-permute-start(bf16[256,1920]{1,0:T(8,128)(2,1)S(1)} %join_grad.1.refs_6_.refs_0_.refs_2_), channel_id=1, source_target_pairs={{0,6},{1,7},{2,0},{3,1},{4,2},{5,3},{6,4},{7,5},{8,14},{9,15},{10,... | collective-permute-start | bytes 2949128 | tf_op jit(solution)/shard_map/ppermute | solution.py:300
  204.9 22.4 %collective-permute-start.20 = (bf16[256,1920]{1,0:T(8,128)(2,1)S(1)}, bf16[256,1920]{1,0:T(8,128)(2,1)}, u32[]{:S(2)}, u32[]{:S(2)}) collective-permute-start(bf16[256,1920]{1,0:T(8,128)(2,1)S(1)} %join_grad.1.refs_6_.refs_0_.refs_2_), channel_id=1, source_target_pairs={{0,2},{1,3},{2,4},{3,5},{4,6},{5,7},{6,0},{7,1},{8,10},{9,11},{10,... | collective-permute-start | bytes 2949128 | tf_op jit(solution)/shard_map/ppermute | solution.py:300
  227.3 7.1 %collective-permute-start.21 = (f32[4,128,1024]{2,1,0:T(8,128)}, f32[4,128,1024]{2,1,0:T(8,128)}, u32[]{:S(2)}, u32[]{:S(2)}) collective-permute-start(f32[4,128,1024]{2,1,0:T(8,128)} %hold.8), channel_id=1, source_target_pairs={{0,8},{8,0},{16,24},{24,16},{32,40},{40,32},{48,56},{56,48},{64,72... | collective-permute-start | bytes 6291464 | tf_op jit(solution)/shard_map/ppermute | solution.py:388
  229.3 15.7 %collective-permute-start.25 = (bf16[128,1920]{1,0:T(8,128)(2,1)}, bf16[128,1920]{1,0:T(8,128)(2,1)S(1)}, u32[]{:S(2)}, u32[]{:S(2)}) collective-permute-start(bf16[128,1920]{1,0:T(8,128)(2,1)} %hold.9), channel_id=1, source_target_pairs={{0,2},{1,3},{2,4},{3,5},{4,6},{5,7},{6,0},{7,1},{8,10},{9,11},{10,... | collective-permute-start | bytes 1474568 | tf_op jit(solution)/shard_map/ppermute | solution.py:295
  231.2 14.7 %collective-permute-start.26 = (bf16[128,1920]{1,0:T(8,128)(2,1)}, bf16[128,1920]{1,0:T(8,128)(2,1)S(1)}, u32[]{:S(2)}, u32[]{:S(2)}) collective-permute-start(bf16[128,1920]{1,0:T(8,128)(2,1)} %hold.10), channel_id=1, source_target_pairs={{0,6},{1,7},{2,0},{3,1},{4,2},{5,3},{6,4},{7,5},{8,14},{9,15},{10,... | collective-permute-start | bytes 1474568 | tf_op jit(solution)/shard_map/ppermute | solution.py:295
  237.8 19.5 %collective-permute-start.22 = (bf16[4,32,1024]{2,1,0:T(8,128)(2,1)}, bf16[4,32,1024]{2,1,0:T(8,128)(2,1)S(1)}, u32[]{:S(2)}, u32[]{:S(2)}) collective-permute-start(bf16[4,32,1024]{2,1,0:T(8,128)(2,1)} %get-tuple-element.47), channel_id=1, source_target_pairs={{0,16},{8,24},{16,32},{24,40},{32,48},{40,56},{48,0},{56,8},{64,80... | collective-permute-start | bytes 786440 | tf_op jit(solution)/shard_map/ppermute | solution.py:396
  237.8 24.2 %collective-permute-start.23 = (bf16[4,32,1024]{2,1,0:T(8,128)(2,1)}, bf16[4,32,1024]{2,1,0:T(8,128)(2,1)S(1)}, u32[]{:S(2)}, u32[]{:S(2)}) collective-permute-start(bf16[4,32,1024]{2,1,0:T(8,128)(2,1)} %get-tuple-element.48), channel_id=1, source_target_pairs={{0,32},{8,40},{16,48},{24,56},{32,0},{40,8},{48,16},{56,24},{64,96... | collective-permute-start | bytes 786440 | tf_op jit(solution)/shard_map/ppermute | solution.py:396
  242.3 19.6 %collective-permute-start.24 = (bf16[4,32,1024]{2,1,0:T(8,128)(2,1)}, bf16[4,32,1024]{2,1,0:T(8,128)(2,1)S(1)}, u32[]{:S(2)}, u32[]{:S(2)}) collective-permute-start(bf16[4,32,1024]{2,1,0:T(8,128)(2,1)} %get-tuple-element.49), channel_id=1, source_target_pairs={{0,48},{8,56},{16,0},{24,8},{32,16},{40,24},{48,32},{56,40},{64,11... | collective-permute-start | bytes 786440 | tf_op jit(solution)/shard_map/ppermute | solution.py:396
  272.7 24.0 %collective-permute-start.28 = (bf16[4,16,1024]{2,1,0:T(8,128)(2,1)}, bf16[4,16,1024]{2,1,0:T(8,128)(2,1)S(1)}, u32[]{:S(2)}, u32[]{:S(2)}) collective-permute-start(bf16[4,16,1024]{2,1,0:T(8,128)(2,1)} %get-tuple-element.54.refs_9_), channel_id=1, source_target_pairs={{0,64},{8,72},{16,80},{24,88},{32,96},{40,104},{48,112},{56,120},{... | collective-permute-start | bytes 393224 | tf_op jit(solution)/shard_map/ppermute | solution.py:406
  273.9 18.3 %collective-permute-start.29 = (bf16[4,32,1024]{2,1,0:T(8,128)(2,1)}, bf16[4,32,1024]{2,1,0:T(8,128)(2,1)S(1)}, u32[]{:S(2)}, u32[]{:S(2)}) collective-permute-start(bf16[4,32,1024]{2,1,0:T(8,128)(2,1)} %get-tuple-element.55), channel_id=1, source_target_pairs={{0,16},{8,24},{16,32},{24,40},{32,48},{40,56},{48,0},{56,8},{64,80... | collective-permute-start | bytes 786440 | tf_op jit(solution)/shard_map/ppermute | solution.py:396
  275.2 17.0 %collective-permute-start.30 = (bf16[4,32,1024]{2,1,0:T(8,128)(2,1)}, bf16[4,32,1024]{2,1,0:T(8,128)(2,1)S(1)}, u32[]{:S(2)}, u32[]{:S(2)}) collective-permute-start(bf16[4,32,1024]{2,1,0:T(8,128)(2,1)} %get-tuple-element.56), channel_id=1, source_target_pairs={{0,32},{8,40},{16,48},{24,56},{32,0},{40,8},{48,16},{56,24},{64,96... | collective-permute-start | bytes 786440 | tf_op jit(solution)/shard_map/ppermute | solution.py:396
  277.8 14.5 %collective-permute-start.31 = (bf16[4,32,1024]{2,1,0:T(8,128)(2,1)}, bf16[4,32,1024]{2,1,0:T(8,128)(2,1)S(1)}, u32[]{:S(2)}, u32[]{:S(2)}) collective-permute-start(bf16[4,32,1024]{2,1,0:T(8,128)(2,1)} %get-tuple-element.57), channel_id=1, source_target_pairs={{0,48},{8,56},{16,0},{24,8},{32,16},{40,24},{48,32},{56,40},{64,11... | collective-permute-start | bytes 786440 | tf_op jit(solution)/shard_map/ppermute | solution.py:396
  (42 other events, 370.0 us)

commit v6 on v5

--- a/solution.py
+++ b/solution.py
@@ -22,7 +22,7 @@
 ZHI_SWAP = [(k, k ^ 1) for k in range(8)]
 Y_RIGHT = [(k, (k + 2) % 8) for k in range(8)]
 Y_LEFT = [(k, (k - 2) % 8) for k in range(8)]
-CB = 384
+CB = 640
 DB = 256
 
 

time: 305 us -> 300 us (0.984)
  Pallas kernels: 96.9 us -> 90.5 us
    pallas_call x9, Pallas kernels: 72.3 us -> 65.9 us  [call(): pl.pallas_call(run, out_shape=[shape for shape, _, _ in outs], grid_spec=...]
  transfers between devices with their start and end apart: 35 -> 35, of which waited for: 18 -> 19; matrix products, arithmetic and copies ran while one was open for 2% -> 2% of each run, Pallas kernels for 26% -> 24%
where the time goes in v6:
time: 300 us; the launch traced here: 299 us
  waiting for transfers between devices  114 us (38%)
  Pallas kernels  90.5 us (30%)
  starting transfers between devices  61.2 us (20%)
  local copies, waits for them, and re-layouts  30.2 us (10%)
    pallas_call x9, Pallas kernels, call(): pl.pallas_call(run, out_shape=[shape for shape, _, _ in outs], grid_spec=...  65.9 us
    unnamed x78, local copies, waits for them, and re-layouts  24.7 us
    ppermute x3, waiting for transfers between devices, wide_gather(): lax.ppermute(pair, WIDE, X_SHIFT[(4 - d) % 4])  23.8 us
    ppermute x2, waiting for transfers between devices, near_sum(): lax.ppermute(right, NARROW, Y_RIGHT)  22.3 us
    ppermute x2, waiting for transfers between devices, own_sum(): return (keep, lax.ppermute(send, NARROW, ZHI_SWAP), send)  19.8 us
    pallas_call x10, Pallas kernels, simple_call(): pl.pallas_call(run, out_shape=outs, in_specs=[spec(a) for a in ins] + [HB...  16.5 us
    ppermute x6, starting transfers between devices, x_exchange(): lax.ppermute(block, WIDE, X_SHIFT[d])  14.2 us
    ppermute x2, waiting for transfers between devices, narrow_gather(): lax.ppermute(own, NARROW, Y_RIGHT)  10.7 us
  transfers between devices with their start and end apart: 35, of which 19 were waited for; matrix products, arithmetic and copies ran while one was open for 2% of the time, Pallas kernels for 24%

profile of v6, /device:TPU:0, one launch (start us, length us, event | category | flops | bytes accessed | tf_op | source)
XLA Modules:
  0.0 298.7 jit_solution(1865773776547349276)
XLA Ops:
  6.7 6.3 %collective-permute-done = bf16[128,1024]{1,0:T(8,128)(2,1)S(1)} collective-permute-done((bf16[128,1024]{1,0:T(8,128)(2,1)S(1)}, bf16[128,1024]{1,0:T(8,128)(2,1)S(1)}, u32[]{:S(2)}, u32[]{:S(2)}) %collective-permute-start) | collective-permute-done | bytes 262176 | tf_op jit(solution)/shard_map/ppermute | solution.py:412
  17.6 20.1 %collective-permute-done.1.refs_1_ = bf16[2,128,1024]{2,1,0:T(8,128)(2,1)S(1)} collective-permute-done((bf16[2,128,1024]{2,1,0:T(8,128)(2,1)S(1)}, bf16[2,128,1024]{2,1,0:T(8,128)(2,1)S(1)}, u32[]{:S(2)}, u32[]{:S(2)}) %collective-permute-start.1) | collective-permute-done | bytes 524320 | tf_op jit(solution)/shard_map/ppermute | solution.py:414
  37.7 3.7 %collective-permute-done.3.refs_3_ = bf16[2,128,1024]{2,1,0:T(8,128)(2,1)S(1)} collective-permute-done((bf16[2,128,1024]{2,1,0:T(8,128)(2,1)S(1)}, bf16[2,128,1024]{2,1,0:T(8,128)(2,1)S(1)}, u32[]{:S(2)}, u32[]{:S(2)}) %collective-permute-start.3) | collective-permute-done | bytes 524320 | tf_op jit(solution)/shard_map/ppermute | solution.py:414
  41.6 4.1 %collective-permute-done.4 = bf16[8,128,1024]{2,1,0:T(8,128)(2,1)S(1)} collective-permute-done((bf16[8,128,1024]{2,1,0:T(8,128)(2,1)S(1)}, bf16[8,128,1024]{2,1,0:T(8,128)(2,1)S(1)}, u32[]{:S(2)}, u32[]{:S(2)}) %collective-permute-start.4) | collective-permute-done | bytes 2097184 | tf_op jit(solution)/shard_map/ppermute | solution.py:416
  48.6 5.2 %far.1 = (bf16[2,128,1920]{2,1,0:T(8,128)(2,1)}, bf16[2,128,1920]{2,1,0:T(8,128)(2,1)}) custom-call(s32[6]{0:T(128)S(1)} %concatenate.3.refs_0_.s_ref, bf16[8,2,4,16,1024]{4,3,2,1,0:T(8,128)(2,1)S(1)} %bitcast.9, bf16[8,2,4,16,1024]{4,3,2,1,0:T(8,128)(2,1)S(1)} %bitcast.19, bf16[8,2,4,16,1024]{4,3,2,1,0:T(8,128)(2,1)S(1)} %bitcast.10, ...), custom_call_target="tpu_custom_call" | custom-call | flops 2013265920 | bytes 5898240 | tf_op jit(solution)/shard_map/far/pallas_call | solution.py:55
  57.1 8.1 %relay.1 = (bf16[16,64,1920]{2,1,0:T(8,128)(2,1)S(1)}, bf16[16,64,1920]{2,1,0:T(8,128)(2,1)S(1)}) custom-call(s32[6]{0:T(128)S(1)} %concatenate.3.refs_0_.s_ref, bf16[1,1,1966592]{2,1,0:T(2,128)(2,1)S(1)} %copy-done.14, bf16[1,1,1966592]{2,1,0:T(2,128)(2,1)} %down_ref.1, bf16[2,128,1024]{2,1,0:T(8,128)(2,1)S(1)} %pad_maximum_fusion.refs_0_), custom_call_target="tpu_custom_call" | custom-call | bytes 32000000 | tf_op jit(solution)/shard_map/relay/pallas_call | solution.py:187
  69.1 4.7 %all-to-all-start = ((bf16[16,64,1920]{2,1,0:T(8,128)(2,1)}), bf16[16,64,1920]{2,1,0:T(8,128)(2,1)}, u32[]{:S(2)}, u32[]{:S(2)}) async-start(bf16[16,64,1920]{2,1,0:T(8,128)(2,1)} %hold.6), calls=%async_computation | async-start | bytes 7864320 | tf_op jit(solution)/shard_map/all_to_all | solution.py:306
  73.7 5.4 %collective-permute-done.5.refs_5_ = bf16[2,128,1920]{2,1,0:T(8,128)(2,1)S(1)} collective-permute-done((bf16[2,128,1920]{2,1,0:T(8,128)(2,1)}, bf16[2,128,1920]{2,1,0:T(8,128)(2,1)S(1)}, u32[]{:S(2)}, u32[]{:S(2)}) %collective-permute-start.5) | collective-permute-done | bytes 983072 | tf_op jit(solution)/shard_map/ppermute | solution.py:271
  82.9 5.2 %hidden_near.1 = (bf16[256,1920]{1,0:T(8,128)(2,1)S(1)}, bf16[256,1920]{1,0:T(8,128)(2,1)S(1)}) custom-call(s32[6]{0:T(128)S(1)} %concatenate.3.refs_0_.s_ref, bf16[8,2,4,16,1024]{4,3,2,1,0:T(8,128)(2,1)S(1)} %bitcast.13, bf16[8,2,4,16,1024]{4,3,2,1,0:T(8,128)(2,1)S(1)} %bitcast.23, bf16[8,2,4,16,1024]{4,3,2,1,0:T(8,128)(2,1)S(1)} %bitcast.14, ...), custom_call_target="tpu_custom_call" | custom-call | flops 2013265920 | bytes 5898240 | tf_op jit(solution)/shard_map/hidden_near/pallas_call | solution.py:55
  91.5 5.5 %back_near.1 = (bf16[256,1920]{1,0:T(8,128)(2,1)}, bf16[256,1920]{1,0:T(8,128)(2,1)}) custom-call(s32[6]{0:T(128)S(1)} %concatenate.3.refs_0_.s_ref, bf16[8,2,4,16,1024]{4,3,2,1,0:T(8,128)(2,1)S(1)} %bitcast.15, bf16[8,2,4,16,1024]{4,3,2,1,0:T(8,128)(2,1)S(1)} %bitcast.25, bf16[8,2,4,16,1024]{4,3,2,1,0:T(8,128)(2,1)S(1)} %bitcast.16, ...), custom_call_target="tpu_custom_call" | custom-call | flops 2013265920 | bytes 5898240 | tf_op jit(solution)/shard_map/back_near/pallas_call | solution.py:55
  97.0 15.3 %collective-permute-done.7.refs_3_ = bf16[256,1920]{1,0:T(8,128)(2,1)S(1)} collective-permute-done((bf16[256,1920]{1,0:T(8,128)(2,1)S(1)}, bf16[256,1920]{1,0:T(8,128)(2,1)S(1)}, u32[]{:S(2)}, u32[]{:S(2)}) %collective-permute-start.7) | collective-permute-done | bytes 983072 | tf_op jit(solution)/shard_map/ppermute | solution.py:279
  112.4 3.1 %hidden_own.1 = (f32[128,1920]{1,0:T(8,128)S(1)}, bf16[128,1920]{1,0:T(8,128)(2,1)S(1)}) custom-call(s32[6]{0:T(128)S(1)} %concatenate.3.refs_0_.s_ref, bf16[8,2,4,16,1024]{4,3,2,1,0:T(8,128)(2,1)S(1)} %bitcast.17, bf16[8,2,4,16,1024]{4,3,2,1,0:T(8,128)(2,1)S(1)} %bitcast.27, bf16[1024,1920]{1,0:T(8,128)(2,1)S(1)} %copy-done.12, ...), custom_call_target="tpu_custom_call" | custom-call | flops 1006632960 | bytes 4915200 | tf_op jit(solution)/shard_map/hidden_own/pallas_call | solution.py:55
  115.5 3.6 %collective-permute-start.9 = (bf16[128,1920]{1,0:T(8,128)(2,1)S(1)}, bf16[128,1920]{1,0:T(8,128)(2,1)S(1)}, u32[]{:S(2)}, u32[]{:S(2)}) collective-permute-start(bf16[128,1920]{1,0:T(8,128)(2,1)S(1)} %get-tuple-element.38), channel_id=1, source_target_pairs={{0,1},{1,0},{2,3},{3,2},{4,5},{5,4},{6,7},{7,6},{8,9},{9,8},{10,11... | collective-permute-start | bytes 1474568 | tf_op jit(solution)/shard_map/ppermute | solution.py:286
  122.3 11.1 %collective-permute-done.9 = bf16[128,1920]{1,0:T(8,128)(2,1)S(1)} collective-permute-done((bf16[128,1920]{1,0:T(8,128)(2,1)S(1)}, bf16[128,1920]{1,0:T(8,128)(2,1)S(1)}, u32[]{:S(2)}, u32[]{:S(2)}) %collective-permute-start.9) | collective-permute-done | bytes 491552 | tf_op jit(solution)/shard_map/ppermute | solution.py:286
  135.5 7.0 %collective-permute-done.11.refs_3_ = bf16[256,1920]{1,0:T(8,128)(2,1)} collective-permute-done((bf16[256,1920]{1,0:T(8,128)(2,1)}, bf16[256,1920]{1,0:T(8,128)(2,1)}, u32[]{:S(2)}, u32[]{:S(2)}) %collective-permute-start.11) | collective-permute-done | bytes 983072 | tf_op jit(solution)/shard_map/ppermute | solution.py:279
  142.4 7.6 %collective-permute-done.10.refs_5_.refs_1_ = bf16[128,1920]{1,0:T(8,128)(2,1)} collective-permute-done((bf16[128,1920]{1,0:T(8,128)(2,1)}, bf16[128,1920]{1,0:T(8,128)(2,1)}, u32[]{:S(2)}, u32[]{:S(2)}) %collective-permute-start.10) | collective-permute-done | bytes 491552 | tf_op jit(solution)/shard_map/ppermute | solution.py:481
  153.7 4.3 %back_own.1 = (f32[128,1920]{1,0:T(8,128)S(1)}, bf16[128,1920]{1,0:T(8,128)(2,1)S(1)}) custom-call(s32[6]{0:T(128)S(1)} %concatenate.3.refs_0_.s_ref, bf16[8,2,4,16,1024]{4,3,2,1,0:T(8,128)(2,1)S(1)} %bitcast.18, bf16[8,2,4,16,1024]{4,3,2,1,0:T(8,128)(2,1)S(1)} %bitcast.28, bf16[1024,1920]{1,0:T(8,128)(2,1)S(1)} %copy-done.7, ...), custom_call_target="tpu_custom_call" | custom-call | flops 1006632960 | bytes 4915200 | tf_op jit(solution)/shard_map/back_own/pallas_call | solution.py:55
  162.9 8.7 %collective-permute-done.17 = bf16[128,1920]{1,0:T(8,128)(2,1)S(1)} collective-permute-done((bf16[128,1920]{1,0:T(8,128)(2,1)S(1)}, bf16[128,1920]{1,0:T(8,128)(2,1)S(1)}, u32[]{:S(2)}, u32[]{:S(2)}) %collective-permute-start.17) | collective-permute-done | bytes 491552 | tf_op jit(solution)/shard_map/ppermute | solution.py:286
  172.7 10.6 %collective-permute-done.14.refs_2_.refs_4_ = bf16[256,1920]{1,0:T(8,128)(2,1)S(1)} collective-permute-done((bf16[256,1920]{1,0:T(8,128)(2,1)S(1)}, bf16[256,1920]{1,0:T(8,128)(2,1)S(1)}, u32[]{:S(2)}, u32[]{:S(2)}) %collective-permute-start.14) | collective-permute-done | bytes 983072 | tf_op jit(solution)/shard_map/ppermute | solution.py:300
  184.5 3.1 %collective-permute-start.16 = (bf16[128,1920]{1,0:T(8,128)(2,1)}, bf16[128,1920]{1,0:T(8,128)(2,1)S(1)}, u32[]{:S(2)}, u32[]{:S(2)}) collective-permute-start(bf16[128,1920]{1,0:T(8,128)(2,1)} %slice.17), channel_id=1, source_target_pairs={{0,6},{1,7},{2,0},{3,1},{4,2},{5,3},{6,4},{7,5},{8,14},{9,15},{10,... | collective-permute-start | bytes 1474568 | tf_op jit(solution)/shard_map/ppermute | solution.py:295
  188.4 5.9 %all-to-all-start.1 = ((bf16[16,64,1920]{2,1,0:T(8,128)(2,1)}), bf16[16,64,1920]{2,1,0:T(8,128)(2,1)}, u32[]{:S(2)}, u32[]{:S(2)}) async-start(bf16[16,64,1920]{2,1,0:T(8,128)(2,1)} %hold.7.refs_4_), calls=%async_computation.1 | async-start | bytes 7864320 | tf_op jit(solution)/shard_map/all_to_all | solution.py:306
  198.3 3.7 %collective-permute-start.19 = (bf16[256,1920]{1,0:T(8,128)(2,1)S(1)}, bf16[256,1920]{1,0:T(8,128)(2,1)}, u32[]{:S(2)}, u32[]{:S(2)}) collective-permute-start(bf16[256,1920]{1,0:T(8,128)(2,1)S(1)} %join_grad.1.refs_6_.refs_0_.refs_2_), channel_id=1, source_target_pairs={{0,6},{1,7},{2,0},{3,1},{4,2},{5,3},{6,4},{7,5},{8,14},{9,15},{10,... | collective-permute-start | bytes 2949128 | tf_op jit(solution)/shard_map/ppermute | solution.py:300
  202.0 10.6 %out_rows.1 = (f32[4,128,1024]{2,1,0:T(8,128)}, f32[4,128,1024]{2,1,0:T(8,128)}) custom-call(s32[6]{0:T(128)} %copy-done.23, bf16[256,1920]{1,0:T(8,128)(2,1)} %copy-done.16, bf16[256,1920]{1,0:T(8,128)(2,1)} %copy-done.26, bf16[256,1920]{1,0:T(8,128)(2,1)} %copy-done.25, bf16[128,1920]{1,0:T(8,128)(2,1)} %copy-done.19, bf16[128,1920]{1,0:T(8,128)(2,1)} %copy-done.20, ...), custom_call_target="tpu_custom_call" | custom-call | flops 4026531840 | bytes 16252928 | tf_op jit(solution)/shard_map/out_rows/pallas_call | solution.py:55
  212.6 10.7 %down_update.1.refs_1_ = bf16[1024,1920]{1,0:T(8,128)(2,1)} custom-call(s32[6]{0:T(128)} %copy-done.23, bf16[8,2,4,16,1024]{4,3,2,1,0:T(8,128)(2,1)} %bitcast.11, bf16[8,2,4,16,1024]{4,3,2,1,0:T(8,128)(2,1)} %bitcast.21, bf16[256,1920]{1,0:T(8,128)(2,1)} %copy-done.16, bf16[256,1920]{1,0:T(8,128)(2,1)} %copy-done.26, bf16[256,1920]{1,0:T(8,128)(2,1)} %copy-done.25, ...), custom_call_target="tpu_custom_call" | custom-call | flops 4026531840 | bytes 13893632 | tf_op jit(solution)/shard_map/down_update/pallas_call | solution.py:55
  227.1 3.2 %collective-permute-start.26 = (bf16[128,1920]{1,0:T(8,128)(2,1)}, bf16[128,1920]{1,0:T(8,128)(2,1)S(1)}, u32[]{:S(2)}, u32[]{:S(2)}) collective-permute-start(bf16[128,1920]{1,0:T(8,128)(2,1)} %hold.10), channel_id=1, source_target_pairs={{0,6},{1,7},{2,0},{3,1},{4,2},{5,3},{6,4},{7,5},{8,14},{9,15},{10,... | collective-permute-start | bytes 1474568 | tf_op jit(solution)/shard_map/ppermute | solution.py:295
  230.3 3.4 %merge_out.1 = (f32[4,32,1024]{2,1,0:T(8,128)}, bf16[4,32,1024]{2,1,0:T(8,128)(2,1)}, bf16[4,32,1024]{2,1,0:T(8,128)(2,1)}, bf16[4,32,1024]{2,1,0:T(8,128)(2,1)}) custom-call(f32[4,128,1024]{2,1,0:T(8,128)} %get-tuple-element.44.refs_0_, f32[4,128,1024]{2,1,0:T(8,128)} %collective-permute-done.21.refs_1_), custom_call_target="tpu_custom_call" | custom-call | bytes 8000000 | tf_op jit(solution)/shard_map/merge_out/pallas_call | solution.py:103
  234.3 4.4 %collective-permute-start.23 = (bf16[4,32,1024]{2,1,0:T(8,128)(2,1)}, bf16[4,32,1024]{2,1,0:T(8,128)(2,1)S(1)}, u32[]{:S(2)}, u32[]{:S(2)}) collective-permute-start(bf16[4,32,1024]{2,1,0:T(8,128)(2,1)} %get-tuple-element.48), channel_id=1, source_target_pairs={{0,32},{8,40},{16,48},{24,56},{32,0},{40,8},{48,16},{56,24},{64,96... | collective-permute-start | bytes 786440 | tf_op jit(solution)/shard_map/ppermute | solution.py:396
  242.5 10.6 %grad_rows.1 = (f32[4,128,1024]{2,1,0:T(8,128)}, f32[4,128,1024]{2,1,0:T(8,128)}) custom-call(s32[6]{0:T(128)} %copy-done.23, bf16[256,1920]{1,0:T(8,128)(2,1)} %copy-done.15, bf16[256,1920]{1,0:T(8,128)(2,1)} %collective-permute-done.19.refs_1_.refs_2_.refs_3_, bf16[256,1920]{1,0:T(8,128)(2,1)} %collective-permute-done.20.refs_2_.refs_3_.refs_4_, ...), custom_call_target="tpu_custom_call" | custom-call | flops 4026531840 | bytes 16252928 | tf_op jit(solution)/shard_map/grad_rows/pallas_call | solution.py:55
  253.2 5.3 %collective-permute-done.23.refs_2_ = bf16[4,32,1024]{2,1,0:T(8,128)(2,1)S(1)} collective-permute-done((bf16[4,32,1024]{2,1,0:T(8,128)(2,1)}, bf16[4,32,1024]{2,1,0:T(8,128)(2,1)S(1)}, u32[]{:S(2)}, u32[]{:S(2)}) %collective-permute-start.23) | collective-permute-done | bytes 262176 | tf_op jit(solution)/shard_map/ppermute | solution.py:396
  259.3 4.5 %collective-permute-done.27.refs_1_ = f32[4,128,1024]{2,1,0:T(8,128)} collective-permute-done((f32[4,128,1024]{2,1,0:T(8,128)}, f32[4,128,1024]{2,1,0:T(8,128)}, u32[]{:S(2)}, u32[]{:S(2)}) %collective-permute-start.27) | collective-permute-done | bytes 2097184 | tf_op jit(solution)/shard_map/ppermute | solution.py:388
  263.8 3.4 %merge_grad.1 = (f32[4,32,1024]{2,1,0:T(8,128)}, bf16[4,32,1024]{2,1,0:T(8,128)(2,1)}, bf16[4,32,1024]{2,1,0:T(8,128)(2,1)}, bf16[4,32,1024]{2,1,0:T(8,128)(2,1)}) custom-call(f32[4,128,1024]{2,1,0:T(8,128)} %get-tuple-element.50.refs_0_, f32[4,128,1024]{2,1,0:T(8,128)} %collective-permute-done.27.refs_1_), custom_call_target="tpu_custom_call" | custom-call | bytes 8000000 | tf_op jit(solution)/shard_map/merge_grad/pallas_call | solution.py:103
  276.9 10.7 %up_update.1.refs_4_ = bf16[1024,1920]{1,0:T(8,128)(2,1)} custom-call(s32[6]{0:T(128)} %copy-done.23, bf16[8,2,4,16,1024]{4,3,2,1,0:T(8,128)(2,1)} %bitcast.12, bf16[8,2,4,16,1024]{4,3,2,1,0:T(8,128)(2,1)} %bitcast.22, bf16[256,1920]{1,0:T(8,128)(2,1)} %copy-done.15, bf16[256,1920]{1,0:T(8,128)(2,1)} %collective-permute-done.19.refs_1_.refs_2_.refs_3_, ...), custom_call_target="tpu_custom_call" | custom-call | flops 4026531840 | bytes 13893632 | tf_op jit(solution)/shard_map/up_update/pallas_call | solution.py:55
  (150 shorter events, 78.7 us)
Async XLA Ops:
  4.6 8.4 %collective-permute-start = (bf16[128,1024]{1,0:T(8,128)(2,1)S(1)}, bf16[128,1024]{1,0:T(8,128)(2,1)S(1)}, u32[]{:S(2)}, u32[]{:S(2)}) collective-permute-start(bf16[128,1024]{1,0:T(8,128)(2,1)S(1)} %pick.1), channel_id=1, source_target_pairs={{0,64},{8,72},{16,80},{24,88},{32,96},{40,104},{48,112},{56,120},{... | collective-permute-start | bytes 786440 | tf_op jit(solution)/shard_map/ppermute | solution.py:412
  13.1 24.6 %collective-permute-start.1 = (bf16[2,128,1024]{2,1,0:T(8,128)(2,1)S(1)}, bf16[2,128,1024]{2,1,0:T(8,128)(2,1)S(1)}, u32[]{:S(2)}, u32[]{:S(2)}) collective-permute-start(bf16[2,128,1024]{2,1,0:T(8,128)(2,1)S(1)} %pad_maximum_fusion.refs_0_), channel_id=1, source_target_pairs={{0,48},{8,56},{16,0},{24,8},{32,16},{40,24},{48,32},{56,40},{64,11... | collective-permute-start | bytes 1572872 | tf_op jit(solution)/shard_map/ppermute | solution.py:414
  15.9 21.8 %collective-permute-start.2 = (bf16[2,128,1024]{2,1,0:T(8,128)(2,1)S(1)}, bf16[2,128,1024]{2,1,0:T(8,128)(2,1)S(1)}, u32[]{:S(2)}, u32[]{:S(2)}) collective-permute-start(bf16[2,128,1024]{2,1,0:T(8,128)(2,1)S(1)} %pad_maximum_fusion.refs_0_), channel_id=1, source_target_pairs={{0,32},{8,40},{16,48},{24,56},{32,0},{40,8},{48,16},{56,24},{64,96... | collective-permute-start | bytes 1572872 | tf_op jit(solution)/shard_map/ppermute | solution.py:414
  16.7 24.6 %collective-permute-start.3 = (bf16[2,128,1024]{2,1,0:T(8,128)(2,1)S(1)}, bf16[2,128,1024]{2,1,0:T(8,128)(2,1)S(1)}, u32[]{:S(2)}, u32[]{:S(2)}) collective-permute-start(bf16[2,128,1024]{2,1,0:T(8,128)(2,1)S(1)} %pad_maximum_fusion.refs_0_), channel_id=1, source_target_pairs={{0,16},{8,24},{16,32},{24,40},{32,48},{40,56},{48,0},{56,8},{64,80... | collective-permute-start | bytes 1572872 | tf_op jit(solution)/shard_map/ppermute | solution.py:414
  53.8 25.3 %collective-permute-start.5 = (bf16[2,128,1920]{2,1,0:T(8,128)(2,1)}, bf16[2,128,1920]{2,1,0:T(8,128)(2,1)S(1)}, u32[]{:S(2)}, u32[]{:S(2)}) collective-permute-start(bf16[2,128,1920]{2,1,0:T(8,128)(2,1)} %get-tuple-element.32.refs_7_), channel_id=1, source_target_pairs={{0,2},{1,3},{2,4},{3,5},{4,6},{5,7},{6,0},{7,1},{8,10},{9,11},{10,... | collective-permute-start | bytes 2949128 | tf_op jit(solution)/shard_map/ppermute | solution.py:271
  55.4 23.8 %collective-permute-start.6 = (bf16[2,128,1920]{2,1,0:T(8,128)(2,1)}, bf16[2,128,1920]{2,1,0:T(8,128)(2,1)}, u32[]{:S(2)}, u32[]{:S(2)}) collective-permute-start(bf16[2,128,1920]{2,1,0:T(8,128)(2,1)} %get-tuple-element.33), channel_id=1, source_target_pairs={{0,6},{1,7},{2,0},{3,1},{4,2},{5,3},{6,4},{7,5},{8,14},{9,15},{10,... | collective-permute-start | bytes 2949128 | tf_op jit(solution)/shard_map/ppermute | solution.py:271
  69.1 66.4 %all-to-all-start = ((bf16[16,64,1920]{2,1,0:T(8,128)(2,1)}), bf16[16,64,1920]{2,1,0:T(8,128)(2,1)}, u32[]{:S(2)}, u32[]{:S(2)}) async-start(bf16[16,64,1920]{2,1,0:T(8,128)(2,1)} %hold.6), calls=%async_computation | async-start | bytes 7864320 | tf_op jit(solution)/shard_map/all_to_all | solution.py:306
  88.2 24.2 %collective-permute-start.7 = (bf16[256,1920]{1,0:T(8,128)(2,1)S(1)}, bf16[256,1920]{1,0:T(8,128)(2,1)S(1)}, u32[]{:S(2)}, u32[]{:S(2)}) collective-permute-start(bf16[256,1920]{1,0:T(8,128)(2,1)S(1)} %get-tuple-element.34.refs_7_), channel_id=1, source_target_pairs={{0,2},{1,3},{2,4},{3,5},{4,6},{5,7},{6,0},{7,1},{8,10},{9,11},{10,... | collective-permute-start | bytes 2949128 | tf_op jit(solution)/shard_map/ppermute | solution.py:279
  89.8 22.5 %collective-permute-start.8 = (bf16[256,1920]{1,0:T(8,128)(2,1)S(1)}, bf16[256,1920]{1,0:T(8,128)(2,1)S(1)}, u32[]{:S(2)}, u32[]{:S(2)}) collective-permute-start(bf16[256,1920]{1,0:T(8,128)(2,1)S(1)} %get-tuple-element.35), channel_id=1, source_target_pairs={{0,6},{1,7},{2,0},{3,1},{4,2},{5,3},{6,4},{7,5},{8,14},{9,15},{10,... | collective-permute-start | bytes 2949128 | tf_op jit(solution)/shard_map/ppermute | solution.py:279
  115.5 17.9 %collective-permute-start.9 = (bf16[128,1920]{1,0:T(8,128)(2,1)S(1)}, bf16[128,1920]{1,0:T(8,128)(2,1)S(1)}, u32[]{:S(2)}, u32[]{:S(2)}) collective-permute-start(bf16[128,1920]{1,0:T(8,128)(2,1)S(1)} %get-tuple-element.38), channel_id=1, source_target_pairs={{0,1},{1,0},{2,3},{3,2},{4,5},{5,4},{6,7},{7,6},{8,9},{9,8},{10,11... | collective-permute-start | bytes 1474568 | tf_op jit(solution)/shard_map/ppermute | solution.py:286
  119.1 23.3 %collective-permute-start.11 = (bf16[256,1920]{1,0:T(8,128)(2,1)}, bf16[256,1920]{1,0:T(8,128)(2,1)}, u32[]{:S(2)}, u32[]{:S(2)}) collective-permute-start(bf16[256,1920]{1,0:T(8,128)(2,1)} %get-tuple-element.36.refs_5_), channel_id=1, source_target_pairs={{0,2},{1,3},{2,4},{3,5},{4,6},{5,7},{6,0},{7,1},{8,10},{9,11},{10,... | collective-permute-start | bytes 2949128 | tf_op jit(solution)/shard_map/ppermute | solution.py:279
  120.2 22.2 %collective-permute-start.12 = (bf16[256,1920]{1,0:T(8,128)(2,1)}, bf16[256,1920]{1,0:T(8,128)(2,1)}, u32[]{:S(2)}, u32[]{:S(2)}) collective-permute-start(bf16[256,1920]{1,0:T(8,128)(2,1)} %get-tuple-element.39), channel_id=1, source_target_pairs={{0,6},{1,7},{2,0},{3,1},{4,2},{5,3},{6,4},{7,5},{8,14},{9,15},{10,... | collective-permute-start | bytes 2949128 | tf_op jit(solution)/shard_map/ppermute | solution.py:279
  135.3 14.8 %collective-permute-start.10 = (bf16[128,1920]{1,0:T(8,128)(2,1)}, bf16[128,1920]{1,0:T(8,128)(2,1)}, u32[]{:S(2)}, u32[]{:S(2)}) collective-permute-start(bf16[128,1920]{1,0:T(8,128)(2,1)} %multiply_convert_fusion.refs_0_), channel_id=1, source_target_pairs={{0,1},{1,0},{2,3},{3,2},{4,5},{5,4},{6,7},{7,6},{8,9},{9,8},{10,11... | collective-permute-start | bytes 1474568 | tf_op jit(solution)/shard_map/ppermute | solution.py:481
  158.0 13.7 %collective-permute-start.17 = (bf16[128,1920]{1,0:T(8,128)(2,1)S(1)}, bf16[128,1920]{1,0:T(8,128)(2,1)S(1)}, u32[]{:S(2)}, u32[]{:S(2)}) collective-permute-start(bf16[128,1920]{1,0:T(8,128)(2,1)S(1)} %get-tuple-element.41.refs_2_), channel_id=1, source_target_pairs={{0,1},{1,0},{2,3},{3,2},{4,5},{5,4},{6,7},{7,6},{8,9},{9,8},{10,11... | collective-permute-start | bytes 1474568 | tf_op jit(solution)/shard_map/ppermute | solution.py:286
  159.6 23.7 %collective-permute-start.14 = (bf16[256,1920]{1,0:T(8,128)(2,1)S(1)}, bf16[256,1920]{1,0:T(8,128)(2,1)S(1)}, u32[]{:S(2)}, u32[]{:S(2)}) collective-permute-start(bf16[256,1920]{1,0:T(8,128)(2,1)S(1)} %join_act.1.refs_0_.refs_2_), channel_id=1, source_target_pairs={{0,2},{1,3},{2,4},{3,5},{4,6},{5,7},{6,0},{7,1},{8,10},{9,11},{10,... | collective-permute-start | bytes 2949128 | tf_op jit(solution)/shard_map/ppermute | solution.py:300
  160.3 23.2 %collective-permute-start.13 = (bf16[256,1920]{1,0:T(8,128)(2,1)S(1)}, bf16[256,1920]{1,0:T(8,128)(2,1)S(1)}, u32[]{:S(2)}, u32[]{:S(2)}) collective-permute-start(bf16[256,1920]{1,0:T(8,128)(2,1)S(1)} %join_act.1.refs_0_.refs_2_), channel_id=1, source_target_pairs={{0,6},{1,7},{2,0},{3,1},{4,2},{5,3},{6,4},{7,5},{8,14},{9,15},{10,... | collective-permute-start | bytes 2949128 | tf_op jit(solution)/shard_map/ppermute | solution.py:300
  172.3 15.3 %collective-permute-start.18 = (bf16[128,1920]{1,0:T(8,128)(2,1)S(1)}, bf16[128,1920]{1,0:T(8,128)(2,1)S(1)}, u32[]{:S(2)}, u32[]{:S(2)}) collective-permute-start(bf16[128,1920]{1,0:T(8,128)(2,1)S(1)} %fusion.5.refs_0_), channel_id=1, source_target_pairs={{0,1},{1,0},{2,3},{3,2},{4,5},{5,4},{6,7},{7,6},{8,9},{9,8},{10,11... | collective-permute-start | bytes 1474568 | tf_op jit(solution)/shard_map/ppermute | solution.py:485
  183.4 12.3 %collective-permute-start.15 = (bf16[128,1920]{1,0:T(8,128)(2,1)S(1)}, bf16[128,1920]{1,0:T(8,128)(2,1)S(1)}, u32[]{:S(2)}, u32[]{:S(2)}) collective-permute-start(bf16[128,1920]{1,0:T(8,128)(2,1)S(1)} %slice.16), channel_id=1, source_target_pairs={{0,2},{1,3},{2,4},{3,5},{4,6},{5,7},{6,0},{7,1},{8,10},{9,11},{10,... | collective-permute-start | bytes 1474568 | tf_op jit(solution)/shard_map/ppermute | solution.py:295
  184.5 11.6 %collective-permute-start.16 = (bf16[128,1920]{1,0:T(8,128)(2,1)}, bf16[128,1920]{1,0:T(8,128)(2,1)S(1)}, u32[]{:S(2)}, u32[]{:S(2)}) collective-permute-start(bf16[128,1920]{1,0:T(8,128)(2,1)} %slice.17), channel_id=1, source_target_pairs={{0,6},{1,7},{2,0},{3,1},{4,2},{5,3},{6,4},{7,5},{8,14},{9,15},{10,... | collective-permute-start | bytes 1474568 | tf_op jit(solution)/shard_map/ppermute | solution.py:295
  188.4 64.8 %all-to-all-start.1 = ((bf16[16,64,1920]{2,1,0:T(8,128)(2,1)}), bf16[16,64,1920]{2,1,0:T(8,128)(2,1)}, u32[]{:S(2)}, u32[]{:S(2)}) async-start(bf16[16,64,1920]{2,1,0:T(8,128)(2,1)} %hold.7.refs_4_), calls=%async_computation.1 | async-start | bytes 7864320 | tf_op jit(solution)/shard_map/all_to_all | solution.py:306
  198.3 24.9 %collective-permute-start.19 = (bf16[256,1920]{1,0:T(8,128)(2,1)S(1)}, bf16[256,1920]{1,0:T(8,128)(2,1)}, u32[]{:S(2)}, u32[]{:S(2)}) collective-permute-start(bf16[256,1920]{1,0:T(8,128)(2,1)S(1)} %join_grad.1.refs_6_.refs_0_.refs_2_), channel_id=1, source_target_pairs={{0,6},{1,7},{2,0},{3,1},{4,2},{5,3},{6,4},{7,5},{8,14},{9,15},{10,... | collective-permute-start | bytes 2949128 | tf_op jit(solution)/shard_map/ppermute | solution.py:300
  202.0 21.3 %collective-permute-start.20 = (bf16[256,1920]{1,0:T(8,128)(2,1)S(1)}, bf16[256,1920]{1,0:T(8,128)(2,1)}, u32[]{:S(2)}, u32[]{:S(2)}) collective-permute-start(bf16[256,1920]{1,0:T(8,128)(2,1)S(1)} %join_grad.1.refs_6_.refs_0_.refs_2_), channel_id=1, source_target_pairs={{0,2},{1,3},{2,4},{3,5},{4,6},{5,7},{6,0},{7,1},{8,10},{9,11},{10,... | collective-permute-start | bytes 2949128 | tf_op jit(solution)/shard_map/ppermute | solution.py:300
  223.3 7.0 %collective-permute-start.21 = (f32[4,128,1024]{2,1,0:T(8,128)}, f32[4,128,1024]{2,1,0:T(8,128)}, u32[]{:S(2)}, u32[]{:S(2)}) collective-permute-start(f32[4,128,1024]{2,1,0:T(8,128)} %hold.8), channel_id=1, source_target_pairs={{0,8},{8,0},{16,24},{24,16},{32,40},{40,32},{48,56},{56,48},{64,72... | collective-permute-start | bytes 6291464 | tf_op jit(solution)/shard_map/ppermute | solution.py:388
  225.2 16.2 %collective-permute-start.25 = (bf16[128,1920]{1,0:T(8,128)(2,1)}, bf16[128,1920]{1,0:T(8,128)(2,1)S(1)}, u32[]{:S(2)}, u32[]{:S(2)}) collective-permute-start(bf16[128,1920]{1,0:T(8,128)(2,1)} %hold.9), channel_id=1, source_target_pairs={{0,2},{1,3},{2,4},{3,5},{4,6},{5,7},{6,0},{7,1},{8,10},{9,11},{10,... | collective-permute-start | bytes 1474568 | tf_op jit(solution)/shard_map/ppermute | solution.py:295
  227.1 14.7 %collective-permute-start.26 = (bf16[128,1920]{1,0:T(8,128)(2,1)}, bf16[128,1920]{1,0:T(8,128)(2,1)S(1)}, u32[]{:S(2)}, u32[]{:S(2)}) collective-permute-start(bf16[128,1920]{1,0:T(8,128)(2,1)} %hold.10), channel_id=1, source_target_pairs={{0,6},{1,7},{2,0},{3,1},{4,2},{5,3},{6,4},{7,5},{8,14},{9,15},{10,... | collective-permute-start | bytes 1474568 | tf_op jit(solution)/shard_map/ppermute | solution.py:295
  233.7 19.5 %collective-permute-start.22 = (bf16[4,32,1024]{2,1,0:T(8,128)(2,1)}, bf16[4,32,1024]{2,1,0:T(8,128)(2,1)S(1)}, u32[]{:S(2)}, u32[]{:S(2)}) collective-permute-start(bf16[4,32,1024]{2,1,0:T(8,128)(2,1)} %get-tuple-element.47), channel_id=1, source_target_pairs={{0,16},{8,24},{16,32},{24,40},{32,48},{40,56},{48,0},{56,8},{64,80... | collective-permute-start | bytes 786440 | tf_op jit(solution)/shard_map/ppermute | solution.py:396
  234.3 24.2 %collective-permute-start.23 = (bf16[4,32,1024]{2,1,0:T(8,128)(2,1)}, bf16[4,32,1024]{2,1,0:T(8,128)(2,1)S(1)}, u32[]{:S(2)}, u32[]{:S(2)}) collective-permute-start(bf16[4,32,1024]{2,1,0:T(8,128)(2,1)} %get-tuple-element.48), channel_id=1, source_target_pairs={{0,32},{8,40},{16,48},{24,56},{32,0},{40,8},{48,16},{56,24},{64,96... | collective-permute-start | bytes 786440 | tf_op jit(solution)/shard_map/ppermute | solution.py:396
  238.7 19.8 %collective-permute-start.24 = (bf16[4,32,1024]{2,1,0:T(8,128)(2,1)}, bf16[4,32,1024]{2,1,0:T(8,128)(2,1)S(1)}, u32[]{:S(2)}, u32[]{:S(2)}) collective-permute-start(bf16[4,32,1024]{2,1,0:T(8,128)(2,1)} %get-tuple-element.49), channel_id=1, source_target_pairs={{0,48},{8,56},{16,0},{24,8},{32,16},{40,24},{48,32},{56,40},{64,11... | collective-permute-start | bytes 786440 | tf_op jit(solution)/shard_map/ppermute | solution.py:396
  269.3 22.8 %collective-permute-start.28 = (bf16[4,16,1024]{2,1,0:T(8,128)(2,1)}, bf16[4,16,1024]{2,1,0:T(8,128)(2,1)S(1)}, u32[]{:S(2)}, u32[]{:S(2)}) collective-permute-start(bf16[4,16,1024]{2,1,0:T(8,128)(2,1)} %get-tuple-element.54.refs_9_), channel_id=1, source_target_pairs={{0,64},{8,72},{16,80},{24,88},{32,96},{40,104},{48,112},{56,120},{... | collective-permute-start | bytes 393224 | tf_op jit(solution)/shard_map/ppermute | solution.py:406
  270.4 17.2 %collective-permute-start.29 = (bf16[4,32,1024]{2,1,0:T(8,128)(2,1)}, bf16[4,32,1024]{2,1,0:T(8,128)(2,1)S(1)}, u32[]{:S(2)}, u32[]{:S(2)}) collective-permute-start(bf16[4,32,1024]{2,1,0:T(8,128)(2,1)} %get-tuple-element.55), channel_id=1, source_target_pairs={{0,16},{8,24},{16,32},{24,40},{32,48},{40,56},{48,0},{56,8},{64,80... | collective-permute-start | bytes 786440 | tf_op jit(solution)/shard_map/ppermute | solution.py:396
  271.7 15.9 %collective-permute-start.30 = (bf16[4,32,1024]{2,1,0:T(8,128)(2,1)}, bf16[4,32,1024]{2,1,0:T(8,128)(2,1)S(1)}, u32[]{:S(2)}, u32[]{:S(2)}) collective-permute-start(bf16[4,32,1024]{2,1,0:T(8,128)(2,1)} %get-tuple-element.56), channel_id=1, source_target_pairs={{0,32},{8,40},{16,48},{24,56},{32,0},{40,8},{48,16},{56,24},{64,96... | collective-permute-start | bytes 786440 | tf_op jit(solution)/shard_map/ppermute | solution.py:396
  274.3 13.3 %collective-permute-start.31 = (bf16[4,32,1024]{2,1,0:T(8,128)(2,1)}, bf16[4,32,1024]{2,1,0:T(8,128)(2,1)S(1)}, u32[]{:S(2)}, u32[]{:S(2)}) collective-permute-start(bf16[4,32,1024]{2,1,0:T(8,128)(2,1)} %get-tuple-element.57), channel_id=1, source_target_pairs={{0,48},{8,56},{16,0},{24,8},{32,16},{40,24},{48,32},{56,40},{64,11... | collective-permute-start | bytes 786440 | tf_op jit(solution)/shard_map/ppermute | solution.py:396
  (42 other events, 364.6 us)
